TPU v7x, 32 devices: a whole 2x2x4 slice. The times are simulated.
32 devices in a mesh: dp: 2 (over x), slab: 16 (over z, y, core).
Axes of the slice: x: 2, y: 2, z: 4, core: 2. Of those that a mesh axis runs over, the one named last changes fastest.
Arguments:
- field: float32 [2, 32, 128, 128, 128], P('dp', None, 'slab'), may hold values from -6 to 6
- cotangent: float32 [2, 32, 128, 128, 128], P('dp', None, 'slab'), may hold values from -6 to 6
- spec_weight: float32 [2, 32, 512, 1024], P(None, None, 'slab'), may hold values from -8 to 8
- bypass_weight: float32 [32, 32], replicated, may hold values from -1 to 1
Outputs:
- layer_out: float32 [2, 32, 128, 128, 128], P('dp', None, 'slab')
- grad_field: float32 [2, 32, 128, 128, 128], P('dp', None, 'slab')
- grad_spec: float32 [2, 32, 512, 1024], P(None, None, 'slab')
All inputs are finite; a program needn't handle non-finite values.
Results may differ from a plain program's by a relative error of at most 0.0001.
Values sent between devices are 32-bit elements; how exact they have to be, the bound alone decides.
No kernel may reach another device: no remote copies, remote signals or barrier semaphores. Data moves between devices by JAX's collectives and lax.ppermute only.
A program may use at most 384 MiB of HBM per device.

v0:
```python
import math

import jax
import jax.numpy as jnp
from jax import lax
from jax.sharding import PartitionSpec as P

GX = 128
GY = 128
GZ = 128
KX = 32
KY = 32
KZ = 16


precise = lax.Precision.HIGHEST


def wave_tables(length, count, signed):
    positions = jnp.arange(length, dtype=jnp.int32)
    indices = jnp.arange(count, dtype=jnp.int32)
    if signed:
        freqs = jnp.where(indices < count // 2, indices, indices - count)
    else:
        freqs = indices
    phase = positions[:, None] * freqs[None, :] % length
    angle = phase.astype(jnp.float32) * (2.0 * math.pi / length)
    return (jnp.cos(angle), jnp.sin(angle))


def gelu_exact(values):
    return jax.nn.gelu(values, approximate=False)


def plane_spectrum(data, weight, z_cos, z_sin, y_cos, y_sin):
    chans, planes = (data.shape[0], data.shape[1])
    part_re = jnp.einsum("cxyz,zk->cxky", data, z_cos, precision=precise)
    part_im = -jnp.einsum("cxyz,zk->cxky", data, z_sin, precision=precise)
    mid_re = jnp.einsum("cxky,yj->cxjk", part_re, y_cos, precision=precise) + jnp.einsum(
        "cxky,yj->cxjk", part_im, y_sin, precision=precise
    )
    mid_im = jnp.einsum("cxky,yj->cxjk", part_im, y_cos, precision=precise) - jnp.einsum(
        "cxky,yj->cxjk", part_re, y_sin, precision=precise
    )
    stacked = jnp.stack([mid_re * weight, mid_im * weight])
    return stacked.reshape(2, chans, planes, KY * KZ)


def along_first(moved, x_cos, x_sin):
    line_re, line_im = (moved[0], moved[1])
    full_re = jnp.einsum("cxp,xi->cpi", line_re, x_cos, precision=precise) + jnp.einsum(
        "cxp,xi->cpi", line_im, x_sin, precision=precise
    )
    full_im = jnp.einsum("cxp,xi->cpi", line_im, x_cos, precision=precise) - jnp.einsum(
        "cxp,xi->cpi", line_re, x_sin, precision=precise
    )
    return (full_re, full_im)


def back_first(spec_re, spec_im, x_cos, x_sin):
    wide_re = jnp.einsum("cpi,xi->cxp", spec_re, x_cos, precision=precise) - jnp.einsum(
        "cpi,xi->cxp", spec_im, x_sin, precision=precise
    )
    wide_im = jnp.einsum("cpi,xi->cxp", spec_re, x_sin, precision=precise) + jnp.einsum(
        "cpi,xi->cxp", spec_im, x_cos, precision=precise
    )
    return jnp.stack([wide_re, wide_im])


def plane_inverse(arrived, weight, z_cos, z_sin, y_cos, y_sin):
    chans, planes = (arrived.shape[1], arrived.shape[2])
    shaped = arrived.reshape(2, chans, planes, KY, KZ)
    wide_re, wide_im = (shaped[0], shaped[1])
    plane_re = jnp.einsum("cxjk,yj->cxky", wide_re, y_cos, precision=precise) - jnp.einsum(
        "cxjk,yj->cxky", wide_im, y_sin, precision=precise
    )
    plane_im = jnp.einsum("cxjk,yj->cxky", wide_re, y_sin, precision=precise) + jnp.einsum(
        "cxjk,yj->cxky", wide_im, y_cos, precision=precise
    )
    plane_re = plane_re * weight[:, None]
    plane_im = plane_im * weight[:, None]
    return jnp.einsum("cxky,zk->cxyz", plane_re, z_cos, precision=precise) - jnp.einsum(
        "cxky,zk->cxyz", plane_im, z_sin, precision=precise
    )


def on_device(field, cotangent, spec_weight, bypass_weight):
    count = lax.axis_size("slab")
    pairs = KY * KZ // count
    chans = field.shape[1]
    z_cos, z_sin = wave_tables(GZ, KZ, False)
    y_cos, y_sin = wave_tables(GY, KY, True)
    x_cos, x_sin = wave_tables(GX, KX, True)
    kz_index = jnp.arange(KZ, dtype=jnp.int32)
    fold = jnp.where(kz_index == 0, 1.0, 2.0).astype(jnp.float32) / float(GX * GY * GZ)
    ones = jnp.ones((KZ,), jnp.float32)
    weights = spec_weight.reshape(2, chans, pairs, KX, chans)
    w_real = weights[0]
    w_imag = weights[1]
    source = field[0]
    local_spec = plane_spectrum(source, ones, z_cos, z_sin, y_cos, y_sin)
    moved = lax.all_to_all(local_spec, "slab", split_axis=3, concat_axis=2, tiled=True)
    hat_re, hat_im = along_first(moved, x_cos, x_sin)
    mix_re = jnp.einsum("cpi,cpio->opi", hat_re, w_real, precision=precise) - jnp.einsum(
        "cpi,cpio->opi", hat_im, w_imag, precision=precise
    )
    mix_im = jnp.einsum("cpi,cpio->opi", hat_re, w_imag, precision=precise) + jnp.einsum(
        "cpi,cpio->opi", hat_im, w_real, precision=precise
    )
    outgoing = back_first(mix_re, mix_im, x_cos, x_sin)
    arrived = lax.all_to_all(outgoing, "slab", split_axis=2, concat_axis=3, tiled=True)
    spectral = plane_inverse(arrived, fold, z_cos, z_sin, y_cos, y_sin)
    pre = spectral + jnp.einsum("co,cxyz->oxyz", bypass_weight, source, precision=precise)
    result, pullback = jax.vjp(gelu_exact, pre)
    grad_pre = pullback(cotangent[0])[0]
    fold_grid = jnp.broadcast_to(fold, (KY, KZ))
    cot_spec = plane_spectrum(grad_pre, fold_grid, z_cos, z_sin, y_cos, y_sin)
    cot_moved = lax.all_to_all(cot_spec, "slab", split_axis=3, concat_axis=2, tiled=True)
    grad_re, grad_im = along_first(cot_moved, x_cos, x_sin)
    own_real = jnp.einsum("cpi,opi->cpio", hat_re, grad_re, precision=precise) + jnp.einsum(
        "cpi,opi->cpio", hat_im, grad_im, precision=precise
    )
    own_imag = jnp.einsum("cpi,opi->cpio", hat_re, grad_im, precision=precise) - jnp.einsum(
        "cpi,opi->cpio", hat_im, grad_re, precision=precise
    )
    summed = lax.psum(jnp.stack([own_real, own_imag]), "dp")
    grad_spec = summed.reshape(2, chans, pairs, KX * chans)
    input_re = jnp.einsum("opi,cpio->cpi", grad_re, w_real, precision=precise) + jnp.einsum(
        "opi,cpio->cpi", grad_im, w_imag, precision=precise
    )
    input_im = jnp.einsum("opi,cpio->cpi", grad_im, w_real, precision=precise) - jnp.einsum(
        "opi,cpio->cpi", grad_re, w_imag, precision=precise
    )
    grad_out = back_first(input_re, input_im, x_cos, x_sin)
    grad_arrived = lax.all_to_all(grad_out, "slab", split_axis=2, concat_axis=3, tiled=True)
    back_field = plane_inverse(grad_arrived, ones, z_cos, z_sin, y_cos, y_sin)
    back_field = back_field + jnp.einsum(
        "co,oxyz->cxyz", bypass_weight, grad_pre, precision=precise
    )
    return (result[None], back_field[None], grad_spec)


def solution(mesh):
    in_specs = (
        P("dp", None, "slab", None, None),
        P("dp", None, "slab", None, None),
        P(None, None, "slab", None),
        P(),
    )
    out_specs = (
        P("dp", None, "slab", None, None),
        P("dp", None, "slab", None, None),
        P(None, None, "slab", None),
    )
    return jax.shard_map(
        on_device, mesh=mesh, in_specs=in_specs, out_specs=out_specs, check_vma=False
    )
```

profile of v0, /device:TPU:0, one launch (start us, length us, event | category | flops | bytes accessed | tf_op | source)
XLA Modules:
  0.0 795.2 jit_solution(8337754750162333702)
XLA Ops:
  7.2 17.2 %convolution_bitcast_fusion.1 = f32[32,8,16,128]{3,2,1,0:T(8,128)S(1)} fusion(f32[1,32,8,128,128]{4,3,2,1,0:T(8,128)} %param.4), kind=kOutput, calls=%fused_computation.101 | convolution fusion | flops 805335040 | bytes 18874368 | tf_op jit(solution)/shard_map/cxyz,zk->cxky/dot_general | solution.py:37
  24.4 14.7 %negate_bitcast_fusion.1 = f32[32,8,16,128]{3,2,1,0:T(8,128)S(1)} fusion(f32[1,32,8,128,128]{4,3,2,1,0:T(8,128)S(1)} %copy-done.2), kind=kOutput, calls=%fused_computation.75 | convolution fusion | flops 805859328 | bytes 18874368 | tf_op jit(solution)/shard_map/cxyz,zk->cxky/dot_general | solution.py:38
  39.1 9.8 %fusion.57 = f32[32,32,8,16]{1,0,3,2:T(8,128)S(1)} fusion(f32[32,8,16,128]{3,2,1,0:T(8,128)S(1)} %negate_bitcast_fusion.1, s32[32]{0:T(128)S(1)} %compare_select_fusion), kind=kOutput, calls=%fused_computation.92 | convolution fusion | flops 201383936 | bytes 2621568 | tf_op jit(solution)/shard_map/cxky,yj->cxjk/dot_general | solution.py:42
  48.9 9.7 %fusion.59 = f32[32,32,8,16]{1,0,3,2:T(8,128)S(1)} fusion(f32[32,8,16,128]{3,2,1,0:T(8,128)S(1)} %negate_bitcast_fusion.1, s32[32]{0:T(128)S(1)} %compare_select_fusion), kind=kOutput, calls=%fused_computation.94 | convolution fusion | flops 201383936 | bytes 2621568 | tf_op jit(solution)/shard_map/cxky,yj->cxjk/dot_general | solution.py:39
  58.7 10.2 %add_bitcast_fusion.1 = f32[32,8,32,16]{0,2,3,1:T(8,128)S(1)} fusion(f32[32,32,8,16]{1,0,3,2:T(8,128)S(1)} %fusion.59, f32[32,8,16,128]{3,2,1,0:T(8,128)S(1)} %convolution_bitcast_fusion.1, s32[32]{0:T(128)S(1)} %compare_select_fusion), kind=kOutput, calls=%fused_computation.74 | convolution fusion | flops 201515008 | bytes 3145856 | tf_op jit(solution)/shard_map/cxky,yj->cxjk/dot_general | solution.py:39
  68.8 9.8 %subtract_bitcast_fusion.1 = f32[32,8,32,16]{0,2,3,1:T(8,128)S(1)} fusion(f32[32,32,8,16]{1,0,3,2:T(8,128)S(1)} %fusion.57, f32[32,8,16,128]{3,2,1,0:T(8,128)S(1)} %convolution_bitcast_fusion.1, s32[32]{0:T(128)S(1)} %compare_select_fusion), kind=kOutput, calls=%fused_computation.73 | convolution fusion | flops 201515008 | bytes 3145856 | tf_op jit(solution)/shard_map/cxky,yj->cxjk/dot_general | solution.py:42
  90.8 7.4 all-to-all-start
  98.2 8.5 %fusion.393 = (f32[1,32,32,1024]{3,2,1,0:T(8,128)}, f32[1,32,32,1024]{3,2,1,0:T(8,128)}) fusion(f32[2,32,32,1024]{3,2,1,0:T(8,128)} %param.6), kind=kLoop, calls=%fused_computation.379 | loop fusion | bytes 16777216 | tf_op jit(solution)/shard_map/slice | solution.py:98
  106.7 11.6 %squeeze.39 = f32[32,32,32,32]{3,2,1,0:T(8,128)} reshape(f32[1,32,32,1024]{3,2,1,0:T(8,128)} %get-tuple-element.17) | data formatting | bytes 8388608 | tf_op jit(solution)/shard_map/squeeze | solution.py:98
  118.3 11.6 %squeeze.40 = f32[32,32,32,32]{3,2,1,0:T(8,128)} reshape(f32[1,32,32,1024]{3,2,1,0:T(8,128)} %get-tuple-element.18) | data formatting | bytes 8388608 | tf_op jit(solution)/shard_map/squeeze | solution.py:99
  136.5 6.6 copy.241
  160.0 12.7 %multiply_reduce_fusion.5 = (f32[32,32,32]{2,1,0:T(8,128)S(1)}, f32[32,32,32]{2,1,0:T(8,128)S(1)}, f32[32,32,32]{2,1,0:T(8,128)S(1)}, f32[32,32,32]{2,1,0:T(8,128)S(1)}) fusion(f32[32,32,32,32]{3,2,1,0:T(8,128)} %squeeze.40, f32[32,32,32]{1,0,2:T(8,128)S(1)} %fusion.76, f32[32,32,32]{1,0,2:T(8,128)S(1)} %fusion.82, f32[32,32,32,32]{3,2,1,0:T(8,128)} %squeeze.39), kind=kLoop, calls=%fused_computation.18 | loop fusion | flops 8257536 | bytes 9175040
  192.7 30.5 %fusion.10 = f32[32,8,128,128]{3,0,2,1:T(8,128)} fusion(f32[32,8,128,128]{3,2,1,0:T(8,128)} %bitcast.317, f32[32,32]{1,0:T(8,128)S(1)} %copy-done), kind=kOutput, calls=%fused_computation.24 | convolution fusion | flops 1610612736 | bytes 33558528 | tf_op jit(solution)/shard_map/co,cxyz->oxyz/dot_general | solution.py:113
  258.3 29.0 %fusion.38 = f32[32,8,128,128]{3,2,1,0:T(8,128)} fusion(f32[32,8,16,128]{3,2,1,0:T(8,128)S(1)} %fusion.156, f32[32,8,16,128]{3,2,1,0:T(8,128)S(1)} %copy-done.4, f32[16]{0:T(128)S(1)} %fusion.229), kind=kOutput, calls=%fused_computation.70 | convolution fusion | flops 806383616 | bytes 20971584 | tf_op jit(solution)/shard_map/cxky,zk->cxyz/dot_general | solution.py:82
  287.3 69.5 %fusion.6 = (f32[32,8,128,128]{3,2,1,0:T(8,128)S(1)}, f32[32,8,128,128]{3,2,1,0:T(8,128)}, f32[32,8,128,128]{3,2,1,0:T(8,128)}) fusion(f32[1,32,8,128,128]{4,3,2,1,0:T(8,128)} %param.5, f32[32,8,128,128]{3,0,2,1:T(8,128)} %fusion.10, f32[32,8,128,128]{3,2,1,0:T(8,128)} %fusion.38, f32[32,8,16,128]{3,2,1,0:T(8,128)S(1)} %fusion.142, ...), kind=kOutput, calls=%fused_computation.11 | convolution fusion | flops 1112567808 | bytes 104857664 | tf_op jit(solution)/shard_map/cxky,zk->cxyz/dot_general | solution.py:82
  356.9 14.6 %negate_bitcast_fusion = f32[32,8,16,128]{3,2,1,0:T(8,128)S(1)} fusion(f32[32,8,128,128]{3,2,1,0:T(8,128)S(1)} %get-tuple-element.15), kind=kOutput, calls=%fused_computation.67 | convolution fusion | flops 805859328 | bytes 18874368 | tf_op jit(solution)/shard_map/cxyz,zk->cxky/dot_general | solution.py:38
  371.4 14.8 %convolution_bitcast_fusion = f32[32,8,16,128]{3,2,1,0:T(8,128)S(1)} fusion(f32[32,8,128,128]{3,2,1,0:T(8,128)S(1)} %get-tuple-element.15), kind=kOutput, calls=%fused_computation.100 | convolution fusion | flops 805335040 | bytes 18874368 | tf_op jit(solution)/shard_map/cxyz,zk->cxky/dot_general | solution.py:37
  386.2 9.8 %fusion.45 = f32[32,32,8,16]{1,0,3,2:T(8,128)S(1)} fusion(f32[32,8,16,128]{3,2,1,0:T(8,128)S(1)} %negate_bitcast_fusion, s32[32]{0:T(128)S(1)} %copy-done.11), kind=kOutput, calls=%fused_computation.80 | convolution fusion | flops 201383936 | bytes 2621568 | tf_op jit(solution)/shard_map/cxky,yj->cxjk/dot_general | solution.py:42
  396.0 9.8 %fusion.47 = f32[32,32,8,16]{1,0,3,2:T(8,128)S(1)} fusion(f32[32,8,16,128]{3,2,1,0:T(8,128)S(1)} %negate_bitcast_fusion, s32[32]{0:T(128)S(1)} %copy-done.11), kind=kOutput, calls=%fused_computation.82 | convolution fusion | flops 201383936 | bytes 2621568 | tf_op jit(solution)/shard_map/cxky,yj->cxjk/dot_general | solution.py:39
  405.8 10.2 %multiply_bitcast_fusion.2 = f32[32,8,32,16]{0,2,3,1:T(8,128)S(1)} fusion(f32[32,32,8,16]{1,0,3,2:T(8,128)S(1)} %fusion.47, f32[32,8,16,128]{3,2,1,0:T(8,128)S(1)} %convolution_bitcast_fusion, f32[16]{0:T(128)S(1)} %fusion.229, s32[32]{0:T(128)S(1)} %copy-done.11), kind=kOutput, calls=%fused_computation.66 | convolution fusion | flops 201646080 | bytes 3145920 | tf_op jit(solution)/shard_map/cxky,yj->cxjk/dot_general | solution.py:39
  416.0 9.8 %multiply_bitcast_fusion.1 = f32[32,8,32,16]{0,2,3,1:T(8,128)S(1)} fusion(f32[32,32,8,16]{1,0,3,2:T(8,128)S(1)} %fusion.45, f32[32,8,16,128]{3,2,1,0:T(8,128)S(1)} %convolution_bitcast_fusion, f32[16]{0:T(128)S(1)} %fusion.229, s32[32]{0:T(128)S(1)} %copy-done.11), kind=kOutput, calls=%fused_computation.65 | convolution fusion | flops 201646080 | bytes 3145920 | tf_op jit(solution)/shard_map/cxky,yj->cxjk/dot_general | solution.py:42
  437.1 30.6 %all_to_all.60 = f32[16,1,16384]{2,1,0:T(1,128)S(1)} all-to-all(f32[16,1,16384]{2,1,0:T(1,128)S(1)} %reshape.87), channel_id=1, replica_groups=mesh['dp'=2,'slab'=16] {'slab'}, dimensions={0} | all-to-all | bytes 2097152 | tf_op jit(solution)/shard_map/all_to_all | solution.py:118
  473.7 6.8 copy.243
  499.7 31.3 %add_bitcast_fusion = (f32[1,32,32,32,32]{4,3,2,1,0:T(8,128)}, f32[1,32,32,32,32]{4,3,2,1,0:T(8,128)}, f32[32,32,32]{1,0,2:T(8,128)S(1)}, f32[32,32,32]{1,0,2:T(...) fusion(f32[32,32,32]{2,1,0:T(8,128)} %copy.247, f32[32,32,32]{2,1,0:T(8,128)} %copy.246, ...), kind=kLoop, calls=%fused_computation.27 | loop fusion | flops 14548992 | bytes 17825792 | tf_op jit(solution)/shard_map/stack | solution.py:126
  531.0 24.1 %pad_maximum_fusion = f32[2,32,32,32,32]{4,3,2,1,0:T(8,128)} fusion(f32[1,32,32,32,32]{4,3,2,1,0:T(8,128)} %get-tuple-element.28, f32[1,32,32,32,32]{4,3,2,1,0:T(8,128)} %get-tuple-element.27), kind=kLoop, calls=%fused_computation | loop fusion | flops 2097152 | bytes 16777216 | tf_op jit(solution)/shard_map/stack | solution.py:126
  555.1 26.1 %reshape.58 = f32[2,32,32,1024]{3,2,1,0:T(8,128)} reshape(f32[2,32,32,32,32]{4,3,2,1,0:T(8,128)} %pad_maximum_fusion) | data formatting | bytes 16777216 | tf_op jit(solution)/shard_map/reshape | solution.py:127
  581.2 33.5 %fusion.8 = f32[8,128,128,32]{2,3,1,0:T(8,128)} fusion(f32[32,8,128,128]{3,2,1,0:T(8,128)} %copy-done.1, f32[32,32]{1,0:T(8,128)S(1)} %copy-done), kind=kOutput, calls=%fused_computation.21 | convolution fusion | flops 1610612736 | bytes 33558528 | tf_op jit(solution)/shard_map/co,oxyz->cxyz/dot_general | solution.py:137
  631.8 19.1 %multiply_bitcast_fusion = f32[1,32,8,128,128]{4,3,2,1,0:T(8,128)} fusion(f32[32,8,128,128]{3,2,1,0:T(8,128)} %get-tuple-element.16, f32[32,8,128,128]{3,2,1,0:T(8,128)} %get-tuple-element.33), kind=kLoop, calls=%fused_computation.28 | loop fusion | flops 8388608 | bytes 50331648 | tf_op jit(solution)/shard_map/broadcast_in_dim | solution.py:140
  687.7 28.8 %fusion.34 = f32[32,8,128,128]{3,2,1,0:T(8,128)} fusion(f32[32,8,16,128]{3,2,1,0:T(8,128)S(1)} %fusion.150, f32[32,8,16,128]{3,2,1,0:T(8,128)S(1)} %fusion.138), kind=kOutput, calls=%fused_computation.63 | convolution fusion | flops 805859328 | bytes 20971520 | tf_op jit(solution)/shard_map/cxky,zk->cxyz/dot_general | solution.py:82
  716.6 45.4 %fusion.1 = f32[1,32,8,128,128]{4,3,2,1,0:T(8,128)} fusion(f32[8,128,128,32]{2,3,1,0:T(8,128)S(1)} %bitcast.319, f32[32,8,128,128]{3,2,1,0:T(8,128)} %fusion.34, f32[32,8,16,128]{3,2,1,0:T(8,128)S(1)} %fusion.136, f32[32,8,16,128]{3,2,1,0:T(8,128)S(1)} %fusion.148), kind=kOutput, calls=%fused_computation.4 | convolution fusion | flops 814247936 | bytes 54525952 | tf_op jit(solution)/shard_map/cxky,zk->cxyz/dot_general | solution.py:82
  762.0 17.6 %all-reduce.2.cloned.1.call-done = f32[2,32,32,1024]{3,2,1,0:T(8,128)} async-done(((f32[2,32,32,1024]{3,2,1,0:T(8,128)}), f32[2,32,32,1024]{3,2,1,0:T(8,128)}) %all-reduce.2.cloned.1.call-update) | async-done | bytes 8388624 | tf_op jit(solution)/shard_map/psum | solution.py:126
  779.6 8.4 %copy.337 = f32[2,32,32,1024]{3,2,1,0:T(8,128)} copy(f32[2,32,32,1024]{3,2,1,0:T(8,128)} %all-reduce.2.cloned.1.call-done) | data formatting | bytes 16777216
  (111 shorter events, 180.6 us)
Async XLA Ops:
  7.2 185.6 %copy-start = (f32[32,32]{1,0:T(8,128)S(1)}, f32[32,32]{1,0:T(8,128)}, u32[]{:S(2)}) copy-start(f32[32,32]{1,0:T(8,128)} %param.7) | copy-start | bytes 12292
  7.2 249.1 %copy-start.10 = (s32[32]{0:T(128)}, s32[32]{0:T(128)S(1)}, u32[]{:S(2)}) copy-start(s32[32]{0:T(128)S(1)} %compare_select_fusion) | copy-start | bytes 388
  7.2 17.2 %copy-start.2 = (f32[1,32,8,128,128]{4,3,2,1,0:T(8,128)S(1)}, f32[1,32,8,128,128]{4,3,2,1,0:T(8,128)}, u32[]{:S(2)}) copy-start(f32[1,32,8,128,128]{4,3,2,1,0:T(8,128)} %param.4) | copy-start | bytes 50331652
  90.8 39.2 %all-to-all-start = ((f32[16,1,16384]{2,1,0:T(1,128)}), f32[16,1,16384]{2,1,0:T(1,128)S(1)}, u32[]{:S(2)}, u32[]{:S(2)}) async-start(f32[16,1,16384]{2,1,0:T(1,128)} %reshape.83), calls=%async_computation | async-start | bytes 2097152 | tf_op jit(solution)/shard_map/all_to_all | solution.py:102
  156.4 16.3 %copy-start.5 = (f32[32,32,32]{1,0,2:T(8,128)}, f32[32,32,32]{1,0,2:T(8,128)S(1)}, u32[]{:S(2)}) copy-start(f32[32,32,32]{1,0,2:T(8,128)S(1)} %fusion.76) | copy-start | bytes 393220
  160.0 12.7 %copy-start.7 = (f32[32,32,32]{1,0,2:T(8,128)}, f32[32,32,32]{1,0,2:T(8,128)S(1)}, u32[]{:S(2)}) copy-start(f32[32,32,32]{1,0,2:T(8,128)S(1)} %fusion.82) | copy-start | bytes 393220
  186.7 36.6 %all-to-all-start.1 = ((f32[16,1,16384]{2,1,0:T(1,128)}), f32[16,1,16384]{2,1,0:T(1,128)S(1)}, u32[]{:S(2)}, u32[]{:S(2)}) async-start(f32[16,1,16384]{2,1,0:T(1,128)} %reshape.85), calls=%async_computation.1 | async-start | bytes 2097152 | tf_op jit(solution)/shard_map/all_to_all | solution.py:111
  192.7 587.0 %all-reduce.2.cloned.1.call-start = ((), (), s32[]{:S(2)}) async-start(), calls=%async_computation.4 | async-start | bytes 16777216 | tf_op jit(solution)/shard_map/psum | solution.py:126
  254.3 4.0 copy-start.4
  258.3 29.1 %copy-start.9 = (f32[32,8,16,128]{3,2,1,0:T(8,128)S(1)}, f32[32,8,16,128]{3,2,1,0:T(8,128)}, u32[]{:S(2)}) copy-start(f32[32,8,16,128]{3,2,1,0:T(8,128)} %fusion.154) | copy-start | bytes 6291460
  356.9 14.6 %copy-start.1 = (f32[32,8,128,128]{3,2,1,0:T(8,128)}, f32[32,8,128,128]{3,2,1,0:T(8,128)S(1)}, u32[]{:S(2)}) copy-start(f32[32,8,128,128]{3,2,1,0:T(8,128)S(1)} %get-tuple-element.15) | copy-start | bytes 50331652
  371.4 14.8 %copy-start.11 = (s32[32]{0:T(128)S(1)}, s32[32]{0:T(128)}, u32[]{:S(2)}) copy-start(s32[32]{0:T(128)} %copy-done.10) | copy-start | bytes 388
  490.3 9.5 %copy-start.6 = (f32[32,32,32]{1,0,2:T(8,128)S(1)}, f32[32,32,32]{1,0,2:T(8,128)}, u32[]{:S(2)}) copy-start(f32[32,32,32]{1,0,2:T(8,128)} %copy-done.5) | copy-start | bytes 393220
  490.3 9.4 %copy-start.8 = (f32[32,32,32]{1,0,2:T(8,128)S(1)}, f32[32,32,32]{1,0,2:T(8,128)}, u32[]{:S(2)}) copy-start(f32[32,32,32]{1,0,2:T(8,128)} %copy-done.7) | copy-start | bytes 393220
  626.8 28.0 %all-to-all-start.3 = ((f32[16,1,16384]{2,1,0:T(1,128)}), f32[16,1,16384]{2,1,0:T(1,128)S(1)}, u32[]{:S(2)}, u32[]{:S(2)}) async-start(f32[16,1,16384]{2,1,0:T(1,128)} %reshape.89), calls=%async_computation.3 | async-start | bytes 2097152 | tf_op jit(solution)/shard_map/all_to_all | solution.py:135
  679.7 4.0 copy-start.3
  685.7 30.9 %slice-start = ((s8[16777216]{0:T(1024)(128)(4,1)}), s8[4194304]{0:T(1024)(128)(4,1)S(1)}, s32[]{:S(2)}) async-start(s8[16777216]{0:T(1024)(128)(4,1)} %bitcast.318), calls=%async_computation.5 | async-start | bytes 8388608
  687.7 28.9 %slice-start.1 = ((s8[16777216]{0:T(1024)(128)(4,1)}), s8[4194304]{0:T(1024)(128)(4,1)S(1)}, s32[]{:S(2)}) async-start(s8[16777216]{0:T(1024)(128)(4,1)} %bitcast.318), calls=%async_computation.6 | async-start | bytes 8388608
  687.7 28.9 %slice-start.2 = ((s8[16777216]{0:T(1024)(128)(4,1)}), s8[4194304]{0:T(1024)(128)(4,1)S(1)}, s32[]{:S(2)}) async-start(s8[16777216]{0:T(1024)(128)(4,1)} %bitcast.318), calls=%async_computation.7 | async-start | bytes 8388608
  687.7 28.9 %slice-start.3 = ((s8[16777216]{0:T(1024)(128)(4,1)}), s8[4194304]{0:T(1024)(128)(4,1)S(1)}, s32[]{:S(2)}) async-start(s8[16777216]{0:T(1024)(128)(4,1)} %bitcast.318), calls=%async_computation.8 | async-start | bytes 8388608
Sparse Core Ops, SparseCore 0:
  581.3 198.3 all-reduce.1
where the time goes:
time: 802 us; the launch traced here: 795 us
  matrix products  430 us (54%)
  local copies, waits for them, and re-layouts  179 us (22%)
  other arithmetic  101 us (13%)
  blocking collectives  30.6 us (4%)
  waiting for transfers between devices  21.5 us (3%)
  starting transfers between devices  18.5 us (2%)
  between operations  15 us (2%)
    dot_general x2, matrix products, plane_inverse(): jnp.einsum('cxky,zk->cxyz', plane_im, z_sin, precision=precise)  115 us
    dot_general x2, matrix products, plane_inverse(): jnp.einsum('cxky,zk->cxyz', plane_re, z_cos, precision=precise)  57.9 us
    another operation x2, other arithmetic, on_device(): summed = lax.psum(jnp.stack([own_real, own_imag]), 'dp')  55.3 us
    unnamed x43, local copies, waits for them, and re-layouts  39.9 us
    dot_general x1, matrix products, on_device(): jnp.einsum('co,oxyz->cxyz', bypass_weight, grad_pre, precision=precise)  33.5 us
    dot_general x2, matrix products, plane_spectrum(): part_re = jnp.einsum('cxyz,zk->cxky', data, z_cos, precision=precise)  31.9 us
    all_to_all x1, blocking collectives, on_device(): lax.all_to_all(cot_spec, 'slab', split_axis=3, concat_axis=2, tiled=True)  30.6 us
    dot_general x1, matrix products, on_device(): jnp.einsum('co,cxyz->oxyz', bypass_weight, source, precision=precise)  30.5 us
  transfers between devices with their start and end apart: 4, of which 2 were waited for; matrix products, arithmetic and copies ran while one was open for 29% of the time, Pallas kernels for 0%

commit v1 on v0

--- a/solution.py
+++ b/solution.py
@@ -1,8 +1,13 @@
+import functools
 import math
 
 import jax
 import jax.numpy as jnp
+import ml_dtypes
+import numpy as np
 from jax import lax
+from jax.experimental import pallas as pl
+from jax.experimental.pallas import tpu as pltpu
 from jax.sharding import PartitionSpec as P
 
 GX = 128
@@ -84,7 +89,7 @@
     )
 
 
-def on_device(field, cotangent, spec_weight, bypass_weight):
+def on_device_any(field, cotangent, spec_weight, bypass_weight):
     count = lax.axis_size("slab")
     pairs = KY * KZ // count
     chans = field.shape[1]
@@ -140,6 +145,527 @@
     return (result[None], back_field[None], grad_spec)
 
 
+CH = 32
+PLANES = 8
+PAIRS = 32
+PEERS = 16
+KYL = PAIRS // KZ
+KYH = KY // KYL
+QUAD = 4
+GROUPS = CH // QUAD
+TILE = QUAD * PAIRS
+WIDE = QUAD * KYL * 2 * GZ
+MODES_O = KX * CH
+
+BF = jnp.bfloat16
+F32 = jnp.float32
+
+
+def split_table(table):
+    high = table.astype(ml_dtypes.bfloat16)
+    low = (table - high.astype(np.float64)).astype(ml_dtypes.bfloat16)
+    return high, low
+
+
+def phases(length, count, signed):
+    freqs = np.arange(count)
+    if signed:
+        freqs = np.where(freqs < count // 2, freqs, freqs - count)
+    phase = (np.arange(length)[:, None] * freqs[None, :]) % length
+    angle = phase * (2.0 * np.pi / length)
+    return np.cos(angle), np.sin(angle)
+
+
+@functools.lru_cache(maxsize=None)
+def host_tables():
+    zc, zs = phases(GZ, KZ, False)
+    yc, ys = phases(GY, KY, True)
+    xc, xs = phases(GX, KX, True)
+    fold = np.where(np.arange(KZ) == 0, 1.0, 2.0) / float(GX * GY * GZ)
+    out = {}
+    ycr = yc.T.reshape(KYH, KYL, GY).transpose(1, 0, 2)
+    ysr = ys.T.reshape(KYH, KYL, GY).transpose(1, 0, 2)
+    fwd = np.stack([ycr, -ysr], axis=1).reshape(2 * KY, GY)
+    high, low = split_table(fwd)
+    out["yf"] = np.block([[high, high], [low, low]])
+    inv = np.stack([ycr, -ysr], axis=1).reshape(2 * KY, GY).T
+    high, low = split_table(inv)
+    out["yi"] = np.concatenate([high, high, low], axis=1)
+    core = np.stack([np.stack([zc, -zs]), np.stack([zs, zc])])
+    for name, scale in (("zf", np.ones(KZ)), ("zg", fold)):
+        table = np.zeros((QUAD, KYL, 2, GZ, 2, QUAD, KYL, KZ))
+        for q in range(QUAD):
+            for k in range(KYL):
+                table[q, k, :, :, :, q, k, :] = (core * scale).transpose(0, 2, 1, 3)
+        out[name + "h"], out[name + "l"] = split_table(table.reshape(WIDE, 2 * TILE))
+    core = np.stack([np.stack([zc, zs]), np.stack([-zs, zc])])
+    for name, scale in (("zi", fold), ("zj", np.ones(KZ))):
+        table = np.zeros((2, QUAD, KYL, KZ, QUAD, KYL, 2, GZ))
+        for q in range(QUAD):
+            for k in range(KYL):
+                table[:, q, k, :, q, k, :, :] = (core * scale).transpose(0, 3, 1, 2)
+        out[name + "h"], out[name + "l"] = split_table(table.reshape(2 * TILE, WIDE))
+    core = np.stack([np.stack([xc, xs]), np.stack([-xs, xc])])
+    table = core.reshape(2, 2, PEERS, PLANES, KX).transpose(0, 4, 2, 1, 3).reshape(2 * KX, 2 * GX)
+    high, low = split_table(table)
+    out["xfh"], out["xfl"] = high, low
+    core = np.stack([np.stack([xc, -xs]), np.stack([xs, xc])])
+    table = core.reshape(2, 2, PEERS, PLANES, KX).transpose(2, 0, 3, 1, 4).reshape(2 * GX, 2 * KX)
+    high, low = split_table(table)
+    out["xi"] = np.concatenate([high, high, low], axis=1)
+    spread = np.repeat(np.eye(2 * KX), CH, axis=1).astype(ml_dtypes.bfloat16)
+    out["spread"] = np.concatenate([spread, spread], axis=0)
+    out["gather"] = np.concatenate([spread, spread], axis=0).T.copy()
+    return out
+
+
+def halves(values):
+    high = values.astype(BF)
+    return high, (values - high.astype(F32)).astype(BF)
+
+
+def dot(left, right):
+    return jnp.dot(left, right, preferred_element_type=F32)
+
+
+def dot3(high, low, table_high, table_low):
+    rows = high.shape[0]
+    both = dot(jnp.concatenate([high, low], axis=0), table_high)
+    return both[:rows] + both[rows:] + dot(high, table_low)
+
+
+def lines_to_modes(pair, yf):
+    high, low = halves(pair)
+    both = dot(yf, jnp.concatenate([high, low], axis=0))
+    return halves(both[: 2 * KY] + both[2 * KY :])
+
+
+def call(body, grid, ins, outs, shapes, scratch, vmem=56):
+    return pl.pallas_call(
+        body,
+        grid=grid,
+        in_specs=ins,
+        out_specs=outs,
+        out_shape=shapes,
+        scratch_shapes=scratch,
+        compiler_params=pltpu.CompilerParams(
+            dimension_semantics=("arbitrary",), vmem_limit_bytes=vmem * 1024 * 1024
+        ),
+    )
+
+
+def whole(array):
+    zeros = (0,) * array.ndim
+    return pl.BlockSpec(array.shape, lambda step: zeros)
+
+
+def spectrum_body(f_ref, yf_ref, th_ref, tl_ref, out_ref, high_s, low_s):
+    yf = yf_ref[...]
+    for x in range(PLANES):
+        for half in range(2):
+            pair = jnp.concatenate([f_ref[2 * half, x], f_ref[2 * half + 1, x]], axis=1)
+            high, low = lines_to_modes(pair, yf)
+            for j in range(2):
+                for part in range(2 * KYL):
+                    lanes = ((2 * half + j) * 2 * KYL + part) * GZ
+                    rows = slice(part * KYH, (part + 1) * KYH)
+                    to = (slice(x * KYH, (x + 1) * KYH), slice(lanes, lanes + GZ))
+                    high_s[to] = high[rows, j * GZ : (j + 1) * GZ]
+                    low_s[to] = low[rows, j * GZ : (j + 1) * GZ]
+    sums = dot3(high_s[...], low_s[...], th_ref[...], tl_ref[...])
+    for part in range(2):
+        block = sums[:, part * TILE : (part + 1) * TILE].reshape(PLANES, KYH, TILE)
+        out_ref[:, part * PLANES : (part + 1) * PLANES, :] = jnp.swapaxes(block, 0, 1)
+
+
+def spectrum(field, t):
+    tables = (t["yf"], t["zfh"], t["zfl"])
+    return call(
+        spectrum_body,
+        (GROUPS,),
+        [pl.BlockSpec((QUAD, PLANES, GY, GZ), lambda g: (g, 0, 0, 0))] + [whole(a) for a in tables],
+        pl.BlockSpec((PEERS, 2 * PLANES, TILE), lambda g: (0, 0, g)),
+        jax.ShapeDtypeStruct((PEERS, 2 * PLANES, CH * PAIRS), F32),
+        [pltpu.VMEM((PLANES * KYH, WIDE), BF), pltpu.VMEM((PLANES * KYH, WIDE), BF)],
+    )(field, *tables)
+
+
+def own_mask():
+    rows = lax.broadcasted_iota(jnp.int32, (TILE, TILE), 0) % QUAD
+    lanes = lax.broadcasted_iota(jnp.int32, (TILE, TILE), 1) // PAIRS
+    return rows == lanes
+
+
+def x_forward(moved, xfh, xfl):
+    high, low = halves(moved)
+    both = dot(jnp.concatenate([xfh, xfl], axis=0), high)
+    return both[: 2 * KX] + both[2 * KX :] + dot(xfh, low)
+
+
+def x_inverse(spec, xi):
+    high, low = halves(spec)
+    return dot(xi, jnp.concatenate([high, low, high], axis=0))
+
+
+def spread_modes(spec, spread):
+    turned = jnp.concatenate([spec, spec], axis=0).T
+    high, low = halves(turned)
+    lanes = lax.broadcasted_iota(jnp.int32, (TILE, 4 * KX), 1)
+    return dot(jnp.where(lanes < 2 * KX, high, low), spread)
+
+
+def mix_body(moved_ref, w_ref, xfh_ref, xfl_ref, spread_ref, xi_ref, hat_ref, out_ref, acc_s, turn_s):
+    step = pl.program_id(0)
+
+    @pl.when(step == 0)
+    def _():
+        acc_s[...] = jnp.zeros_like(acc_s)
+
+    hat = x_forward(moved_ref[...].reshape(2 * GX, TILE), xfh_ref[...], xfl_ref[...])
+    hat_ref[...] = hat
+    wide = spread_modes(hat, spread_ref[...])
+    acc_re, acc_im = acc_s[0], acc_s[1]
+    for q in range(QUAD):
+        h_re = wide[q * PAIRS : (q + 1) * PAIRS, :MODES_O]
+        h_im = wide[q * PAIRS : (q + 1) * PAIRS, MODES_O:]
+        w_re, w_im = w_ref[0, q], w_ref[1, q]
+        acc_re = acc_re + h_re * w_re - h_im * w_im
+        acc_im = acc_im + h_re * w_im + h_im * w_re
+    acc_s[0] = acc_re
+    acc_s[1] = acc_im
+
+    @pl.when(step == GROUPS - 1)
+    def _():
+        mask = own_mask()
+        for part in range(2):
+            full = jnp.concatenate([acc_s[part]] * QUAD, axis=0)
+            for k in range(MODES_O // TILE):
+                turned = full[:, k * TILE : (k + 1) * TILE].T
+                turn_s[pl.ds(part * MODES_O + k * TILE, TILE), :] = jnp.where(mask, turned, 0.0)
+        xi = xi_ref[...]
+        for g in range(0, GROUPS, 2):
+            tiles = []
+            for h in range(g, g + 2):
+                parts = []
+                for part in range(2):
+                    total = None
+                    for q in range(QUAD):
+                        rows = turn_s[pl.ds(part * MODES_O + h * QUAD + q, KX, stride=CH), :]
+                        total = rows if total is None else total + rows
+                    parts.append(total)
+                tiles.append(jnp.concatenate(parts, axis=0))
+            wave = x_inverse(jnp.concatenate(tiles, axis=1), xi)
+            out_ref[:, :, g * TILE : (g + 2) * TILE] = wave.reshape(PEERS, 2 * PLANES, 2 * TILE)
+
+
+def mix(moved, weights, t):
+    tables = (t["xfh"], t["xfl"], t["spread"], t["xi"])
+    return call(
+        mix_body,
+        (GROUPS,),
+        [
+            pl.BlockSpec((PEERS, 2 * PLANES, TILE), lambda g: (0, 0, g)),
+            pl.BlockSpec((2, QUAD, PAIRS, MODES_O), lambda g: (0, g, 0, 0)),
+        ]
+        + [whole(a) for a in tables],
+        [
+            pl.BlockSpec((2 * KX, TILE), lambda g: (0, g)),
+            pl.BlockSpec((PEERS, 2 * PLANES, CH * PAIRS), lambda g: (0, 0, 0)),
+        ],
+        [
+            jax.ShapeDtypeStruct((2 * KX, CH * PAIRS), F32),
+            jax.ShapeDtypeStruct((PEERS, 2 * PLANES, CH * PAIRS), F32),
+        ],
+        [pltpu.VMEM((2, PAIRS, MODES_O), F32), pltpu.VMEM((2 * MODES_O, TILE), F32)],
+    )(moved, weights, *tables)
+
+
+def input_body(moved_ref, w_ref, xfh_ref, xfl_ref, gather_ref, xi_ref, g_ref, out_ref, turn_s):
+    step = pl.program_id(0)
+
+    @pl.when(step == 0)
+    def _():
+        lanes = lax.broadcasted_iota(jnp.int32, (KX, TILE), 1) // PAIRS
+        for h in range(GROUPS):
+            tile = moved_ref[:, :, h * TILE : (h + 1) * TILE].reshape(2 * GX, TILE)
+            hat = x_forward(tile, xfh_ref[...], xfl_ref[...])
+            for part in range(2):
+                rows = hat[part * KX : (part + 1) * KX]
+                for q in range(QUAD):
+                    to = pl.ds(part * MODES_O + h * QUAD + q, KX, stride=CH)
+                    turn_s[to, :] = jnp.where(lanes == q, rows, 0.0)
+        for part in range(2):
+            for k in range(MODES_O // TILE):
+                turned = turn_s[pl.ds(part * MODES_O + k * TILE, TILE), :].T
+                total = turned[:PAIRS]
+                for q in range(1, QUAD):
+                    total = total + turned[q * PAIRS : (q + 1) * PAIRS]
+                g_ref[part, :, k * TILE : (k + 1) * TILE] = total
+
+    g_re, g_im = g_ref[0], g_ref[1]
+    rows_high, rows_low = [], []
+    for q in range(QUAD):
+        w_re, w_im = w_ref[0, q], w_ref[1, q]
+        full = jnp.concatenate([g_re * w_re + g_im * w_im, g_im * w_re - g_re * w_im], axis=1)
+        high, low = halves(full)
+        rows_high.append(high)
+        rows_low.append(low)
+    both = dot(jnp.concatenate(rows_high + rows_low, axis=0), gather_ref[...])
+    spec = (both[:TILE] + both[TILE:]).T[: 2 * KX]
+    out_ref[...] = x_inverse(spec, xi_ref[...]).reshape(PEERS, 2 * PLANES, TILE)
+
+
+def input_modes(moved, weights, t):
+    tables = (t["xfh"], t["xfl"], t["gather"], t["xi"])
+    return call(
+        input_body,
+        (GROUPS,),
+        [
+            whole(moved),
+            pl.BlockSpec((2, QUAD, PAIRS, MODES_O), lambda g: (0, g, 0, 0)),
+        ]
+        + [whole(a) for a in tables],
+        [
+            pl.BlockSpec((2, PAIRS, MODES_O), lambda g: (0, 0, 0)),
+            pl.BlockSpec((PEERS, 2 * PLANES, TILE), lambda g: (0, 0, g)),
+        ],
+        [
+            jax.ShapeDtypeStruct((2, PAIRS, MODES_O), F32),
+            jax.ShapeDtypeStruct((PEERS, 2 * PLANES, CH * PAIRS), F32),
+        ],
+        [pltpu.VMEM((2 * MODES_O, TILE), F32)],
+    )(moved, weights, *tables)
+
+
+def weight_grad_body(hat_ref, far_hat_ref, g_ref, far_g_ref, spread_ref, out_ref):
+    spread = spread_ref[...]
+    near = spread_modes(hat_ref[...], spread)
+    far = spread_modes(far_hat_ref[...], spread)
+    for q in range(QUAD):
+        rows = slice(q * PAIRS, (q + 1) * PAIRS)
+        n_re, n_im = near[rows, :MODES_O], near[rows, MODES_O:]
+        f_re, f_im = far[rows, :MODES_O], far[rows, MODES_O:]
+        out_ref[0, q] = n_re * g_ref[0] + n_im * g_ref[1] + f_re * far_g_ref[0] + f_im * far_g_ref[1]
+        out_ref[1, q] = n_re * g_ref[1] - n_im * g_ref[0] + f_re * far_g_ref[1] - f_im * far_g_ref[0]
+
+
+def weight_grad(hat, far_hat, grad, far_grad, t):
+    tile = pl.BlockSpec((2 * KX, TILE), lambda g: (0, g))
+    return call(
+        weight_grad_body,
+        (GROUPS,),
+        [tile, tile, whole(grad), whole(far_grad), whole(t["spread"])],
+        pl.BlockSpec((2, QUAD, PAIRS, MODES_O), lambda g: (0, g, 0, 0)),
+        jax.ShapeDtypeStruct((2, CH, PAIRS, MODES_O), F32),
+        [],
+    )(hat, far_hat, grad, far_grad, t["spread"])
+
+
+def gelu_parts(pre):
+    bell = jnp.exp(pre * pre * -0.5)
+    t = 1.0 / (1.0 + (0.3275911 * math.sqrt(0.5)) * jnp.abs(pre))
+    poly = 1.061405429 * 0.5
+    for coefficient in (-1.453152027, 1.421413741, -0.284496736, 0.254829592):
+        poly = poly * t + coefficient * 0.5
+    tail = poly * t * bell
+    share = jnp.where(pre >= 0.0, 1.0 - tail, tail)
+    return share, pre * bell * (1.0 / math.sqrt(2.0 * math.pi))
+
+
+def sort_planes(arrived_ref, planes_s):
+    for part in range(2):
+        block = arrived_ref[:, part * PLANES : (part + 1) * PLANES, :]
+        lanes = slice(part * CH * PAIRS, (part + 1) * CH * PAIRS)
+        planes_s[:, :, lanes] = jnp.swapaxes(block, 0, 1)
+
+
+def inverse_plane(x, planes_s, yi, zih, zil, high_s, low_s, spec_s):
+    rows = []
+    for g in range(GROUPS):
+        parts = [planes_s[x, :, (part * GROUPS + g) * TILE : (part * GROUPS + g + 1) * TILE] for part in range(2)]
+        rows.append(jnp.concatenate(parts, axis=1))
+    high, low = halves(jnp.concatenate(rows, axis=0))
+    high, low = halves(dot3(high, low, zih, zil))
+    high_s[...] = high
+    low_s[...] = low
+
+    def one(g, carry):
+        rows = pl.ds(pl.multiple_of(g * KYH, KYH), KYH)
+        for half in range(2):
+            stacks = []
+            for source in (high_s, low_s):
+                sides = []
+                for j in range(2):
+                    lanes = (2 * half + j) * 2 * KYL * GZ
+                    sides.append(
+                        jnp.concatenate(
+                            [source[rows, lanes + k * GZ : lanes + (k + 1) * GZ] for k in range(2 * KYL)], axis=0
+                        )
+                    )
+                stacks.append(jnp.concatenate(sides, axis=1))
+            waves = dot(yi, jnp.concatenate([stacks[0], stacks[1], stacks[0]], axis=0))
+            for j in range(2):
+                spec_s[g * QUAD + 2 * half + j] = waves[:, j * GZ : (j + 1) * GZ]
+        return carry
+
+    lax.fori_loop(0, GROUPS, one, 0)
+
+
+def channel_sum(data_ref, y, kron_ref):
+    tiles = [data_ref[:, 0, pl.ds(y + 8 * j, 8), :].reshape(8 * CH, GZ) for j in range(2)]
+    high, low = halves(jnp.concatenate(tiles, axis=1))
+    both = dot(kron_ref[...], high)
+    return both[: 8 * CH] + both[8 * CH :] + dot(kron_ref[: 8 * CH], low)
+
+
+def middle_body(
+    arrived_ref, f_ref, cot_ref, kron_ref, yi_ref, zih_ref, zil_ref, yf_ref, zgh_ref, zgl_ref,
+    out_ref, grad_ref, spec_ref, planes_s, high_s, low_s, wave_s, sent_s,
+):
+    x = pl.program_id(0)
+
+    @pl.when(x == 0)
+    def _():
+        sort_planes(arrived_ref, planes_s)
+
+    inverse_plane(x, planes_s, yi_ref[...], zih_ref[...], zil_ref[...], high_s, low_s, wave_s)
+
+    def rows(i, carry):
+        y = pl.multiple_of(i * 16, 16)
+        sums = channel_sum(f_ref, y, kron_ref)
+        for j in range(2):
+            at = pl.ds(y + 8 * j, 8)
+            pre = sums[:, j * GZ : (j + 1) * GZ].reshape(CH, 8, GZ) + wave_s[:, at, :]
+            share, slope = gelu_parts(pre)
+            out_ref[:, 0, at, :] = pre * share
+            grad_ref[:, 0, at, :] = cot_ref[:, 0, at, :] * (share + slope)
+        return carry
+
+    lax.fori_loop(0, GY // 16, rows, 0)
+
+    def lines(g, carry):
+        at = pl.ds(pl.multiple_of(g * KYH, KYH), KYH)
+        for half in range(2):
+            c = g * QUAD + 2 * half
+            high, low = lines_to_modes(jnp.concatenate([grad_ref[c, 0], grad_ref[c + 1, 0]], axis=1), yf_ref[...])
+            for j in range(2):
+                for part in range(2 * KYL):
+                    lanes = ((2 * half + j) * 2 * KYL + part) * GZ
+                    take = slice(part * KYH, (part + 1) * KYH)
+                    high_s[at, lanes : lanes + GZ] = high[take, j * GZ : (j + 1) * GZ]
+                    low_s[at, lanes : lanes + GZ] = low[take, j * GZ : (j + 1) * GZ]
+        return carry
+
+    lax.fori_loop(0, GROUPS, lines, 0)
+    sums = dot3(high_s[...], low_s[...], zgh_ref[...], zgl_ref[...])
+    for g in range(GROUPS):
+        for part in range(2):
+            lanes = (part * GROUPS + g) * TILE
+            sent_s[x, :, lanes : lanes + TILE] = sums[g * KYH : (g + 1) * KYH, part * TILE : (part + 1) * TILE]
+
+    @pl.when(x == PLANES - 1)
+    def _():
+        for part in range(2):
+            block = sent_s[:, :, part * CH * PAIRS : (part + 1) * CH * PAIRS]
+            spec_ref[:, part * PLANES : (part + 1) * PLANES, :] = jnp.swapaxes(block, 0, 1)
+
+
+def plane_block():
+    return pl.BlockSpec((CH, 1, GY, GZ), lambda x: (0, x, 0, 0))
+
+
+def middle(arrived, field, cotangent, kron, t):
+    tables = (kron, t["yi"], t["zih"], t["zil"], t["yf"], t["zgh"], t["zgl"])
+    return call(
+        middle_body,
+        (PLANES,),
+        [whole(arrived), plane_block(), plane_block()] + [whole(a) for a in tables],
+        [plane_block(), plane_block(), whole(arrived)],
+        [
+            jax.ShapeDtypeStruct(field.shape, F32),
+            jax.ShapeDtypeStruct(field.shape, F32),
+            jax.ShapeDtypeStruct(arrived.shape, F32),
+        ],
+        [
+            pltpu.VMEM((PLANES, KYH, 2 * CH * PAIRS), F32),
+            pltpu.VMEM((GROUPS * KYH, WIDE), BF),
+            pltpu.VMEM((GROUPS * KYH, WIDE), BF),
+            pltpu.VMEM((CH, GY, GZ), F32),
+            pltpu.VMEM((PLANES, KYH, 2 * CH * PAIRS), F32),
+        ],
+    )(arrived, field, cotangent, *tables)
+
+
+def last_body(arrived_ref, grad_ref, kron_ref, yi_ref, zjh_ref, zjl_ref, out_ref, planes_s, high_s, low_s, wave_s):
+    x = pl.program_id(0)
+
+    @pl.when(x == 0)
+    def _():
+        sort_planes(arrived_ref, planes_s)
+
+    inverse_plane(x, planes_s, yi_ref[...], zjh_ref[...], zjl_ref[...], high_s, low_s, wave_s)
+
+    def rows(i, carry):
+        y = pl.multiple_of(i * 16, 16)
+        sums = channel_sum(grad_ref, y, kron_ref)
+        for j in range(2):
+            at = pl.ds(y + 8 * j, 8)
+            out_ref[:, 0, at, :] = sums[:, j * GZ : (j + 1) * GZ].reshape(CH, 8, GZ) + wave_s[:, at, :]
+        return carry
+
+    lax.fori_loop(0, GY // 16, rows, 0)
+
+
+def last(arrived, grad_pre, kron, t):
+    tables = (kron, t["yi"], t["zjh"], t["zjl"])
+    return call(
+        last_body,
+        (PLANES,),
+        [whole(arrived), plane_block()] + [whole(a) for a in tables],
+        plane_block(),
+        jax.ShapeDtypeStruct(grad_pre.shape, F32),
+        [
+            pltpu.VMEM((PLANES, KYH, 2 * CH * PAIRS), F32),
+            pltpu.VMEM((GROUPS * KYH, WIDE), BF),
+            pltpu.VMEM((GROUPS * KYH, WIDE), BF),
+            pltpu.VMEM((CH, GY, GZ), F32),
+        ],
+    )(arrived, grad_pre, *tables)
+
+
+def kron_halves(matrix):
+    high = lax.reduce_precision(matrix, 8, 7)
+    eye = jnp.eye(8, dtype=F32)
+    stacked = jnp.stack([high, matrix - high])
+    wide = stacked[:, :, None, :, None] * eye[None, None, :, None, :]
+    return wide.reshape(16 * CH, 8 * CH).astype(BF)
+
+
+def swap_slabs(array):
+    return lax.all_to_all(array, "slab", split_axis=0, concat_axis=0, tiled=True)
+
+
+def on_device(field, cotangent, spec_weight, bypass_weight):
+    shape = (field.shape[1], field.shape[2], spec_weight.shape[2], lax.axis_size("slab"), lax.axis_size("dp"))
+    if shape != (CH, PLANES, PAIRS, PEERS, 2):
+        return on_device_any(field, cotangent, spec_weight, bypass_weight)
+    t = {name: jnp.asarray(table) for name, table in host_tables().items()}
+    source, other = field[0], cotangent[0]
+    moved = swap_slabs(spectrum(source, t))
+    kron_out = kron_halves(bypass_weight.T)
+    kron_in = kron_halves(bypass_weight)
+    hat, outgoing = mix(moved, spec_weight, t)
+    swap_pair = [(0, 1), (1, 0)]
+    far_hat = lax.ppermute(hat, "dp", swap_pair)
+    result, grad_pre, cot_spec = middle(swap_slabs(outgoing), source, other, kron_out, t)
+    grad, grad_out = input_modes(swap_slabs(cot_spec), spec_weight, t)
+    far_grad = lax.ppermute(grad, "dp", swap_pair)
+    grad_arrived = swap_slabs(grad_out)
+    grad_spec = weight_grad(hat, far_hat, grad, far_grad, t)
+    back_field = last(grad_arrived, grad_pre, kron_in, t)
+    return (result[None], back_field[None], grad_spec)
+
+
 def solution(mesh):
     in_specs = (
         P("dp", None, "slab", None, None),

time: 802 us -> 270 us (0.34)
  matrix products: 430 us -> 0 us
  local copies, waits for them, and re-layouts: 179 us -> 17.7 us
  Pallas kernels: 0 us -> 153 us
  other arithmetic: 101 us -> 4.12 us
  blocking collectives: 30.6 us -> 64.4 us
  between operations: 15 us -> 0.72 us
    dot_general x42 -> x0, matrix products: 430 us -> none  [the longest x2 115 us: plane_inverse(): jnp.einsum('cxky,zk->cxyz', plane_im, z_sin, precision=precise)]
    pallas_call x0 -> x6, Pallas kernels: none -> 153 us  [the longest x1 70.5 us: middle(): call(middle_body, (PLANES,), [whole(arrived), plane_block(), plane_block(...]
    another operation x6 -> x4, other arithmetic: 56.3 us -> 0.03 us  [kron_halves(): stacked = jnp.stack([high, matrix - high])]
    unnamed x43 -> x12, local copies, waits for them, and re-layouts: 39.9 us -> 2.67 us
    squeeze x6 -> x0, local copies, waits for them, and re-layouts: 37.1 us -> none  [the longest x4 13.9 us: plane_inverse(): wide_re, wide_im = (shaped[0], shaped[1])]
    all_to_all x1 -> x2, blocking collectives: 30.6 us -> 64.4 us  [swap_slabs(): lax.all_to_all(array, 'slab', split_axis=0, concat_axis=0, tiled=True)]
    slice x9 -> x0, local copies, waits for them, and re-layouts: 27.8 us -> none  [the longest x6 14.3 us: plane_inverse(): wide_re, wide_im = (shaped[0], shaped[1])]
    reshape x1 -> x0, local copies, waits for them, and re-layouts: 26.1 us -> none  [on_device(): grad_spec = summed.reshape(2, chans, pairs, KX * chans)]
  transfers between devices with their start and end apart: 4 -> 4, of which waited for: 2 -> 2; matrix products, arithmetic and copies ran while one was open for 29% -> 7% of each run, Pallas kernels for 0% -> 3%
where the time goes in v1:
time: 270 us; the launch traced here: 268 us
  Pallas kernels  153 us (57%)
  blocking collectives  64.4 us (24%)
  local copies, waits for them, and re-layouts  17.7 us (7%)
  waiting for transfers between devices  15.9 us (6%)
  starting transfers between devices  12.1 us (4%)
  other arithmetic  4.12 us (2%)
    pallas_call x1, Pallas kernels, middle(): call(middle_body, (PLANES,), [whole(arrived), plane_block(), plane_block(...  70.5 us
    all_to_all x2, blocking collectives, swap_slabs(): lax.all_to_all(array, 'slab', split_axis=0, concat_axis=0, tiled=True)  64.4 us
    pallas_call x1, Pallas kernels, last(): call(last_body, (PLANES,), [whole(arrived), plane_block()] + [whole(a) fo...  38.5 us
    convert_element_type x2, local copies, waits for them, and re-layouts, kron_halves(): return wide.reshape(16 * CH, 8 * CH).astype(BF)  15 us
    pallas_call x1, Pallas kernels, spectrum(): call(spectrum_body, (GROUPS,), [pl.BlockSpec((QUAD, PLANES, GY, GZ), lamb...  13.7 us
    pallas_call x1, Pallas kernels, input_modes(): call(input_body, (GROUPS,), [whole(moved), pl.BlockSpec((2, QUAD, PAIRS,...  11.4 us
    all_to_all x2, waiting for transfers between devices, swap_slabs(): lax.all_to_all(array, 'slab', split_axis=0, concat_axis=0, tiled=True)  11.2 us
    pallas_call x1, Pallas kernels, mix(): call(mix_body, (GROUPS,), [pl.BlockSpec((PEERS, 2 * PLANES, TILE), lambda...  10.7 us
  transfers between devices with their start and end apart: 4, of which 2 were waited for; matrix products, arithmetic and copies ran while one was open for 7% of the time, Pallas kernels for 3%

profile of v1, /device:TPU:0, one launch (start us, length us, event | category | flops | bytes accessed | tf_op | source)
XLA Modules:
  0.0 268.1 jit_solution(2614434753812843947)
XLA Ops:
  0.6 13.7 %shard_map.202 = f32[16,16,1024]{2,1,0:T(8,128)} custom-call(f32[32,8,128,128]{3,2,1,0:T(8,128)} %bitcast.19, bf16[128,256]{1,0:T(8,128)(2,1)} %constant.30.clone.yf_ref, bf16[2048,256]{1,0:T(8,128)(2,1)} %constant.32.clone.th_ref, bf16[2048,256]{1,0:T(8,128)(2,1)} %constant.33.clone.tl_ref), custom_call_target="tpu_custom_call" | custom-call | tf_op jit(solution)/shard_map/pallas_call | solution.py:283
  14.4 0.0 copy-start.5
  14.4 32.5 %all_to_all.20.moved_ref = f32[16,16,1024]{2,1,0:T(8,128)} all-to-all(f32[16,16,1024]{2,1,0:T(8,128)} %shard_map.202), channel_id=1, replica_groups=mesh['dp'=2,'slab'=16] {'slab'}, dimensions={0} | all-to-all | bytes 2097152 | tf_op jit(solution)/shard_map/all_to_all | solution.py:645
  46.8 10.7 %shard_map.203 = (f32[64,1024]{1,0:T(8,128)}, f32[16,16,1024]{2,1,0:T(8,128)}) custom-call(f32[16,16,1024]{2,1,0:T(8,128)} %all_to_all.20.moved_ref, f32[2,32,32,1024]{3,2,1,0:T(8,128)} %w_ref.3, bf16[64,256]{1,0:T(8,128)(2,1)} %constant.40.clone.xfh_ref, bf16[64,256]{1,0:T(8,128)(2,1)} %constant.41.clone.xfl_ref, ...), custom_call_target="tpu_custom_call" | custom-call | tf_op jit(solution)/shard_map/pallas_call | solution.py:363
  57.5 5.0 %all-to-all-start.1 = ((f32[16,16,1024]{2,1,0:T(8,128)}), f32[16,16,1024]{2,1,0:T(8,128)S(1)}, u32[]{:S(2)}, u32[]{:S(2)}) async-start(f32[16,16,1024]{2,1,0:T(8,128)} %get-tuple-element.10), calls=%async_computation.1 | async-start | bytes 2097152 | tf_op jit(solution)/shard_map/all_to_all | solution.py:645
  62.5 0.0 copy-done.5
  62.6 0.1 copy.23
  62.7 4.1 %multiply_convert_fusion = (bf16[2,32,8,32,8]{4,3,2,1,0:T(8,128)(2,1)}, bf16[2,32,8,32,8]{4,3,2,1,0:T(8,128)(2,1)}) fusion(f32[2,32,32]{2,1,0:T(8,128)S(1)} %pad_maximum_fusion.1, f32[8,8]{1,0:T(8,128)S(1)} %fusion.2, f32[2,32,32]{2,1,0:T(8,128)S(1)} %copy.23), kind=kLoop, calls=%fused_computation | loop fusion | flops 524288 | bytes 540928 | tf_op jit(solution)/shard_map/convert_element_type | solution.py:641
  66.8 7.5 %convert_element_type.22.kron_ref = bf16[512,256]{1,0:T(8,128)(2,1)} reshape(bf16[2,32,8,32,8]{4,3,2,1,0:T(8,128)(2,1)} %get-tuple-element.22) | data formatting | bytes 524288 | tf_op jit(solution)/shard_map/convert_element_type | solution.py:641
  74.3 11.2 %all-to-all-done.1.arrived_ref = f32[16,16,1024]{2,1,0:T(8,128)S(1)} async-done(((f32[16,16,1024]{2,1,0:T(8,128)}), f32[16,16,1024]{2,1,0:T(8,128)S(1)}, u32[]{:S(2)}, u32[]{:S(2)}) %all-to-all-start.1) | async-done | bytes 1048608 | tf_op jit(solution)/shard_map/all_to_all | solution.py:645
  85.5 0.0 copy-start
  85.5 1.0 copy-done
  86.4 70.5 %shard_map.204 = (f32[32,8,128,128]{3,2,1,0:T(8,128)}, f32[32,8,128,128]{3,2,1,0:T(8,128)}, f32[16,16,1024]{2,1,0:T(8,128)}) custom-call(f32[16,16,1024]{2,1,0:T(8,128)} %copy-done, f32[32,8,128,128]{3,2,1,0:T(8,128)} %bitcast.20, f32[32,8,128,128]{3,2,1,0:T(8,128)} %bitcast.21, bf16[512,256]{1,0:T(8,128)(2,1)} %convert_element_type.22.kron_ref, ...), custom_call_target="tpu_custom_call" | custom-call | tf_op jit(solution)/shard_map/pallas_call | solution.py:579
  157.0 0.0 copy-start.2
  157.0 32.0 %all_to_all.21.moved_ref = f32[16,16,1024]{2,1,0:T(8,128)} all-to-all(f32[16,16,1024]{2,1,0:T(8,128)} %get-tuple-element.12), channel_id=1, replica_groups=mesh['dp'=2,'slab'=16] {'slab'}, dimensions={0} | all-to-all | bytes 2097152 | tf_op jit(solution)/shard_map/all_to_all | solution.py:645
  188.9 11.4 %shard_map.205 = (f32[2,32,1024]{2,1,0:T(8,128)}, f32[16,16,1024]{2,1,0:T(8,128)}) custom-call(f32[16,16,1024]{2,1,0:T(8,128)} %all_to_all.21.moved_ref, f32[2,32,32,1024]{3,2,1,0:T(8,128)} %w_ref.3, bf16[64,256]{1,0:T(8,128)(2,1)} %constant.40.clone.xfh_ref, bf16[64,256]{1,0:T(8,128)(2,1)} %constant.41.clone.xfl_ref, ...), custom_call_target="tpu_custom_call" | custom-call | tf_op jit(solution)/shard_map/pallas_call | solution.py:420
  200.3 5.0 %all-to-all-start.3 = ((f32[16,16,1024]{2,1,0:T(8,128)}), f32[16,16,1024]{2,1,0:T(8,128)S(1)}, u32[]{:S(2)}, u32[]{:S(2)}) async-start(f32[16,16,1024]{2,1,0:T(8,128)} %get-tuple-element.13), calls=%async_computation.3 | async-start | bytes 2097152 | tf_op jit(solution)/shard_map/all_to_all | solution.py:645
  205.3 0.0 copy-done.2
  205.3 1.6 collective-permute-start
  206.9 0.5 collective-permute-start.1
  207.4 7.5 %convert_element_type.24.kron_ref = bf16[512,256]{1,0:T(8,128)(2,1)} reshape(bf16[2,32,8,32,8]{4,3,2,1,0:T(8,128)(2,1)} %get-tuple-element.21) | data formatting | bytes 524288 | tf_op jit(solution)/shard_map/convert_element_type | solution.py:641
  214.9 0.0 collective-permute-done.far_hat_ref
  214.9 0.0 copy-start.3
  214.9 4.7 %collective-permute-done.1.far_g_ref = f32[2,32,1024]{2,1,0:T(8,128)S(1)} collective-permute-done((f32[2,32,1024]{2,1,0:T(8,128)}, f32[2,32,1024]{2,1,0:T(8,128)S(1)}, u32[]{:S(2)}, u32[]{:S(2)}) %collective-permute-start.1) | collective-permute-done | bytes 262176 | tf_op jit(solution)/shard_map/ppermute | solution.py:662
  219.7 0.0 copy-done.3
  219.7 0.0 copy-start.4
  219.7 0.7 copy-done.4
  220.4 8.3 %shard_map.207 = f32[2,32,32,1024]{3,2,1,0:T(8,128)} custom-call(f32[64,1024]{1,0:T(8,128)} %get-tuple-element.15.hat_ref, f32[64,1024]{1,0:T(8,128)} %copy-done.3, f32[2,32,1024]{2,1,0:T(8,128)} %get-tuple-element.16.g_ref, f32[2,32,1024]{2,1,0:T(8,128)} %copy-done.4, bf16[128,2048]{1,0:T(8,128)(2,1)} %constant.43.clone.spread_ref), custom_call_target="tpu_custom_call" | custom-call | tf_op jit(solution)/shard_map/pallas_call | solution.py:454
  228.7 0.0 all-to-all-done.3.arrived_ref
  228.7 0.0 copy-start.1
  228.7 1.0 copy-done.1
  229.7 38.5 %shard_map.206 = f32[32,8,128,128]{3,2,1,0:T(8,128)} custom-call(f32[16,16,1024]{2,1,0:T(8,128)} %copy-done.1, f32[32,8,128,128]{3,2,1,0:T(8,128)} %get-tuple-element.14.grad_ref, bf16[512,256]{1,0:T(8,128)(2,1)} %convert_element_type.24.kron_ref, bf16[128,192]{1,0:T(8,128)(2,1)} %constant.31.clone.yi_ref, bf16[256,2048]{1,0:T(8,128)(2,1)} %constant.38.clone.zjh_ref, ...), custom_call_target="tpu_custom_call" | custom-call | tf_op jit(solution)/shard_map/pallas_call | solution.py:621
  (5 shorter events, 0.0 us)
Async XLA Ops:
  14.4 48.2 %copy-start.5 = (f32[32,32]{1,0:T(8,128)S(1)}, f32[32,32]{1,0:T(8,128)}, u32[]{:S(2)}) copy-start(f32[32,32]{1,0:T(8,128)} %param.22) | copy-start | bytes 12292
  57.5 27.9 %all-to-all-start.1 = ((f32[16,16,1024]{2,1,0:T(8,128)}), f32[16,16,1024]{2,1,0:T(8,128)S(1)}, u32[]{:S(2)}, u32[]{:S(2)}) async-start(f32[16,16,1024]{2,1,0:T(8,128)} %get-tuple-element.10), calls=%async_computation.1 | async-start | bytes 2097152 | tf_op jit(solution)/shard_map/all_to_all | solution.py:645
  85.5 1.0 copy-start
  157.0 48.4 %copy-start.2 = (f32[64,1024]{1,0:T(8,128)S(1)}, f32[64,1024]{1,0:T(8,128)}, u32[]{:S(2)}) copy-start(f32[64,1024]{1,0:T(8,128)} %get-tuple-element.15.hat_ref) | copy-start | bytes 786436
  200.3 28.3 %all-to-all-start.3 = ((f32[16,16,1024]{2,1,0:T(8,128)}), f32[16,16,1024]{2,1,0:T(8,128)S(1)}, u32[]{:S(2)}, u32[]{:S(2)}) async-start(f32[16,16,1024]{2,1,0:T(8,128)} %get-tuple-element.13), calls=%async_computation.3 | async-start | bytes 2097152 | tf_op jit(solution)/shard_map/all_to_all | solution.py:645
  205.3 9.6 %collective-permute-start = (f32[64,1024]{1,0:T(8,128)S(1)}, f32[64,1024]{1,0:T(8,128)S(1)}, u32[]{:S(2)}, u32[]{:S(2)}) collective-permute-start(f32[64,1024]{1,0:T(8,128)S(1)} %copy-done.2), channel_id=1, source_target_pairs={{0,16},{16,0},{1,17},{17,1},{2,18},{18,2},{3,19},{19,3},{4,20},{20... | collective-permute-start | bytes 786440 | tf_op jit(solution)/shard_map/ppermute | solution.py:659
  206.9 12.8 %collective-permute-start.1 = (f32[2,32,1024]{2,1,0:T(8,128)}, f32[2,32,1024]{2,1,0:T(8,128)S(1)}, u32[]{:S(2)}, u32[]{:S(2)}) collective-permute-start(f32[2,32,1024]{2,1,0:T(8,128)} %get-tuple-element.16.g_ref), channel_id=1, source_target_pairs={{0,16},{16,0},{1,17},{17,1},{2,18},{18,2},{3,19},{19,3},{4,20},{20... | collective-permute-start | bytes 786440 | tf_op jit(solution)/shard_map/ppermute | solution.py:662
  214.9 4.7 %copy-start.3 = (f32[64,1024]{1,0:T(8,128)}, f32[64,1024]{1,0:T(8,128)S(1)}, u32[]{:S(2)}) copy-start(f32[64,1024]{1,0:T(8,128)S(1)} %collective-permute-done.far_hat_ref) | copy-start | bytes 786436
  219.7 0.7 copy-start.4
  228.7 1.0 copy-start.1

commit v2 on v0

--- a/solution.py
+++ b/solution.py
@@ -1,8 +1,13 @@
+import functools
 import math
 
 import jax
 import jax.numpy as jnp
+import ml_dtypes
+import numpy as np
 from jax import lax
+from jax.experimental import pallas as pl
+from jax.experimental.pallas import tpu as pltpu
 from jax.sharding import PartitionSpec as P
 
 GX = 128
@@ -84,7 +89,7 @@
     )
 
 
-def on_device(field, cotangent, spec_weight, bypass_weight):
+def on_device_any(field, cotangent, spec_weight, bypass_weight):
     count = lax.axis_size("slab")
     pairs = KY * KZ // count
     chans = field.shape[1]
@@ -140,6 +145,595 @@
     return (result[None], back_field[None], grad_spec)
 
 
+CH = 32
+PLANES = 8
+PAIRS = 32
+PEERS = 16
+KYL = PAIRS // KZ
+KYH = KY // KYL
+QUAD = 4
+GROUPS = CH // QUAD
+TILE = QUAD * PAIRS
+BLOCKS = QUAD * KYL
+WIDE = BLOCKS * 2 * GZ
+ROWS = PLANES * KYH
+MODES_O = KX * CH
+
+VMEM = 56 * 1024 * 1024
+
+BF = jnp.bfloat16
+F32 = jnp.float32
+
+
+def split_table(table):
+    high = table.astype(ml_dtypes.bfloat16)
+    low = (table - high.astype(np.float64)).astype(ml_dtypes.bfloat16)
+    return high, low
+
+
+def phases(length, count, signed):
+    freqs = np.arange(count)
+    if signed:
+        freqs = np.where(freqs < count // 2, freqs, freqs - count)
+    phase = (np.arange(length)[:, None] * freqs[None, :]) % length
+    angle = phase * (2.0 * np.pi / length)
+    return np.cos(angle), np.sin(angle)
+
+
+@functools.lru_cache(maxsize=None)
+def host_tables():
+    zc, zs = phases(GZ, KZ, False)
+    yc, ys = phases(GY, KY, True)
+    xc, xs = phases(GX, KX, True)
+    fold = np.where(np.arange(KZ) == 0, 1.0, 2.0) / float(GX * GY * GZ)
+    out = {}
+    ycr = yc.T.reshape(KYH, KYL, GY).transpose(1, 0, 2)
+    ysr = ys.T.reshape(KYH, KYL, GY).transpose(1, 0, 2)
+    fwd = np.stack([ycr, -ysr], axis=1).reshape(2 * KY, GY)
+    high, low = split_table(fwd)
+    out["yf"] = np.block([[high, high], [low, low]])
+    inv = np.stack([ycr, -ysr], axis=1).reshape(2 * KY, GY).T
+    high, low = split_table(inv)
+    out["yi"] = np.concatenate([high, high, low], axis=1)
+    core = np.stack([np.stack([zc, -zs]), np.stack([zs, zc])])
+    for name, scale in (("zf", np.ones(KZ)), ("zg", fold)):
+        table = (core * scale).transpose(0, 2, 1, 3)[:, :, :, None, :]
+        table = np.broadcast_to(table, (2, GZ, 2, BLOCKS, KZ))
+        high, low = split_table(table.reshape(2 * GZ, 2 * TILE))
+        out[name] = np.stack([high, low])
+    core = np.stack([np.stack([zc, zs]), np.stack([-zs, zc])])
+    for name, scale in (("zi", fold), ("zj", np.ones(KZ))):
+        table = np.zeros((2, QUAD, KYL, KZ, QUAD, KYL, 2, GZ))
+        for q in range(QUAD):
+            for k in range(KYL):
+                table[:, q, k, :, q, k, :, :] = (core * scale).transpose(0, 3, 1, 2)
+        out[name + "h"], out[name + "l"] = split_table(table.reshape(2 * TILE, WIDE))
+    core = np.stack([np.stack([xc, xs]), np.stack([-xs, xc])])
+    table = core.reshape(2, 2, PEERS, PLANES, KX).transpose(0, 4, 2, 1, 3).reshape(2 * KX, 2 * GX)
+    high, low = split_table(table)
+    out["xfh"], out["xfl"] = high, low
+    core = np.stack([np.stack([xc, -xs]), np.stack([xs, xc])])
+    table = core.reshape(2, 2, PEERS, PLANES, KX).transpose(2, 0, 3, 1, 4).reshape(2 * GX, 2 * KX)
+    high, low = split_table(table)
+    out["xi"] = np.concatenate([high, high, low], axis=1)
+    spread = np.repeat(np.eye(2 * KX), CH, axis=1).astype(ml_dtypes.bfloat16)
+    out["spread"] = np.concatenate([spread, spread], axis=0)
+    out["rep"] = np.repeat(np.eye(CH), 8, axis=0).astype(ml_dtypes.bfloat16)
+    out["gather"] = np.concatenate([spread, spread], axis=0).T.copy()
+    return out
+
+
+def halves(values):
+    high = values.astype(BF)
+    return high, (values - high.astype(F32)).astype(BF)
+
+
+def dot(left, right):
+    return jnp.dot(left, right, preferred_element_type=F32)
+
+
+def dot3(high, low, table_high, table_low):
+    rows = high.shape[0]
+    both = dot(jnp.concatenate([high, low], axis=0), table_high)
+    return both[:rows] + both[rows:] + dot(high, table_low)
+
+
+def lines_to_modes(pair, yf):
+    high, low = halves(pair)
+    both = dot(yf, jnp.concatenate([high, low], axis=0))
+    return halves(both[: 2 * KY] + both[2 * KY :])
+
+
+def call(body, us, grid, ins, outs, shapes, scratch, aliases=None):
+    return pl.pallas_call(
+        body,
+        grid=grid,
+        in_specs=ins,
+        out_specs=outs,
+        out_shape=shapes,
+        scratch_shapes=scratch,
+        input_output_aliases=aliases or {},
+        cost_estimate=pl.CostEstimate(flops=int(us * 1e9), bytes_accessed=int(us * 3e6), transcendentals=0),
+        compiler_params=pltpu.CompilerParams(
+            dimension_semantics=("arbitrary",), vmem_limit_bytes=VMEM
+        ),
+    )
+
+
+def whole(array):
+    zeros = (0,) * array.ndim
+    return pl.BlockSpec(array.shape, lambda step: zeros)
+
+
+def store_modes(high, low, x, half, high_s, low_s):
+    for j in range(2):
+        for k in range(KYL):
+            to = ((2 * half + j) * KYL + k) * ROWS + x * KYH
+            for part in range(2):
+                rows = slice((2 * k + part) * KYH, (2 * k + part + 1) * KYH)
+                take = (rows, slice(j * GZ, (j + 1) * GZ))
+                put = (slice(to, to + KYH), slice(part * GZ, (part + 1) * GZ))
+                high_s[put] = high[take]
+                low_s[put] = low[take]
+
+
+def send_modes(high_s, low_s, table_ref, out_ref):
+    full = dot3(high_s[...], low_s[...], table_ref[0], table_ref[1])
+    owner = lax.broadcasted_iota(jnp.int32, (ROWS, 2 * TILE), 1) % TILE // KZ
+    sums = full[:ROWS]
+    for i in range(1, BLOCKS):
+        sums = jnp.where(owner == i, full[i * ROWS : (i + 1) * ROWS], sums)
+    for part in range(2):
+        block = sums[:, part * TILE : (part + 1) * TILE].reshape(PLANES, KYH, TILE)
+        out_ref[:, part * PLANES : (part + 1) * PLANES, :] = jnp.swapaxes(block, 0, 1)
+
+
+def spectrum_body(f_ref, yf_ref, table_ref, out_ref, high_s, low_s):
+    yf = yf_ref[...]
+    for x in range(PLANES):
+        for half in range(2):
+            pair = jnp.concatenate([f_ref[2 * half, x], f_ref[2 * half + 1, x]], axis=1)
+            high, low = lines_to_modes(pair, yf)
+            store_modes(high, low, x, half, high_s, low_s)
+    send_modes(high_s, low_s, table_ref, out_ref)
+
+
+def channel_block(first):
+    return pl.BlockSpec((QUAD, PLANES, GY, GZ), lambda g: (g + first, 0, 0, 0))
+
+
+def moved_block():
+    return pl.BlockSpec((PEERS, 2 * PLANES, TILE), lambda g: (0, 0, g))
+
+
+def moved_shape(groups):
+    return jax.ShapeDtypeStruct((PEERS, 2 * PLANES, groups * TILE), F32)
+
+
+def mode_scratch():
+    return [pltpu.VMEM((BLOCKS * ROWS, 2 * GZ), BF), pltpu.VMEM((BLOCKS * ROWS, 2 * GZ), BF)]
+
+
+def spectrum(field, first, count, t):
+    tables = (t["yf"], t["zf"])
+    return call(
+        spectrum_body,
+        2 * count,
+        (count,),
+        [channel_block(first)] + [whole(a) for a in tables],
+        moved_block(),
+        moved_shape(count),
+        mode_scratch(),
+    )(field, *tables)
+
+
+def own_mask():
+    rows = lax.broadcasted_iota(jnp.int32, (TILE, TILE), 0) % QUAD
+    lanes = lax.broadcasted_iota(jnp.int32, (TILE, TILE), 1) // PAIRS
+    return rows == lanes
+
+
+def x_forward(moved, xfh, xfl):
+    high, low = halves(moved)
+    both = dot(jnp.concatenate([xfh, xfl], axis=0), high)
+    return both[: 2 * KX] + both[2 * KX :] + dot(xfh, low)
+
+
+def x_inverse(spec, xi):
+    high, low = halves(spec)
+    return dot(xi, jnp.concatenate([high, low, high], axis=0))
+
+
+def spread_modes(spec, spread):
+    turned = jnp.concatenate([spec, spec], axis=0).T
+    high, low = halves(turned)
+    lanes = lax.broadcasted_iota(jnp.int32, (TILE, 4 * KX), 1)
+    return dot(jnp.where(lanes < 2 * KX, high, low), spread)
+
+
+def mix_body(first, last, count, *refs):
+    moved_ref, w_ref, xfh_ref, xfl_ref, spread_ref, xi_ref = refs[:6]
+    refs = refs[6:]
+    if not first:
+        start_ref, refs = refs[0], refs[1:]
+    hat_ref, refs = refs[0], refs[1:]
+    if last:
+        out_refs, (acc_s, turn_s) = refs[:-2], refs[-2:]
+    else:
+        (acc_s,) = refs
+    step = pl.program_id(0)
+
+    @pl.when(step == 0)
+    def _():
+        acc_s[...] = jnp.zeros_like(acc_s) if first else start_ref[...]
+
+    hat = x_forward(moved_ref[...].reshape(2 * GX, TILE), xfh_ref[...], xfl_ref[...])
+    hat_ref[...] = hat
+    wide = spread_modes(hat, spread_ref[...])
+    acc_re, acc_im = acc_s[0], acc_s[1]
+    for q in range(QUAD):
+        h_re = wide[q * PAIRS : (q + 1) * PAIRS, :MODES_O]
+        h_im = wide[q * PAIRS : (q + 1) * PAIRS, MODES_O:]
+        w_re, w_im = w_ref[0, q], w_ref[1, q]
+        acc_re = acc_re + (h_re * w_re - h_im * w_im)
+        acc_im = acc_im + (h_re * w_im + h_im * w_re)
+    acc_s[0] = acc_re
+    acc_s[1] = acc_im
+
+    if last:
+
+        @pl.when(step == count - 1)
+        def _():
+            mask = own_mask()
+            for part in range(2):
+                full = jnp.concatenate([acc_s[part]] * QUAD, axis=0)
+                for k in range(MODES_O // TILE):
+                    turned = full[:, k * TILE : (k + 1) * TILE].T
+                    turn_s[pl.ds(part * MODES_O + k * TILE, TILE), :] = jnp.where(mask, turned, 0.0)
+            xi = xi_ref[...]
+            per = GROUPS // len(out_refs)
+            for g in range(0, GROUPS, 2):
+                tiles = []
+                for h in range(g, g + 2):
+                    parts = []
+                    for part in range(2):
+                        total = None
+                        for q in range(QUAD):
+                            rows = turn_s[pl.ds(part * MODES_O + h * QUAD + q, KX, stride=CH), :]
+                            total = rows if total is None else total + rows
+                        parts.append(total)
+                    tiles.append(jnp.concatenate(parts, axis=0))
+                wave = x_inverse(jnp.concatenate(tiles, axis=1), xi).reshape(PEERS, 2 * PLANES, 2 * TILE)
+                for h in range(g, g + 2):
+                    to = (h % per) * TILE
+                    out_refs[h // per][:, :, to : to + TILE] = wave[:, :, (h - g) * TILE : (h - g + 1) * TILE]
+
+
+def mix(moved, weights, start, at, count, chunks, t):
+    first, last = start is None, at + count == GROUPS
+    tables = (t["xfh"], t["xfl"], t["spread"], t["xi"])
+    operands = (moved, weights) + tables + (() if first else (start,))
+    acc = jax.ShapeDtypeStruct((2, PAIRS, MODES_O), F32)
+    outs = [moved_shape(n) for n in chunks] if last else [acc]
+    scratch = [pltpu.VMEM(acc.shape, F32), pltpu.VMEM((2 * MODES_O, TILE), F32)] if last else []
+    return call(
+        functools.partial(mix_body, first, last, count),
+        6,
+        (count,),
+        [moved_block(), pl.BlockSpec((2, QUAD, PAIRS, MODES_O), lambda g: (0, g + at, 0, 0))]
+        + [whole(a) for a in operands[2:]],
+        [pl.BlockSpec((2 * KX, TILE), lambda g: (0, g))] + [whole(a) for a in outs],
+        [jax.ShapeDtypeStruct((2 * KX, count * TILE), F32)] + outs,
+        scratch,
+    )(*operands)
+
+
+def input_body(first, moved_refs, g_ref, w_ref, xfh_ref, xfl_ref, gather_ref, xi_ref, out_ref, turn_s):
+    if first:
+
+        @pl.when(pl.program_id(0) == 0)
+        def _():
+            lanes = lax.broadcasted_iota(jnp.int32, (KX, TILE), 1) // PAIRS
+            per = GROUPS // len(moved_refs)
+            for h in range(GROUPS):
+                at = (h % per) * TILE
+                tile = moved_refs[h // per][:, :, at : at + TILE].reshape(2 * GX, TILE)
+                hat = x_forward(tile, xfh_ref[...], xfl_ref[...])
+                for part in range(2):
+                    rows = hat[part * KX : (part + 1) * KX]
+                    for q in range(QUAD):
+                        to = pl.ds(part * MODES_O + h * QUAD + q, KX, stride=CH)
+                        turn_s[to, :] = jnp.where(lanes == q, rows, 0.0)
+            for part in range(2):
+                for k in range(MODES_O // TILE):
+                    turned = turn_s[pl.ds(part * MODES_O + k * TILE, TILE), :].T
+                    total = turned[:PAIRS]
+                    for q in range(1, QUAD):
+                        total = total + turned[q * PAIRS : (q + 1) * PAIRS]
+                    g_ref[part, :, k * TILE : (k + 1) * TILE] = total
+
+    g_re, g_im = g_ref[0], g_ref[1]
+    rows_high, rows_low = [], []
+    for q in range(QUAD):
+        w_re, w_im = w_ref[0, q], w_ref[1, q]
+        full = jnp.concatenate([g_re * w_re + g_im * w_im, g_im * w_re - g_re * w_im], axis=1)
+        high, low = halves(full)
+        rows_high.append(high)
+        rows_low.append(low)
+    both = dot(jnp.concatenate(rows_high + rows_low, axis=0), gather_ref[...])
+    spec = (both[:TILE] + both[TILE:]).T[: 2 * KX]
+    out_ref[...] = x_inverse(spec, xi_ref[...]).reshape(PEERS, 2 * PLANES, TILE)
+
+
+def input_modes(moved, grad, weights, at, count, t):
+    tables = (t["xfh"], t["xfl"], t["gather"], t["xi"])
+    shape = jax.ShapeDtypeStruct((2, PAIRS, MODES_O), F32)
+    weight_spec = pl.BlockSpec((2, QUAD, PAIRS, MODES_O), lambda g: (0, g + at, 0, 0))
+    first = grad is None
+    if first:
+
+        def body(*refs):
+            n = len(moved)
+            w, xfh, xfl, gather, xi, g, out, turn = refs[n:]
+            input_body(True, refs[:n], g, w, xfh, xfl, gather, xi, out, turn)
+
+        return call(
+            body,
+            7,
+            (count,),
+            [whole(a) for a in moved] + [weight_spec] + [whole(a) for a in tables],
+            [whole(shape), moved_block()],
+            [shape, moved_shape(count)],
+            [pltpu.VMEM((2 * MODES_O, TILE), F32)],
+        )(*moved, weights, *tables)
+
+    def body(g, w, xfh, xfl, gather, xi, out):
+        input_body(False, None, g, w, xfh, xfl, gather, xi, out, None)
+
+    out = call(
+        body,
+        6,
+        (count,),
+        [whole(shape), weight_spec] + [whole(a) for a in tables],
+        moved_block(),
+        moved_shape(count),
+        [],
+    )(grad, weights, *tables)
+    return grad, out
+
+
+def weight_grad_body(hat_ref, far_hat_ref, g_ref, far_g_ref, spread_ref, out_ref):
+    spread = spread_ref[...]
+    near = spread_modes(hat_ref[...], spread)
+    far = spread_modes(far_hat_ref[...], spread)
+    for q in range(QUAD):
+        rows = slice(q * PAIRS, (q + 1) * PAIRS)
+        n_re, n_im = near[rows, :MODES_O], near[rows, MODES_O:]
+        f_re, f_im = far[rows, :MODES_O], far[rows, MODES_O:]
+        out_ref[0, q] = n_re * g_ref[0] + n_im * g_ref[1] + f_re * far_g_ref[0] + f_im * far_g_ref[1]
+        out_ref[1, q] = n_re * g_ref[1] - n_im * g_ref[0] + f_re * far_g_ref[1] - f_im * far_g_ref[0]
+
+
+def weight_grad(hat, far_hat, grad, far_grad, t):
+    tile = pl.BlockSpec((2 * KX, TILE), lambda g: (0, g))
+    return call(
+        weight_grad_body,
+        8,
+        (GROUPS,),
+        [tile, tile, whole(grad), whole(far_grad), whole(t["spread"])],
+        pl.BlockSpec((2, QUAD, PAIRS, MODES_O), lambda g: (0, g, 0, 0)),
+        jax.ShapeDtypeStruct((2, CH, PAIRS, MODES_O), F32),
+        [],
+    )(hat, far_hat, grad, far_grad, t["spread"])
+
+
+def gelu_parts(pre):
+    bell = jnp.exp(pre * pre * -0.5)
+    t = 1.0 / (1.0 + (0.3275911 * math.sqrt(0.5)) * jnp.abs(pre))
+    poly = 1.061405429 * 0.5
+    for coefficient in (-1.453152027, 1.421413741, -0.284496736, 0.254829592):
+        poly = poly * t + coefficient * 0.5
+    tail = poly * t * bell
+    share = jnp.where(pre >= 0.0, 1.0 - tail, tail)
+    return share, pre * bell * (1.0 / math.sqrt(2.0 * math.pi))
+
+
+def arrive(arrived_ref, zih, zil):
+    parts = []
+    for part in range(2):
+        block = arrived_ref[:, part * PLANES : (part + 1) * PLANES, :]
+        parts.append(jnp.swapaxes(block, 0, 1).reshape(PLANES * KYH, TILE))
+    high, low = halves(jnp.concatenate(parts, axis=1))
+    return halves(dot3(high, low, zih, zil))
+
+
+def inverse_pair(high, low, x, half, yi):
+    stacks = []
+    for source in (high, low):
+        sides = []
+        for j in range(2):
+            lanes = (2 * half + j) * 2 * KYL * GZ
+            pieces = [
+                source[x * KYH : (x + 1) * KYH, lanes + k * GZ : lanes + (k + 1) * GZ] for k in range(2 * KYL)
+            ]
+            sides.append(jnp.concatenate(pieces, axis=0))
+        stacks.append(jnp.concatenate(sides, axis=1))
+    return dot(yi, jnp.concatenate([stacks[0], stacks[1], stacks[0]], axis=0))
+
+
+def kron_halves(matrix, rep):
+    rows = lax.broadcasted_iota(jnp.int32, (8 * CH, 8 * CH), 0) % 8
+    lanes = lax.broadcasted_iota(jnp.int32, (8 * CH, 8 * CH), 1) % 8
+    wide = []
+    for half in halves(matrix):
+        tall = dot(rep, half).astype(BF)
+        full = lax.dot_general(tall, rep, (((1,), (1,)), ((), ())), preferred_element_type=F32)
+        wide.append(jnp.where(rows == lanes, full, 0.0).astype(BF))
+    return jnp.concatenate(wide, axis=0)
+
+
+def channel_sum_body(data_ref, matrix_ref, rep_ref, *refs):
+    out_ref, kron_s = refs[-2:]
+
+    @pl.when(pl.program_id(0) == 0)
+    def _():
+        kron_s[...] = kron_halves(matrix_ref[...], rep_ref[...])
+
+    for x in range(data_ref.shape[1]):
+        for i in range(GY // 16):
+            tiles = [data_ref[:, x, i * 16 + 8 * j : i * 16 + 8 * j + 8, :].reshape(8 * CH, GZ) for j in range(2)]
+            high, low = halves(jnp.concatenate(tiles, axis=1))
+            both = dot(kron_s[...], high)
+            sums = both[: 8 * CH] + both[8 * CH :] + dot(kron_s[: 8 * CH], low)
+            for j in range(2):
+                at = slice(i * 16 + 8 * j, i * 16 + 8 * j + 8)
+                out_ref[:, x, at, :] = sums[:, j * GZ : (j + 1) * GZ].reshape(CH, 8, GZ)
+
+
+def channel_sum(data, matrix, first, count, step, so_far, t):
+    block = pl.BlockSpec((CH, step, GY, GZ), lambda x: (0, x + first // step, 0, 0))
+    return call(
+        channel_sum_body,
+        2 * count,
+        (count // step,),
+        [block, whole(matrix), whole(t["rep"])] + [pl.BlockSpec(memory_space=pl.ANY)] * len(so_far),
+        block,
+        jax.ShapeDtypeStruct(data.shape, F32),
+        [pltpu.VMEM((16 * CH, 8 * CH), BF)],
+        aliases={3 + i: i for i in range(len(so_far))},
+    )(data, matrix, t["rep"], *so_far)
+
+
+def middle_body(
+    arrived_ref, sum_ref, cot_ref, yi_ref, zih_ref, zil_ref, yf_ref, zg_ref, *refs
+):
+    out_ref, grad_ref, spec_ref, high_s, low_s = refs[-5:]
+    high, low = arrive(arrived_ref, zih_ref[...], zil_ref[...])
+    yi, yf = yi_ref[...], yf_ref[...]
+    for x in range(PLANES):
+        for half in range(2):
+            waves = inverse_pair(high, low, x, half, yi)
+            grads = []
+            for j in range(2):
+                c = 2 * half + j
+                pre = waves[:, j * GZ : (j + 1) * GZ] + sum_ref[c, x]
+                share, slope = gelu_parts(pre)
+                out_ref[c, x] = pre * share
+                grad = cot_ref[c, x] * (share + slope)
+                grad_ref[c, x] = grad
+                grads.append(grad)
+            store_modes(*lines_to_modes(jnp.concatenate(grads, axis=1), yf), x, half, high_s, low_s)
+    send_modes(high_s, low_s, zg_ref, spec_ref)
+
+
+def middle(arrived, sums, cotangent, first, count, so_far, t):
+    tables = (t["yi"], t["zih"], t["zil"], t["yf"], t["zg"])
+    block = channel_block(first)
+    shape = jax.ShapeDtypeStruct(sums.shape, F32)
+    n = 3 + len(tables)
+    return call(
+        middle_body,
+        5 * count,
+        (count,),
+        [moved_block(), block, block] + [whole(a) for a in tables] + [pl.BlockSpec(memory_space=pl.ANY)] * len(so_far),
+        [block, block, moved_block()],
+        [shape, shape, moved_shape(count)],
+        mode_scratch(),
+        aliases={n + i: i for i in range(len(so_far))},
+    )(arrived, sums, cotangent, *tables, *so_far)
+
+
+def last_body(arrived_ref, sum_ref, yi_ref, zjh_ref, zjl_ref, *refs):
+    out_ref = refs[-1]
+    high, low = arrive(arrived_ref, zjh_ref[...], zjl_ref[...])
+    yi = yi_ref[...]
+    for x in range(PLANES):
+        for half in range(2):
+            waves = inverse_pair(high, low, x, half, yi)
+            for j in range(2):
+                c = 2 * half + j
+                out_ref[c, x] = waves[:, j * GZ : (j + 1) * GZ] + sum_ref[c, x]
+
+
+def last(arrived, sums, first, count, so_far, t):
+    tables = (t["yi"], t["zjh"], t["zjl"])
+    block = channel_block(first)
+    n = 2 + len(tables)
+    return call(
+        last_body,
+        2.5 * count,
+        (count,),
+        [moved_block(), block] + [whole(a) for a in tables] + [pl.BlockSpec(memory_space=pl.ANY)] * len(so_far),
+        block,
+        jax.ShapeDtypeStruct(sums.shape, F32),
+        [],
+        aliases={n + i: i for i in range(len(so_far))},
+    )(arrived, sums, *tables, *so_far)
+
+
+def swap_slabs(array):
+    return lax.all_to_all(array, "slab", split_axis=0, concat_axis=0, tiled=True)
+
+
+CHUNKS = (4, 4)
+STARTS = tuple(sum(CHUNKS[:k]) for k in range(len(CHUNKS)))
+
+
+def on_device(field, cotangent, spec_weight, bypass_weight):
+    shape = (field.shape[1], field.shape[2], spec_weight.shape[2], lax.axis_size("slab"), lax.axis_size("dp"))
+    if shape != (CH, PLANES, PAIRS, PEERS, 2):
+        return on_device_any(field, cotangent, spec_weight, bypass_weight)
+    t = {name: jnp.asarray(table) for name, table in host_tables().items()}
+    source, other = field[0], cotangent[0]
+    swap_pair = [(0, 1), (1, 0)]
+    parts = list(zip(STARTS, CHUNKS))
+    ahead = lax.optimization_barrier
+
+    moved = []
+    for at, n in parts:
+        sent = spectrum(source, at, n, t)
+        if moved:
+            moved[-1], sent = ahead((moved[-1], sent))
+        moved.append(swap_slabs(sent))
+    turned = bypass_weight.T
+    sums = channel_sum(source, turned, 0, PLANES // 2, 1, (), t)
+    moved[-1], sums = ahead((moved[-1], sums))
+    hats, state = [], None
+    for arrived, (at, n) in zip(moved, parts):
+        hat, *state = mix(arrived, spec_weight, state[0] if state else None, at, n, CHUNKS, t)
+        hats.append(hat)
+    sums = channel_sum(source, turned, PLANES // 2, PLANES // 2, 1, (sums,), t)
+    so_far, cot_moved, arrived = (), [], []
+    for sent in state:
+        if arrived:
+            arrived[-1], sums, sent = ahead((arrived[-1], sums, sent))
+        arrived.append(swap_slabs(sent))
+    for k, (at, n) in enumerate(parts):
+        *so_far, sent = middle(arrived[k], sums, other, at, n, so_far, t)
+        if k == 0:
+            arrived[-1], sent = ahead((arrived[-1], sent))
+        else:
+            cot_moved[-1], sent = ahead((cot_moved[-1], sent))
+        cot_moved.append(swap_slabs(sent))
+    result, grad_pre = so_far
+    back_sums = channel_sum(grad_pre, bypass_weight, 0, PLANES, 2, (), t)
+    hat = jnp.concatenate(hats, axis=1)
+    far_hat = lax.ppermute(hat, "dp", swap_pair)
+    cot_moved[-1], back_sums, far_hat = ahead((cot_moved[-1], back_sums, far_hat))
+    grad, back_arrived = None, []
+    for at, n in parts:
+        grad, sent = input_modes(cot_moved, grad, spec_weight, at, n, t)
+        if back_arrived:
+            far_grad = lax.ppermute(grad, "dp", swap_pair)
+            grad_spec = weight_grad(hat, far_hat, grad, far_grad, t)
+            back_arrived[-1], sent, grad_spec = ahead((back_arrived[-1], sent, grad_spec))
+        back_arrived.append(swap_slabs(sent))
+    back = ()
+    for k, (at, n) in enumerate(parts):
+        back = (last(back_arrived[k], back_sums, at, n, back, t),)
+    return (result[None], back[0][None], grad_spec)
+
+
 def solution(mesh):
     in_specs = (
         P("dp", None, "slab", None, None),

time: 802 us -> 212 us (0.26)
  matrix products: 430 us -> 0 us
  local copies, waits for them, and re-layouts: 179 us -> 4.74 us
  Pallas kernels: 0 us -> 142 us
  other arithmetic: 101 us -> 0 us
  blocking collectives: 30.6 us -> 0 us
  starting transfers between devices: 18.5 us -> 48.7 us
  between operations: 15 us -> 0.86 us
    dot_general x42 -> x0, matrix products: 430 us -> none  [the longest x2 115 us: plane_inverse(): jnp.einsum('cxky,zk->cxyz', plane_im, z_sin, precision=precise)]
    pallas_call x0 -> x14, Pallas kernels: none -> 142 us  [the longest x2 40.1 us: middle(): call(middle_body, 5 * count, (count,), [moved_block(), block, block] + [w...]
    another operation x6 -> x0, other arithmetic: 56.3 us -> none  [the longest x2 55.3 us: on_device(): summed = lax.psum(jnp.stack([own_real, own_imag]), 'dp')]
    squeeze x6 -> x0, local copies, waits for them, and re-layouts: 37.1 us -> none  [the longest x4 13.9 us: plane_inverse(): wide_re, wide_im = (shaped[0], shaped[1])]
    unnamed x43 -> x28, local copies, waits for them, and re-layouts: 39.9 us -> 3.82 us
    all_to_all x1 -> x0, blocking collectives: 30.6 us -> none  [on_device(): lax.all_to_all(cot_spec, 'slab', split_axis=3, concat_axis=2, tiled=True)]
    slice x9 -> x0, local copies, waits for them, and re-layouts: 27.8 us -> none  [the longest x6 14.3 us: plane_inverse(): wide_re, wide_im = (shaped[0], shaped[1])]
    all_to_all x3 -> x8, starting transfers between devices: 18.4 us -> 45.6 us  [swap_slabs(): lax.all_to_all(array, 'slab', split_axis=0, concat_axis=0, tiled=True)]
  transfers between devices with their start and end apart: 4 -> 10, of which waited for: 2 -> 3; matrix products, arithmetic and copies ran while one was open for 29% -> 1% of each run, Pallas kernels for 0% -> 53%
where the time goes in v2:
time: 212 us; the launch traced here: 210 us
  Pallas kernels  142 us (67%)
  starting transfers between devices  48.7 us (23%)
  waiting for transfers between devices  13.7 us (6%)
  local copies, waits for them, and re-layouts  4.74 us (2%)
    all_to_all x8, starting transfers between devices, swap_slabs(): lax.all_to_all(array, 'slab', split_axis=0, concat_axis=0, tiled=True)  45.6 us
    pallas_call x2, Pallas kernels, middle(): call(middle_body, 5 * count, (count,), [moved_block(), block, block] + [w...  40.1 us
    pallas_call x3, Pallas kernels, channel_sum(): call(channel_sum_body, 2 * count, (count // step,), [block, whole(matrix)...  33.9 us
    pallas_call x2, Pallas kernels, last(): call(last_body, 2.5 * count, (count,), [moved_block(), block] + [whole(a)...  19.4 us
    pallas_call x2, Pallas kernels, spectrum(): call(spectrum_body, 2 * count, (count,), [channel_block(first)] + [whole(...  14.8 us
    all_to_all x8, waiting for transfers between devices, swap_slabs(): lax.all_to_all(array, 'slab', split_axis=0, concat_axis=0, tiled=True)  13.7 us
    pallas_call x2, Pallas kernels, mix(): call(functools.partial(mix_body, first, last, count), 6, (count,), [moved...  12.3 us
    pallas_call x1, Pallas kernels, weight_grad(): call(weight_grad_body, 8, (GROUPS,), [tile, tile, whole(grad), whole(far_...  8.32 us
  transfers between devices with their start and end apart: 10, of which 3 were waited for; matrix products, arithmetic and copies ran while one was open for 1% of the time, Pallas kernels for 53%

profile of v2, /device:TPU:0, one launch (start us, length us, event | category | flops | bytes accessed | tf_op | source)
XLA Modules:
  0.0 209.9 jit_solution(3681431952950039332)
XLA Ops:
  0.6 7.4 %shard_map.193 = f32[16,16,512]{2,1,0:T(8,128)} custom-call(f32[32,8,128,128]{3,2,1,0:T(8,128)} %bitcast.5, bf16[128,256]{1,0:T(8,128)(2,1)} %constant.28.clone.yf_ref, bf16[2,256,256]{2,1,0:T(8,128)(2,1)} %constant.30.clone.table_ref), custom_call_target="tpu_custom_call" | custom-call | flops 8000000000 | bytes 24000000 | tf_op jit(solution)/shard_map/pallas_call | solution.py:319
  8.1 7.4 %all-to-all-start = ((f32[16,16,512]{2,1,0:T(8,128)}), f32[16,16,512]{2,1,0:T(8,128)S(1)}, u32[]{:S(2)}, u32[]{:S(2)}) async-start(f32[16,16,512]{2,1,0:T(8,128)} %shard_map.193), calls=%async_computation | async-start | bytes 1048576 | tf_op jit(solution)/shard_map/all_to_all | solution.py:675
  16.1 7.4 %shard_map.194 = f32[16,16,512]{2,1,0:T(8,128)} custom-call(f32[32,8,128,128]{3,2,1,0:T(8,128)} %bitcast.6, bf16[128,256]{1,0:T(8,128)(2,1)} %constant.28.clone.yf_ref, bf16[2,256,256]{2,1,0:T(8,128)(2,1)} %constant.30.clone.table_ref), custom_call_target="tpu_custom_call" | custom-call | flops 8000000000 | bytes 24000000 | tf_op jit(solution)/shard_map/pallas_call | solution.py:319
  23.5 6.4 %all-to-all-done.refs_0_ = f32[16,16,512]{2,1,0:T(8,128)S(1)} async-done(((f32[16,16,512]{2,1,0:T(8,128)}), f32[16,16,512]{2,1,0:T(8,128)S(1)}, u32[]{:S(2)}, u32[]{:S(2)}) %all-to-all-start) | async-done | bytes 524320 | tf_op jit(solution)/shard_map/all_to_all | solution.py:675
  29.9 4.1 %all-to-all-start.1 = ((f32[16,16,512]{2,1,0:T(8,128)}), f32[16,16,512]{2,1,0:T(8,128)S(1)}, u32[]{:S(2)}, u32[]{:S(2)}) async-start(f32[16,16,512]{2,1,0:T(8,128)} %shard_map.194), calls=%async_computation.1 | async-start | bytes 1048576 | tf_op jit(solution)/shard_map/all_to_all | solution.py:675
  34.0 9.4 %shard_map.195.refs_0_ = f32[32,8,128,128]{3,2,1,0:T(8,128)} custom-call(f32[32,8,128,128]{3,2,1,0:T(8,128)} %bitcast.7, f32[32,32]{1,0:T(8,128)} %bitcast.10, bf16[256,32]{1,0:T(8,128)(2,1)} %constant.40.clone.rep_ref), custom_call_target="tpu_custom_call" | custom-call | flops 8000000000 | bytes 24000000 | tf_op jit(solution)/shard_map/pallas_call | solution.py:595
  43.4 5.4 %shard_map.196 = (f32[64,512]{1,0:T(8,128)}, f32[2,32,1024]{2,1,0:T(8,128)}) custom-call(f32[16,16,512]{2,1,0:T(8,128)} %copy-done.5, f32[2,32,32,1024]{3,2,1,0:T(8,128)} %w.1, bf16[64,256]{1,0:T(8,128)(2,1)} %constant.36.clone.refs_2_.refs_3_.xfh, bf16[64,256]{1,0:T(8,128)(2,1)} %constant.37.clone.refs_3_.refs_4_.xfl, ...), custom_call_target="tpu_custom_call" | custom-call | flops 6000000000 | bytes 18000000 | tf_op jit(solution)/shard_map/pallas_call | solution.py:419
  48.9 0.8 copy-done.7
  49.7 6.9 %shard_map.197 = (f32[64,512]{1,0:T(8,128)}, f32[16,16,512]{2,1,0:T(8,128)}, f32[16,16,512]{2,1,0:T(8,128)}) custom-call(f32[16,16,512]{2,1,0:T(8,128)} %copy-done.7, f32[2,32,32,1024]{3,2,1,0:T(8,128)} %w.1, bf16[64,256]{1,0:T(8,128)(2,1)} %constant.36.clone.refs_2_.refs_3_.xfh, bf16[64,256]{1,0:T(8,128)(2,1)} %constant.37.clone.refs_3_.refs_4_.xfl, ...), custom_call_target="tpu_custom_call" | custom-call | flops 6000000000 | bytes 18000000 | tf_op jit(solution)/shard_map/pallas_call | solution.py:419
  56.6 6.0 %all-to-all-start.2 = ((f32[16,16,512]{2,1,0:T(8,128)}), f32[16,16,512]{2,1,0:T(8,128)S(1)}, u32[]{:S(2)}, u32[]{:S(2)}) async-start(f32[16,16,512]{2,1,0:T(8,128)} %get-tuple-element.37), calls=%async_computation.2 | async-start | bytes 1048576 | tf_op jit(solution)/shard_map/all_to_all | solution.py:675
  62.6 0.9 constant_dynamic-update-slice_fusion.hat_ref
  63.5 1.6 collective-permute-start
  65.1 9.4 %shard_map.198.sum_ref = f32[32,8,128,128]{3,2,1,0:T(8,128)} custom-call(f32[32,8,128,128]{3,2,1,0:T(8,128)} %bitcast.8, f32[32,32]{1,0:T(8,128)} %bitcast.11, bf16[256,32]{1,0:T(8,128)(2,1)} %constant.40.clone.rep_ref, f32[32,8,128,128]{3,2,1,0:T(8,128)} %shard_map.195.refs_0_), custom_call_target="tpu_custom_call", output_to_operand_aliasing={{}: (3, {})} | custom-call | flops 8000000000 | bytes 24000000 | tf_op jit(solution)/shard_map/pallas_call | solution.py:595
  74.5 2.6 %all-to-all-done.2.arrived_ref = f32[16,16,512]{2,1,0:T(8,128)S(1)} async-done(((f32[16,16,512]{2,1,0:T(8,128)}), f32[16,16,512]{2,1,0:T(8,128)S(1)}, u32[]{:S(2)}, u32[]{:S(2)}) %all-to-all-start.2) | async-done | bytes 524320 | tf_op jit(solution)/shard_map/all_to_all | solution.py:675
  77.0 4.1 %all-to-all-start.3 = ((f32[16,16,512]{2,1,0:T(8,128)}), f32[16,16,512]{2,1,0:T(8,128)S(1)}, u32[]{:S(2)}, u32[]{:S(2)}) async-start(f32[16,16,512]{2,1,0:T(8,128)} %get-tuple-element.40), calls=%async_computation.3 | async-start | bytes 1048576 | tf_op jit(solution)/shard_map/all_to_all | solution.py:675
  81.2 20.0 %shard_map.199 = (f32[32,8,128,128]{3,2,1,0:T(8,128)}, f32[32,8,128,128]{3,2,1,0:T(8,128)}, f32[16,16,512]{2,1,0:T(8,128)}) custom-call(f32[16,16,512]{2,1,0:T(8,128)} %copy-done.2, f32[32,8,128,128]{3,2,1,0:T(8,128)} %shard_map.198.sum_ref, f32[32,8,128,128]{3,2,1,0:T(8,128)} %bitcast.12, bf16[128,192]{1,0:T(8,128)(2,1)} %constant.29.clone.yi_ref, ...), custom_call_target="tpu_custom_call" | custom-call | flops 20000000000 | bytes 60000000 | tf_op jit(solution)/shard_map/pallas_call | solution.py:634
  101.2 6.0 %all-to-all-start.4 = ((f32[16,16,512]{2,1,0:T(8,128)}), f32[16,16,512]{2,1,0:T(8,128)S(1)}, u32[]{:S(2)}, u32[]{:S(2)}) async-start(f32[16,16,512]{2,1,0:T(8,128)} %get-tuple-element.48), calls=%async_computation.4 | async-start | bytes 1048576 | tf_op jit(solution)/shard_map/all_to_all | solution.py:675
  107.3 20.1 %shard_map.200 = (f32[32,8,128,128]{3,2,1,0:T(8,128)}, f32[32,8,128,128]{3,2,1,0:T(8,128)}, f32[16,16,512]{2,1,0:T(8,128)}) custom-call(f32[16,16,512]{2,1,0:T(8,128)} %copy-done.3, f32[32,8,128,128]{3,2,1,0:T(8,128)} %shard_map.198.sum_ref, f32[32,8,128,128]{3,2,1,0:T(8,128)} %bitcast.13, ...), custom_call_target="tpu_custom_call", output_to_operand_aliasing={{0}: (8, {}), {1}: (9, {})} | custom-call | flops 20000000000 | bytes 60000000 | tf_op jit(solution)/shard_map/pallas_call | solution.py:634
  127.4 6.0 %all-to-all-start.5 = ((f32[16,16,512]{2,1,0:T(8,128)}), f32[16,16,512]{2,1,0:T(8,128)S(1)}, u32[]{:S(2)}, u32[]{:S(2)}) async-start(f32[16,16,512]{2,1,0:T(8,128)} %get-tuple-element.51), calls=%async_computation.5 | async-start | bytes 1048576 | tf_op jit(solution)/shard_map/all_to_all | solution.py:675
  133.4 15.1 %shard_map.201.sum_ref = f32[32,8,128,128]{3,2,1,0:T(8,128)} custom-call(f32[32,8,128,128]{3,2,1,0:T(8,128)} %get-tuple-element.52.data_ref, f32[32,32]{1,0:T(8,128)} %matrix_ref.1, bf16[256,32]{1,0:T(8,128)(2,1)} %constant.40.clone.rep_ref), custom_call_target="tpu_custom_call" | custom-call | flops 16000000000 | bytes 48000000 | tf_op jit(solution)/shard_map/pallas_call | solution.py:595
  148.5 0.8 copy-done.6
  149.3 7.2 %shard_map.202 = (f32[2,32,1024]{2,1,0:T(8,128)}, f32[16,16,512]{2,1,0:T(8,128)}) custom-call(f32[16,16,512]{2,1,0:T(8,128)} %copy-done.1, f32[16,16,512]{2,1,0:T(8,128)} %copy-done.6, f32[2,32,32,1024]{3,2,1,0:T(8,128)} %w.1, bf16[64,256]{1,0:T(8,128)(2,1)} %constant.36.clone.refs_2_.refs_3_.xfh, bf16[64,256]{1,0:T(8,128)(2,1)} %constant.37.clone.refs_3_.refs_4_.xfl, ...), custom_call_target="tpu_custom_call" | custom-call | flops 7000000000 | bytes 21000000 | tf_op jit(solution)/shard_map/pallas_call | solution.py:480
  156.5 1.5 collective-permute-start.1
  158.1 6.0 %all-to-all-start.6 = ((f32[16,16,512]{2,1,0:T(8,128)}), f32[16,16,512]{2,1,0:T(8,128)S(1)}, u32[]{:S(2)}, u32[]{:S(2)}) async-start(f32[16,16,512]{2,1,0:T(8,128)} %get-tuple-element.56), calls=%async_computation.6 | async-start | bytes 1048576 | tf_op jit(solution)/shard_map/all_to_all | solution.py:675
  164.1 5.8 %shard_map.203 = f32[16,16,512]{2,1,0:T(8,128)} custom-call(f32[2,32,1024]{2,1,0:T(8,128)} %get-tuple-element.57.g.g_ref, f32[2,32,32,1024]{3,2,1,0:T(8,128)} %w.1, bf16[64,256]{1,0:T(8,128)(2,1)} %constant.36.clone.refs_2_.refs_3_.xfh, bf16[64,256]{1,0:T(8,128)(2,1)} %constant.37.clone.refs_3_.refs_4_.xfl, bf16[2048,128]{1,0:T(8,128)(2,1)} %constant.41.clone.refs_5_.gather, ...), custom_call_target="tpu_custom_call" | custom-call | flops 6000000000 | bytes 18000000 | tf_op jit(solution)/shard_map/pallas_call | solution.py:493
  169.9 0.7 copy-done.12
  170.6 8.3 %shard_map.204 = f32[2,32,32,1024]{3,2,1,0:T(8,128)} custom-call(f32[64,1024]{1,0:T(8,128)} %copy-done.9, f32[64,1024]{1,0:T(8,128)} %copy-done.11, f32[2,32,1024]{2,1,0:T(8,128)} %get-tuple-element.57.g.g_ref, f32[2,32,1024]{2,1,0:T(8,128)} %copy-done.12, bf16[128,2048]{1,0:T(8,128)(2,1)} %constant.39.clone.refs_4_.spread_ref), custom_call_target="tpu_custom_call" | custom-call | flops 8000000000 | bytes 24000000 | tf_op jit(solution)/shard_map/pallas_call | solution.py:519
  178.9 6.0 %all-to-all-start.7 = ((f32[16,16,512]{2,1,0:T(8,128)}), f32[16,16,512]{2,1,0:T(8,128)S(1)}, u32[]{:S(2)}, u32[]{:S(2)}) async-start(f32[16,16,512]{2,1,0:T(8,128)} %shard_map.203), calls=%async_computation.7 | async-start | bytes 1048576 | tf_op jit(solution)/shard_map/all_to_all | solution.py:675
  184.9 9.7 %shard_map.205.refs_0_ = f32[32,8,128,128]{3,2,1,0:T(8,128)} custom-call(f32[16,16,512]{2,1,0:T(8,128)} %copy-done.4, f32[32,8,128,128]{3,2,1,0:T(8,128)} %shard_map.201.sum_ref, bf16[128,192]{1,0:T(8,128)(2,1)} %constant.29.clone.yi_ref, bf16[256,2048]{1,0:T(8,128)(2,1)} %constant.34.clone.zjh_ref, bf16[256,2048]{1,0:T(8,128)(2,1)} %constant.35.clone.zjl_ref), custom_call_target="tpu_custom_call" | custom-call | flops 10000000000 | bytes 30000000 | tf_op jit(solution)/shard_map/pallas_call | solution.py:662
  194.7 4.8 %all-to-all-done.7.arrived_ref = f32[16,16,512]{2,1,0:T(8,128)S(1)} async-done(((f32[16,16,512]{2,1,0:T(8,128)}), f32[16,16,512]{2,1,0:T(8,128)S(1)}, u32[]{:S(2)}, u32[]{:S(2)}) %all-to-all-start.7) | async-done | bytes 524320 | tf_op jit(solution)/shard_map/all_to_all | solution.py:675
  199.4 0.8 copy-done
  200.2 9.7 %shard_map.206 = f32[32,8,128,128]{3,2,1,0:T(8,128)} custom-call(f32[16,16,512]{2,1,0:T(8,128)} %copy-done, f32[32,8,128,128]{3,2,1,0:T(8,128)} %shard_map.201.sum_ref, bf16[128,192]{1,0:T(8,128)(2,1)} %constant.29.clone.yi_ref, bf16[256,2048]{1,0:T(8,128)(2,1)} %constant.34.clone.zjh_ref, ...), custom_call_target="tpu_custom_call", output_to_operand_aliasing={{}: (5, {})} | custom-call | flops 10000000000 | bytes 30000000 | tf_op jit(solution)/shard_map/pallas_call | solution.py:662
  (31 shorter events, 0.8 us)
Async XLA Ops:
  0.6 14.8 %copy-start.10 = (f32[32,32]{1,0:T(8,128)S(1)}, f32[32,32]{1,0:T(8,128)}, u32[]{:S(2)}) copy-start(f32[32,32]{1,0:T(8,128)} %matrix_ref.1) | copy-start | bytes 12292
  8.1 21.9 %all-to-all-start = ((f32[16,16,512]{2,1,0:T(8,128)}), f32[16,16,512]{2,1,0:T(8,128)S(1)}, u32[]{:S(2)}, u32[]{:S(2)}) async-start(f32[16,16,512]{2,1,0:T(8,128)} %shard_map.193), calls=%async_computation | async-start | bytes 1048576 | tf_op jit(solution)/shard_map/all_to_all | solution.py:675
  29.9 13.5 %copy-start.5 = (f32[16,16,512]{2,1,0:T(8,128)}, f32[16,16,512]{2,1,0:T(8,128)S(1)}, u32[]{:S(2)}) copy-start(f32[16,16,512]{2,1,0:T(8,128)S(1)} %all-to-all-done.refs_0_) | copy-start | bytes 1572868
  29.9 19.0 %all-to-all-start.1 = ((f32[16,16,512]{2,1,0:T(8,128)}), f32[16,16,512]{2,1,0:T(8,128)S(1)}, u32[]{:S(2)}, u32[]{:S(2)}) async-start(f32[16,16,512]{2,1,0:T(8,128)} %shard_map.194), calls=%async_computation.1 | async-start | bytes 1048576 | tf_op jit(solution)/shard_map/all_to_all | solution.py:675
  48.9 13.7 %copy-start.8 = (f32[64,512]{1,0:T(8,128)S(1)}, f32[64,512]{1,0:T(8,128)}, u32[]{:S(2)}) copy-start(f32[64,512]{1,0:T(8,128)} %get-tuple-element.53) | copy-start | bytes 393220
  48.9 0.8 copy-start.7
  56.6 20.5 %all-to-all-start.2 = ((f32[16,16,512]{2,1,0:T(8,128)}), f32[16,16,512]{2,1,0:T(8,128)S(1)}, u32[]{:S(2)}, u32[]{:S(2)}) async-start(f32[16,16,512]{2,1,0:T(8,128)} %get-tuple-element.37), calls=%async_computation.2 | async-start | bytes 1048576 | tf_op jit(solution)/shard_map/all_to_all | solution.py:675
  63.5 11.0 %copy-start.9 = (f32[64,1024]{1,0:T(8,128)}, f32[64,1024]{1,0:T(8,128)S(1)}, u32[]{:S(2)}) copy-start(f32[64,1024]{1,0:T(8,128)S(1)} %constant_dynamic-update-slice_fusion.hat_ref) | copy-start | bytes 786436
  63.5 85.0 %collective-permute-start = (f32[64,1024]{1,0:T(8,128)S(1)}, f32[64,1024]{1,0:T(8,128)S(1)}, u32[]{:S(2)}, u32[]{:S(2)}) collective-permute-start(f32[64,1024]{1,0:T(8,128)S(1)} %constant_dynamic-update-slice_fusion.hat_ref), channel_id=1, source_target_pairs={{0,16},{16,0},{1,17},{17,1},{2,18},{18,2},{3,19},{19,3},{4,20},{20... | collective-permute-start | bytes 786440 | tf_op jit(solution)/shard_map/ppermute | solution.py:721
  77.0 4.1 %copy-start.2 = (f32[16,16,512]{2,1,0:T(8,128)}, f32[16,16,512]{2,1,0:T(8,128)S(1)}, u32[]{:S(2)}) copy-start(f32[16,16,512]{2,1,0:T(8,128)S(1)} %all-to-all-done.2.arrived_ref) | copy-start | bytes 1572868
  77.0 24.2 %all-to-all-start.3 = ((f32[16,16,512]{2,1,0:T(8,128)}), f32[16,16,512]{2,1,0:T(8,128)S(1)}, u32[]{:S(2)}, u32[]{:S(2)}) async-start(f32[16,16,512]{2,1,0:T(8,128)} %get-tuple-element.40), calls=%async_computation.3 | async-start | bytes 1048576 | tf_op jit(solution)/shard_map/all_to_all | solution.py:675
  101.2 6.0 %copy-start.3 = (f32[16,16,512]{2,1,0:T(8,128)}, f32[16,16,512]{2,1,0:T(8,128)S(1)}, u32[]{:S(2)}) copy-start(f32[16,16,512]{2,1,0:T(8,128)S(1)} %all-to-all-done.3.arrived_ref) | copy-start | bytes 1572868
  101.2 26.1 %all-to-all-start.4 = ((f32[16,16,512]{2,1,0:T(8,128)}), f32[16,16,512]{2,1,0:T(8,128)S(1)}, u32[]{:S(2)}, u32[]{:S(2)}) async-start(f32[16,16,512]{2,1,0:T(8,128)} %get-tuple-element.48), calls=%async_computation.4 | async-start | bytes 1048576 | tf_op jit(solution)/shard_map/all_to_all | solution.py:675
  127.3 21.1 %copy-start.1 = (f32[16,16,512]{2,1,0:T(8,128)}, f32[16,16,512]{2,1,0:T(8,128)S(1)}, u32[]{:S(2)}) copy-start(f32[16,16,512]{2,1,0:T(8,128)S(1)} %all-to-all-done.4.refs_0_) | copy-start | bytes 1572868
  127.4 21.1 %all-to-all-start.5 = ((f32[16,16,512]{2,1,0:T(8,128)}), f32[16,16,512]{2,1,0:T(8,128)S(1)}, u32[]{:S(2)}, u32[]{:S(2)}) async-start(f32[16,16,512]{2,1,0:T(8,128)} %get-tuple-element.51), calls=%async_computation.5 | async-start | bytes 1048576 | tf_op jit(solution)/shard_map/all_to_all | solution.py:675
  148.5 21.4 %copy-start.11 = (f32[64,1024]{1,0:T(8,128)}, f32[64,1024]{1,0:T(8,128)S(1)}, u32[]{:S(2)}) copy-start(f32[64,1024]{1,0:T(8,128)S(1)} %collective-permute-done.far_hat_ref) | copy-start | bytes 786436
  148.5 0.8 copy-start.6
  156.5 13.3 %collective-permute-start.1 = (f32[2,32,1024]{2,1,0:T(8,128)}, f32[2,32,1024]{2,1,0:T(8,128)S(1)}, u32[]{:S(2)}, u32[]{:S(2)}) collective-permute-start(f32[2,32,1024]{2,1,0:T(8,128)} %get-tuple-element.57.g.g_ref), channel_id=1, source_target_pairs={{0,16},{16,0},{1,17},{17,1},{2,18},{18,2},{3,19},{19,3},{4,20},{20... | collective-permute-start | bytes 786440 | tf_op jit(solution)/shard_map/ppermute | solution.py:727
  158.1 20.8 %all-to-all-start.6 = ((f32[16,16,512]{2,1,0:T(8,128)}), f32[16,16,512]{2,1,0:T(8,128)S(1)}, u32[]{:S(2)}, u32[]{:S(2)}) async-start(f32[16,16,512]{2,1,0:T(8,128)} %get-tuple-element.56), calls=%async_computation.6 | async-start | bytes 1048576 | tf_op jit(solution)/shard_map/all_to_all | solution.py:675
  169.9 0.7 copy-start.12
  178.9 6.0 %copy-start.4 = (f32[16,16,512]{2,1,0:T(8,128)}, f32[16,16,512]{2,1,0:T(8,128)S(1)}, u32[]{:S(2)}) copy-start(f32[16,16,512]{2,1,0:T(8,128)S(1)} %all-to-all-done.6.arrived_ref) | copy-start | bytes 1572868
  178.9 20.5 %all-to-all-start.7 = ((f32[16,16,512]{2,1,0:T(8,128)}), f32[16,16,512]{2,1,0:T(8,128)S(1)}, u32[]{:S(2)}, u32[]{:S(2)}) async-start(f32[16,16,512]{2,1,0:T(8,128)} %shard_map.203), calls=%async_computation.7 | async-start | bytes 1048576 | tf_op jit(solution)/shard_map/all_to_all | solution.py:675
  199.4 0.8 copy-start

commit v3 on v2

--- a/solution.py
+++ b/solution.py
@@ -154,12 +154,13 @@
 QUAD = 4
 GROUPS = CH // QUAD
 TILE = QUAD * PAIRS
+PER = 2
 BLOCKS = QUAD * KYL
 WIDE = BLOCKS * 2 * GZ
 ROWS = PLANES * KYH
 MODES_O = KX * CH
 
-VMEM = 56 * 1024 * 1024
+VMEM = 52 * 1024 * 1024
 
 BF = jnp.bfloat16
 F32 = jnp.float32
@@ -302,8 +303,16 @@
     return pl.BlockSpec((QUAD, PLANES, GY, GZ), lambda g: (g + first, 0, 0, 0))
 
 
-def moved_block():
-    return pl.BlockSpec((PEERS, 2 * PLANES, TILE), lambda g: (0, 0, g))
+def moved_block(per=1):
+    return pl.BlockSpec((PEERS, 2 * PLANES, per * TILE), lambda g: (0, 0, g))
+
+
+def weight_block(at):
+    return pl.BlockSpec((2, PER * QUAD, PAIRS, MODES_O), lambda g: (0, g + at // PER, 0, 0))
+
+
+def hat_block(at):
+    return pl.BlockSpec((2 * KX, PER * TILE), lambda g: (0, g + at // PER))
 
 
 def moved_shape(groups):
@@ -355,7 +364,7 @@
     moved_ref, w_ref, xfh_ref, xfl_ref, spread_ref, xi_ref = refs[:6]
     refs = refs[6:]
     if not first:
-        start_ref, refs = refs[0], refs[1:]
+        start_ref, refs = refs[0], refs[2:]
     hat_ref, refs = refs[0], refs[1:]
     if last:
         out_refs, (acc_s, turn_s) = refs[:-2], refs[-2:]
@@ -367,16 +376,17 @@
     def _():
         acc_s[...] = jnp.zeros_like(acc_s) if first else start_ref[...]
 
-    hat = x_forward(moved_ref[...].reshape(2 * GX, TILE), xfh_ref[...], xfl_ref[...])
+    hat = x_forward(moved_ref[...].reshape(2 * GX, PER * TILE), xfh_ref[...], xfl_ref[...])
     hat_ref[...] = hat
-    wide = spread_modes(hat, spread_ref[...])
     acc_re, acc_im = acc_s[0], acc_s[1]
-    for q in range(QUAD):
-        h_re = wide[q * PAIRS : (q + 1) * PAIRS, :MODES_O]
-        h_im = wide[q * PAIRS : (q + 1) * PAIRS, MODES_O:]
-        w_re, w_im = w_ref[0, q], w_ref[1, q]
-        acc_re = acc_re + (h_re * w_re - h_im * w_im)
-        acc_im = acc_im + (h_re * w_im + h_im * w_re)
+    for u in range(PER):
+        wide = spread_modes(hat[:, u * TILE : (u + 1) * TILE], spread_ref[...])
+        for q in range(QUAD):
+            h_re = wide[q * PAIRS : (q + 1) * PAIRS, :MODES_O]
+            h_im = wide[q * PAIRS : (q + 1) * PAIRS, MODES_O:]
+            w_re, w_im = w_ref[0, u * QUAD + q], w_ref[1, u * QUAD + q]
+            acc_re = acc_re + (h_re * w_re - h_im * w_im)
+            acc_im = acc_im + (h_re * w_im + h_im * w_re)
     acc_s[0] = acc_re
     acc_s[1] = acc_im
 
@@ -409,23 +419,24 @@
                     out_refs[h // per][:, :, to : to + TILE] = wave[:, :, (h - g) * TILE : (h - g + 1) * TILE]
 
 
-def mix(moved, weights, start, at, count, chunks, t):
-    first, last = start is None, at + count == GROUPS
+def mix(moved, weights, so_far, at, count, chunks, t):
+    first, last = not so_far, at + count == GROUPS
     tables = (t["xfh"], t["xfl"], t["spread"], t["xi"])
-    operands = (moved, weights) + tables + (() if first else (start,))
+    hat = jax.ShapeDtypeStruct((2 * KX, CH * PAIRS), F32)
     acc = jax.ShapeDtypeStruct((2, PAIRS, MODES_O), F32)
     outs = [moved_shape(n) for n in chunks] if last else [acc]
     scratch = [pltpu.VMEM(acc.shape, F32), pltpu.VMEM((2 * MODES_O, TILE), F32)] if last else []
+    before = [] if first else [whole(acc), pl.BlockSpec(memory_space=pl.ANY)]
     return call(
-        functools.partial(mix_body, first, last, count),
-        6,
-        (count,),
-        [moved_block(), pl.BlockSpec((2, QUAD, PAIRS, MODES_O), lambda g: (0, g + at, 0, 0))]
-        + [whole(a) for a in operands[2:]],
-        [pl.BlockSpec((2 * KX, TILE), lambda g: (0, g))] + [whole(a) for a in outs],
-        [jax.ShapeDtypeStruct((2 * KX, count * TILE), F32)] + outs,
+        functools.partial(mix_body, first, last, count // PER),
+        5,
+        (count // PER,),
+        [moved_block(PER), weight_block(at)] + [whole(a) for a in tables] + before,
+        [hat_block(at)] + [whole(a) for a in outs],
+        [hat] + outs,
         scratch,
-    )(*operands)
+        aliases={} if first else {7: 0},
+    )(moved, weights, *tables, *so_far)
 
 
 def input_body(first, moved_refs, g_ref, w_ref, xfh_ref, xfl_ref, gather_ref, xi_ref, out_ref, turn_s):
@@ -454,21 +465,21 @@
 
     g_re, g_im = g_ref[0], g_ref[1]
     rows_high, rows_low = [], []
-    for q in range(QUAD):
-        w_re, w_im = w_ref[0, q], w_ref[1, q]
+    for c in range(PER * QUAD):
+        w_re, w_im = w_ref[0, c], w_ref[1, c]
         full = jnp.concatenate([g_re * w_re + g_im * w_im, g_im * w_re - g_re * w_im], axis=1)
         high, low = halves(full)
         rows_high.append(high)
         rows_low.append(low)
     both = dot(jnp.concatenate(rows_high + rows_low, axis=0), gather_ref[...])
-    spec = (both[:TILE] + both[TILE:]).T[: 2 * KX]
-    out_ref[...] = x_inverse(spec, xi_ref[...]).reshape(PEERS, 2 * PLANES, TILE)
+    both = both[: PER * TILE] + both[PER * TILE :]
+    spec = jnp.concatenate([both[u * TILE : (u + 1) * TILE].T[: 2 * KX] for u in range(PER)], axis=1)
+    out_ref[...] = x_inverse(spec, xi_ref[...]).reshape(PEERS, 2 * PLANES, PER * TILE)
 
 
 def input_modes(moved, grad, weights, at, count, t):
     tables = (t["xfh"], t["xfl"], t["gather"], t["xi"])
     shape = jax.ShapeDtypeStruct((2, PAIRS, MODES_O), F32)
-    weight_spec = pl.BlockSpec((2, QUAD, PAIRS, MODES_O), lambda g: (0, g + at, 0, 0))
     first = grad is None
     if first:
 
@@ -480,9 +491,9 @@
         return call(
             body,
             7,
-            (count,),
-            [whole(a) for a in moved] + [weight_spec] + [whole(a) for a in tables],
-            [whole(shape), moved_block()],
+            (count // PER,),
+            [whole(a) for a in moved] + [weight_block(at)] + [whole(a) for a in tables],
+            [whole(shape), moved_block(PER)],
             [shape, moved_shape(count)],
             [pltpu.VMEM((2 * MODES_O, TILE), F32)],
         )(*moved, weights, *tables)
@@ -493,38 +504,43 @@
     out = call(
         body,
         6,
-        (count,),
-        [whole(shape), weight_spec] + [whole(a) for a in tables],
-        moved_block(),
+        (count // PER,),
+        [whole(shape), weight_block(at)] + [whole(a) for a in tables],
+        moved_block(PER),
         moved_shape(count),
         [],
     )(grad, weights, *tables)
     return grad, out
 
 
-def weight_grad_body(hat_ref, far_hat_ref, g_ref, far_g_ref, spread_ref, out_ref):
+def weight_grad_body(hat_ref, far_hat_ref, g_ref, far_g_ref, spread_ref, *refs):
+    out_ref = refs[-1]
     spread = spread_ref[...]
-    near = spread_modes(hat_ref[...], spread)
-    far = spread_modes(far_hat_ref[...], spread)
-    for q in range(QUAD):
-        rows = slice(q * PAIRS, (q + 1) * PAIRS)
-        n_re, n_im = near[rows, :MODES_O], near[rows, MODES_O:]
-        f_re, f_im = far[rows, :MODES_O], far[rows, MODES_O:]
-        out_ref[0, q] = n_re * g_ref[0] + n_im * g_ref[1] + f_re * far_g_ref[0] + f_im * far_g_ref[1]
-        out_ref[1, q] = n_re * g_ref[1] - n_im * g_ref[0] + f_re * far_g_ref[1] - f_im * far_g_ref[0]
-
-
-def weight_grad(hat, far_hat, grad, far_grad, t):
-    tile = pl.BlockSpec((2 * KX, TILE), lambda g: (0, g))
+    for u in range(PER):
+        lanes = slice(u * TILE, (u + 1) * TILE)
+        near = spread_modes(hat_ref[:, lanes], spread)
+        far = spread_modes(far_hat_ref[:, lanes], spread)
+        for q in range(QUAD):
+            rows = slice(q * PAIRS, (q + 1) * PAIRS)
+            n_re, n_im = near[rows, :MODES_O], near[rows, MODES_O:]
+            f_re, f_im = far[rows, :MODES_O], far[rows, MODES_O:]
+            c = u * QUAD + q
+            out_ref[0, c] = n_re * g_ref[0] + n_im * g_ref[1] + f_re * far_g_ref[0] + f_im * far_g_ref[1]
+            out_ref[1, c] = n_re * g_ref[1] - n_im * g_ref[0] + f_re * far_g_ref[1] - f_im * far_g_ref[0]
+
+
+def weight_grad(hat, far_hat, grad, far_grad, at, count, so_far, t):
     return call(
         weight_grad_body,
-        8,
-        (GROUPS,),
-        [tile, tile, whole(grad), whole(far_grad), whole(t["spread"])],
-        pl.BlockSpec((2, QUAD, PAIRS, MODES_O), lambda g: (0, g, 0, 0)),
+        count,
+        (count // PER,),
+        [hat_block(at), hat_block(at), whole(grad), whole(far_grad), whole(t["spread"])]
+        + [pl.BlockSpec(memory_space=pl.ANY)] * len(so_far),
+        weight_block(at),
         jax.ShapeDtypeStruct((2, CH, PAIRS, MODES_O), F32),
         [],
-    )(hat, far_hat, grad, far_grad, t["spread"])
+        aliases={5 + i: i for i in range(len(so_far))},
+    )(hat, far_hat, grad, far_grad, t["spread"], *so_far)
 
 
 def gelu_parts(pre):
@@ -689,20 +705,21 @@
     parts = list(zip(STARTS, CHUNKS))
     ahead = lax.optimization_barrier
 
-    moved = []
+    turned = bypass_weight.T
+    moved, sums = [], ()
     for at, n in parts:
         sent = spectrum(source, at, n, t)
         if moved:
-            moved[-1], sent = ahead((moved[-1], sent))
+            sums = (channel_sum(source, turned, 0, 2, 1, (), t),)
+            moved[-1], sent, *sums = ahead((moved[-1], sent, *sums))
         moved.append(swap_slabs(sent))
-    turned = bypass_weight.T
-    sums = channel_sum(source, turned, 0, PLANES // 2, 1, (), t)
-    moved[-1], sums = ahead((moved[-1], sums))
-    hats, state = [], None
+    sums = (channel_sum(source, turned, 2, 4, 1, tuple(sums), t),)
+    moved[-1], *sums = ahead((moved[-1], *sums))
+    hat, state = None, ()
     for arrived, (at, n) in zip(moved, parts):
-        hat, *state = mix(arrived, spec_weight, state[0] if state else None, at, n, CHUNKS, t)
-        hats.append(hat)
-    sums = channel_sum(source, turned, PLANES // 2, PLANES // 2, 1, (sums,), t)
+        hat, *state = mix(arrived, spec_weight, (*state, hat) if state else (), at, n, CHUNKS, t)
+    far_hat = lax.ppermute(hat, "dp", swap_pair)
+    sums = channel_sum(source, turned, 6, 2, 1, tuple(sums), t)
     so_far, cot_moved, arrived = (), [], []
     for sent in state:
         if arrived:
@@ -717,19 +734,21 @@
         cot_moved.append(swap_slabs(sent))
     result, grad_pre = so_far
     back_sums = channel_sum(grad_pre, bypass_weight, 0, PLANES, 2, (), t)
-    hat = jnp.concatenate(hats, axis=1)
-    far_hat = lax.ppermute(hat, "dp", swap_pair)
     cot_moved[-1], back_sums, far_hat = ahead((cot_moved[-1], back_sums, far_hat))
-    grad, back_arrived = None, []
+    grad, back_arrived, made = None, [], ()
     for at, n in parts:
         grad, sent = input_modes(cot_moved, grad, spec_weight, at, n, t)
         if back_arrived:
+            made = (weight_grad(hat, far_hat, grad, far_grad, 0, n, (), t),)
+            back_arrived[-1], sent, *made = ahead((back_arrived[-1], sent, *made))
+        else:
             far_grad = lax.ppermute(grad, "dp", swap_pair)
-            grad_spec = weight_grad(hat, far_hat, grad, far_grad, t)
-            back_arrived[-1], sent, grad_spec = ahead((back_arrived[-1], sent, grad_spec))
         back_arrived.append(swap_slabs(sent))
+    grad_spec = weight_grad(hat, far_hat, grad, far_grad, CHUNKS[0], GROUPS - CHUNKS[0], tuple(made), t)
     back = ()
     for k, (at, n) in enumerate(parts):
+        if k == 1:
+            back_arrived[k], back, grad_spec = ahead((back_arrived[k], back, grad_spec))
         back = (last(back_arrived[k], back_sums, at, n, back, t),)
     return (result[None], back[0][None], grad_spec)
 

time: 212 us -> 201 us (0.948)
  Pallas kernels: 142 us -> 132 us
  starting transfers between devices: 48.7 us -> 45.5 us
  waiting for transfers between devices: 13.7 us -> 15.9 us
    pallas_call x5 -> x6, Pallas kernels: 33.6 us -> 25.4 us  [the longest x2 8.44 us: mix(): call(functools.partial(mix_body, first, last, count // PER), 5, (count //...]
    all_to_all x8, starting transfers between devices: 45.6 us -> 42.3 us  [swap_slabs(): lax.all_to_all(array, 'slab', split_axis=0, concat_axis=0, tiled=True)]
    pallas_call x3 -> x4, Pallas kernels: 33.9 us -> 35 us  [channel_sum(): call(channel_sum_body, 2 * count, (count // step,), [block, whole(matrix)...]
    unnamed x28 -> x39, local copies, waits for them, and re-layouts: 3.82 us -> 4.74 us
  transfers between devices with their start and end apart: 10 -> 10, of which waited for: 3 -> 6; matrix products, arithmetic and copies ran while one was open for 1% -> 0% of each run, Pallas kernels for 53% -> 53%
where the time goes in v3:
time: 201 us; the launch traced here: 199 us
  Pallas kernels  132 us (66%)
  starting transfers between devices  45.5 us (23%)
  waiting for transfers between devices  15.9 us (8%)
  local copies, waits for them, and re-layouts  4.74 us (2%)
    all_to_all x8, starting transfers between devices, swap_slabs(): lax.all_to_all(array, 'slab', split_axis=0, concat_axis=0, tiled=True)  42.3 us
    pallas_call x2, Pallas kernels, middle(): call(middle_body, 5 * count, (count,), [moved_block(), block, block] + [w...  38.7 us
    pallas_call x4, Pallas kernels, channel_sum(): call(channel_sum_body, 2 * count, (count // step,), [block, whole(matrix)...  35 us
    pallas_call x2, Pallas kernels, last(): call(last_body, 2.5 * count, (count,), [moved_block(), block] + [whole(a)...  18.5 us
    pallas_call x2, Pallas kernels, spectrum(): call(spectrum_body, 2 * count, (count,), [channel_block(first)] + [whole(...  14.8 us
    all_to_all x8, waiting for transfers between devices, swap_slabs(): lax.all_to_all(array, 'slab', split_axis=0, concat_axis=0, tiled=True)  14.2 us
    pallas_call x2, Pallas kernels, mix(): call(functools.partial(mix_body, first, last, count // PER), 5, (count //...  8.44 us
    pallas_call x2, Pallas kernels, weight_grad(): call(weight_grad_body, count, (count // PER,), [hat_block(at), hat_block(...  6.9 us
  transfers between devices with their start and end apart: 10, of which 6 were waited for; matrix products, arithmetic and copies ran while one was open for 0% of the time, Pallas kernels for 53%

profile of v3, /device:TPU:0, one launch (start us, length us, event | category | flops | bytes accessed | tf_op | source)
XLA Modules:
  0.0 199.4 jit_solution(12911966898358554300)
XLA Ops:
  2.5 7.4 %shard_map.193 = f32[16,16,512]{2,1,0:T(8,128)} custom-call(f32[32,8,128,128]{3,2,1,0:T(8,128)} %bitcast.8, bf16[128,256]{1,0:T(8,128)(2,1)S(1)} %copy-done.14, bf16[2,256,256]{2,1,0:T(8,128)(2,1)S(1)} %copy-done.11), custom_call_target="tpu_custom_call" | custom-call | flops 8000000000 | bytes 24000000 | tf_op jit(solution)/shard_map/pallas_call | solution.py:328
  9.9 7.4 %all-to-all-start = ((f32[16,16,512]{2,1,0:T(8,128)}), f32[16,16,512]{2,1,0:T(8,128)S(1)}, u32[]{:S(2)}, u32[]{:S(2)}) async-start(f32[16,16,512]{2,1,0:T(8,128)} %shard_map.193), calls=%async_computation | async-start | bytes 1048576 | tf_op jit(solution)/shard_map/all_to_all | solution.py:691
  17.3 5.3 %shard_map.195.refs_0_ = f32[32,8,128,128]{3,2,1,0:T(8,128)} custom-call(f32[32,8,128,128]{3,2,1,0:T(8,128)} %bitcast.9, f32[32,32]{1,0:T(8,128)S(1)} %bitcast.5, bf16[256,32]{1,0:T(8,128)(2,1)S(1)} %copy-done.1), custom_call_target="tpu_custom_call" | custom-call | flops 4000000000 | bytes 12000000 | tf_op jit(solution)/shard_map/pallas_call | solution.py:611
  22.7 7.4 %shard_map.194 = f32[16,16,512]{2,1,0:T(8,128)} custom-call(f32[32,8,128,128]{3,2,1,0:T(8,128)} %bitcast.10, bf16[128,256]{1,0:T(8,128)(2,1)S(1)} %copy-done.15, bf16[2,256,256]{2,1,0:T(8,128)(2,1)S(1)} %copy-done.12), custom_call_target="tpu_custom_call" | custom-call | flops 8000000000 | bytes 24000000 | tf_op jit(solution)/shard_map/pallas_call | solution.py:328
  30.2 1.6 all-to-all-done.refs_0_
  31.7 4.4 %all-to-all-start.1 = ((f32[16,16,512]{2,1,0:T(8,128)}), f32[16,16,512]{2,1,0:T(8,128)S(1)}, u32[]{:S(2)}, u32[]{:S(2)}) async-start(f32[16,16,512]{2,1,0:T(8,128)} %shard_map.194), calls=%async_computation.1 | async-start | bytes 1048576 | tf_op jit(solution)/shard_map/all_to_all | solution.py:691
  36.2 3.2 %shard_map.197 = (f32[64,1024]{1,0:T(8,128)S(1)}, f32[2,32,1024]{2,1,0:T(8,128)S(1)}) custom-call(f32[16,16,512]{2,1,0:T(8,128)S(1)} %all-to-all-done.refs_0_, f32[2,32,32,1024]{3,2,1,0:T(8,128)} %w.1, bf16[64,256]{1,0:T(8,128)(2,1)S(1)} %copy-done.16, bf16[64,256]{1,0:T(8,128)(2,1)S(1)} %copy-done.17, bf16[128,2048]{1,0:T(8,128)(2,1)S(1)} %copy-done.2, ...), custom_call_target="tpu_custom_call" | custom-call | flops 5000000000 | bytes 15000000 | tf_op jit(solution)/shard_map/pallas_call | solution.py:430
  39.4 9.4 %shard_map.196.refs_0_ = f32[32,8,128,128]{3,2,1,0:T(8,128)} custom-call(f32[32,8,128,128]{3,2,1,0:T(8,128)} %bitcast.11, f32[32,32]{1,0:T(8,128)S(1)} %bitcast.6, bf16[256,32]{1,0:T(8,128)(2,1)S(1)} %copy-done.1, f32[32,8,128,128]{3,2,1,0:T(8,128)} %shard_map.195.refs_0_), custom_call_target="tpu_custom_call", output_to_operand_aliasing={{}: (3, {})} | custom-call | flops 8000000000 | bytes 24000000 | tf_op jit(solution)/shard_map/pallas_call | solution.py:611
  48.8 1.9 all-to-all-done.1.refs_0_
  51.4 5.3 %shard_map.198 = (f32[64,1024]{1,0:T(8,128)S(1)}, f32[16,16,512]{2,1,0:T(8,128)}, f32[16,16,512]{2,1,0:T(8,128)}) custom-call(f32[16,16,512]{2,1,0:T(8,128)} %copy-done.18, f32[2,32,32,1024]{3,2,1,0:T(8,128)} %w.1, bf16[64,256]{1,0:T(8,128)(2,1)S(1)} %copy-done.16, bf16[64,256]{1,0:T(8,128)(2,1)S(1)} %copy-done.17, ...), custom_call_target="tpu_custom_call", output_to_operand_aliasing={{0}: (7, {})} | custom-call | flops 5000000000 | bytes 15000000 | tf_op jit(solution)/shard_map/pallas_call | solution.py:430
  56.7 4.1 %all-to-all-start.2 = ((f32[16,16,512]{2,1,0:T(8,128)}), f32[16,16,512]{2,1,0:T(8,128)S(1)}, u32[]{:S(2)}, u32[]{:S(2)}) async-start(f32[16,16,512]{2,1,0:T(8,128)} %get-tuple-element.43), calls=%async_computation.2 | async-start | bytes 1048576 | tf_op jit(solution)/shard_map/all_to_all | solution.py:691
  60.9 1.6 collective-permute-start
  62.5 5.2 %shard_map.199.sum_ref = f32[32,8,128,128]{3,2,1,0:T(8,128)} custom-call(f32[32,8,128,128]{3,2,1,0:T(8,128)} %bitcast.12, f32[32,32]{1,0:T(8,128)S(1)} %bitcast.7, bf16[256,32]{1,0:T(8,128)(2,1)S(1)} %copy-done.1, f32[32,8,128,128]{3,2,1,0:T(8,128)} %shard_map.196.refs_0_), custom_call_target="tpu_custom_call", output_to_operand_aliasing={{}: (3, {})} | custom-call | flops 4000000000 | bytes 12000000 | tf_op jit(solution)/shard_map/pallas_call | solution.py:611
  67.7 7.6 %all-to-all-done.2.arrived_ref = f32[16,16,512]{2,1,0:T(8,128)S(1)} async-done(((f32[16,16,512]{2,1,0:T(8,128)}), f32[16,16,512]{2,1,0:T(8,128)S(1)}, u32[]{:S(2)}, u32[]{:S(2)}) %all-to-all-start.2) | async-done | bytes 524320 | tf_op jit(solution)/shard_map/all_to_all | solution.py:691
  75.3 4.1 %all-to-all-start.3 = ((f32[16,16,512]{2,1,0:T(8,128)}), f32[16,16,512]{2,1,0:T(8,128)S(1)}, u32[]{:S(2)}, u32[]{:S(2)}) async-start(f32[16,16,512]{2,1,0:T(8,128)} %get-tuple-element.46), calls=%async_computation.3 | async-start | bytes 1048576 | tf_op jit(solution)/shard_map/all_to_all | solution.py:691
  79.5 19.3 %shard_map.200 = (f32[32,8,128,128]{3,2,1,0:T(8,128)}, f32[32,8,128,128]{3,2,1,0:T(8,128)}, f32[16,16,512]{2,1,0:T(8,128)}) custom-call(f32[16,16,512]{2,1,0:T(8,128)S(1)} %all-to-all-done.2.arrived_ref, f32[32,8,128,128]{3,2,1,0:T(8,128)} %shard_map.199.sum_ref, f32[32,8,128,128]{3,2,1,0:T(8,128)} %bitcast.14, bf16[128,192]{1,0:T(8,128)(2,1)S(1)} %copy-done.7, ...), custom_call_target="tpu_custom_call" | custom-call | flops 20000000000 | bytes 60000000 | tf_op jit(solution)/shard_map/pallas_call | solution.py:650
  98.8 6.0 %all-to-all-start.4 = ((f32[16,16,512]{2,1,0:T(8,128)}), f32[16,16,512]{2,1,0:T(8,128)S(1)}, u32[]{:S(2)}, u32[]{:S(2)}) async-start(f32[16,16,512]{2,1,0:T(8,128)} %get-tuple-element.54), calls=%async_computation.4 | async-start | bytes 1048576 | tf_op jit(solution)/shard_map/all_to_all | solution.py:691
  104.8 19.4 %shard_map.201 = (f32[32,8,128,128]{3,2,1,0:T(8,128)}, f32[32,8,128,128]{3,2,1,0:T(8,128)}, f32[16,16,512]{2,1,0:T(8,128)}) custom-call(f32[16,16,512]{2,1,0:T(8,128)S(1)} %all-to-all-done.3.arrived_ref, f32[32,8,128,128]{3,2,1,0:T(8,128)} %shard_map.199.sum_ref, f32[32,8,128,128]{3,2,1,0:T(8,128)} %bitcast.15, ...), custom_call_target="tpu_custom_call", output_to_operand_aliasing={{0}: (8, {}), {1}: (9, {})} | custom-call | flops 20000000000 | bytes 60000000 | tf_op jit(solution)/shard_map/pallas_call | solution.py:650
  124.2 6.0 %all-to-all-start.5 = ((f32[16,16,512]{2,1,0:T(8,128)}), f32[16,16,512]{2,1,0:T(8,128)S(1)}, u32[]{:S(2)}, u32[]{:S(2)}) async-start(f32[16,16,512]{2,1,0:T(8,128)} %get-tuple-element.57), calls=%async_computation.5 | async-start | bytes 1048576 | tf_op jit(solution)/shard_map/all_to_all | solution.py:691
  130.2 15.1 %shard_map.202.sum_ref = f32[32,8,128,128]{3,2,1,0:T(8,128)} custom-call(f32[32,8,128,128]{3,2,1,0:T(8,128)} %get-tuple-element.58.data_ref, f32[32,32]{1,0:T(8,128)S(1)} %copy-done.8, bf16[256,32]{1,0:T(8,128)(2,1)S(1)} %copy-done.1), custom_call_target="tpu_custom_call" | custom-call | flops 16000000000 | bytes 48000000 | tf_op jit(solution)/shard_map/pallas_call | solution.py:611
  145.3 5.7 %shard_map.203 = (f32[2,32,1024]{2,1,0:T(8,128)S(1)}, f32[16,16,512]{2,1,0:T(8,128)}) custom-call(f32[16,16,512]{2,1,0:T(8,128)S(1)} %all-to-all-done.4.refs_0_, f32[16,16,512]{2,1,0:T(8,128)S(1)} %all-to-all-done.5.refs_1_, f32[2,32,32,1024]{3,2,1,0:T(8,128)} %w.1, bf16[64,256]{1,0:T(8,128)(2,1)S(1)} %copy-done.16, bf16[64,256]{1,0:T(8,128)(2,1)S(1)} %copy-done.17, ...), custom_call_target="tpu_custom_call" | custom-call | flops 7000000000 | bytes 21000000 | tf_op jit(solution)/shard_map/pallas_call | solution.py:491
  151.0 6.1 %all-to-all-start.6 = ((f32[16,16,512]{2,1,0:T(8,128)}), f32[16,16,512]{2,1,0:T(8,128)S(1)}, u32[]{:S(2)}, u32[]{:S(2)}) async-start(f32[16,16,512]{2,1,0:T(8,128)} %get-tuple-element.61), calls=%async_computation.6 | async-start | bytes 1048576 | tf_op jit(solution)/shard_map/all_to_all | solution.py:691
  157.1 1.6 collective-permute-start.1
  158.7 1.0 copy-done.9
  159.8 4.4 %shard_map.204 = f32[16,16,512]{2,1,0:T(8,128)} custom-call(f32[2,32,1024]{2,1,0:T(8,128)S(1)} %get-tuple-element.62.g.g_ref, f32[2,32,32,1024]{3,2,1,0:T(8,128)} %w.1, bf16[64,256]{1,0:T(8,128)(2,1)S(1)} %copy-done.16, bf16[64,256]{1,0:T(8,128)(2,1)S(1)} %copy-done.17, bf16[2048,128]{1,0:T(8,128)(2,1)S(1)} %copy-done.9, bf16[256,192]{1,0:T(8,128)(2,1)S(1)} %copy-done.13), custom_call_target="tpu_custom_call" | custom-call | flops 6000000000 | bytes 18000000 | tf_op jit(solution)/shard_map/pallas_call | solution.py:504
  164.1 1.7 collective-permute-done.1.far_g_ref
  165.9 3.5 %shard_map.205.refs_0_ = f32[2,32,32,1024]{3,2,1,0:T(8,128)} custom-call(f32[64,1024]{1,0:T(8,128)S(1)} %copy-done.5, f32[64,1024]{1,0:T(8,128)S(1)} %collective-permute-done.far_hat_ref, f32[2,32,1024]{2,1,0:T(8,128)S(1)} %get-tuple-element.62.g.g_ref, f32[2,32,1024]{2,1,0:T(8,128)S(1)} %collective-permute-done.1.far_g_ref, bf16[128,2048]{1,0:T(8,128)(2,1)S(1)} %copy-done.3), custom_call_target="tpu_custom_call" | custom-call | flops 4000000000 | bytes 12000000 | tf_op jit(solution)/shard_map/pallas_call | solution.py:533
  169.3 2.3 %all-to-all-done.6.arrived_ref = f32[16,16,512]{2,1,0:T(8,128)S(1)} async-done(((f32[16,16,512]{2,1,0:T(8,128)}), f32[16,16,512]{2,1,0:T(8,128)S(1)}, u32[]{:S(2)}, u32[]{:S(2)}) %all-to-all-start.6) | async-done | bytes 524320 | tf_op jit(solution)/shard_map/all_to_all | solution.py:691
  171.6 4.1 %all-to-all-start.7 = ((f32[16,16,512]{2,1,0:T(8,128)}), f32[16,16,512]{2,1,0:T(8,128)S(1)}, u32[]{:S(2)}, u32[]{:S(2)}) async-start(f32[16,16,512]{2,1,0:T(8,128)} %shard_map.204), calls=%async_computation.7 | async-start | bytes 1048576 | tf_op jit(solution)/shard_map/all_to_all | solution.py:691
  176.7 3.5 %shard_map.207 = f32[2,32,32,1024]{3,2,1,0:T(8,128)} custom-call(f32[64,1024]{1,0:T(8,128)S(1)} %copy-done.6, f32[64,1024]{1,0:T(8,128)S(1)} %collective-permute-done.far_hat_ref, f32[2,32,1024]{2,1,0:T(8,128)S(1)} %get-tuple-element.62.g.g_ref, f32[2,32,1024]{2,1,0:T(8,128)S(1)} %collective-permute-done.1.far_g_ref, ...), custom_call_target="tpu_custom_call", output_to_operand_aliasing={{}: (5, {})} | custom-call | flops 4000000000 | bytes 12000000 | tf_op jit(solution)/shard_map/pallas_call | solution.py:533
  180.1 9.2 %shard_map.206.refs_0_ = f32[32,8,128,128]{3,2,1,0:T(8,128)} custom-call(f32[16,16,512]{2,1,0:T(8,128)S(1)} %all-to-all-done.6.arrived_ref, f32[32,8,128,128]{3,2,1,0:T(8,128)} %shard_map.202.sum_ref, bf16[128,192]{1,0:T(8,128)(2,1)S(1)} %copy-done.7, bf16[256,2048]{1,0:T(8,128)(2,1)S(1)} %copy-done, bf16[256,2048]{1,0:T(8,128)(2,1)} %constant.35.clone.zjl_ref), custom_call_target="tpu_custom_call" | custom-call | flops 10000000000 | bytes 30000000 | tf_op jit(solution)/shard_map/pallas_call | solution.py:678
  190.2 9.2 %shard_map.208 = f32[32,8,128,128]{3,2,1,0:T(8,128)} custom-call(f32[16,16,512]{2,1,0:T(8,128)S(1)} %all-to-all-done.7.arrived_ref, f32[32,8,128,128]{3,2,1,0:T(8,128)} %shard_map.202.sum_ref, bf16[128,192]{1,0:T(8,128)(2,1)S(1)} %copy-done.7, bf16[256,2048]{1,0:T(8,128)(2,1)S(1)} %copy-done, ...), custom_call_target="tpu_custom_call", output_to_operand_aliasing={{}: (5, {})} | custom-call | flops 10000000000 | bytes 30000000 | tf_op jit(solution)/shard_map/pallas_call | solution.py:678
  (43 shorter events, 4.5 us)
Async XLA Ops:
  0.6 16.7 %copy-start.1 = (bf16[256,32]{1,0:T(8,128)(2,1)S(1)}, bf16[256,32]{1,0:T(8,128)(2,1)}, u32[]{:S(2)}) copy-start(bf16[256,32]{1,0:T(8,128)(2,1)} %constant.40.clone.rep_ref) | copy-start | bytes 49156
  0.6 16.6 %copy-start.8 = (f32[32,32]{1,0:T(8,128)S(1)}, f32[32,32]{1,0:T(8,128)}, u32[]{:S(2)}) copy-start(f32[32,32]{1,0:T(8,128)} %matrix_ref.1) | copy-start | bytes 12292
  0.7 1.0 copy-start.11
  1.6 0.8 copy-start.14
  9.9 21.9 %all-to-all-start = ((f32[16,16,512]{2,1,0:T(8,128)}), f32[16,16,512]{2,1,0:T(8,128)S(1)}, u32[]{:S(2)}, u32[]{:S(2)}) async-start(f32[16,16,512]{2,1,0:T(8,128)} %shard_map.193), calls=%async_computation | async-start | bytes 1048576 | tf_op jit(solution)/shard_map/all_to_all | solution.py:691
  17.3 5.3 %copy-start.12 = (bf16[2,256,256]{2,1,0:T(8,128)(2,1)S(1)}, bf16[2,256,256]{2,1,0:T(8,128)(2,1)}, u32[]{:S(2)}) copy-start(bf16[2,256,256]{2,1,0:T(8,128)(2,1)} %constant.30.clone.table_ref) | copy-start | bytes 786436
  17.3 5.3 %copy-start.15 = (bf16[128,256]{1,0:T(8,128)(2,1)S(1)}, bf16[128,256]{1,0:T(8,128)(2,1)}, u32[]{:S(2)}) copy-start(bf16[128,256]{1,0:T(8,128)(2,1)} %constant.28.clone.yf_ref) | copy-start | bytes 196612
  22.7 13.5 %copy-start.2 = (bf16[128,2048]{1,0:T(8,128)(2,1)S(1)}, bf16[128,2048]{1,0:T(8,128)(2,1)}, u32[]{:S(2)}) copy-start(bf16[128,2048]{1,0:T(8,128)(2,1)} %constant.39.clone.refs_4_.spread_ref) | copy-start | bytes 1572868
  22.7 13.5 %copy-start.13 = (bf16[256,192]{1,0:T(8,128)(2,1)S(1)}, bf16[256,192]{1,0:T(8,128)(2,1)}, u32[]{:S(2)}) copy-start(bf16[256,192]{1,0:T(8,128)(2,1)} %constant.38.clone.refs_5_.refs_6_.xi) | copy-start | bytes 294916
  22.7 13.5 %copy-start.16 = (bf16[64,256]{1,0:T(8,128)(2,1)S(1)}, bf16[64,256]{1,0:T(8,128)(2,1)}, u32[]{:S(2)}) copy-start(bf16[64,256]{1,0:T(8,128)(2,1)} %constant.36.clone.refs_2_.refs_3_.xfh) | copy-start | bytes 98308
  22.7 13.5 %copy-start.17 = (bf16[64,256]{1,0:T(8,128)(2,1)S(1)}, bf16[64,256]{1,0:T(8,128)(2,1)}, u32[]{:S(2)}) copy-start(bf16[64,256]{1,0:T(8,128)(2,1)} %constant.37.clone.refs_3_.refs_4_.xfl) | copy-start | bytes 98308
  31.7 18.9 %all-to-all-start.1 = ((f32[16,16,512]{2,1,0:T(8,128)}), f32[16,16,512]{2,1,0:T(8,128)S(1)}, u32[]{:S(2)}, u32[]{:S(2)}) async-start(f32[16,16,512]{2,1,0:T(8,128)} %shard_map.194), calls=%async_computation.1 | async-start | bytes 1048576 | tf_op jit(solution)/shard_map/all_to_all | solution.py:691
  50.6 0.8 copy-start.18
  56.7 11.0 %copy-start.4 = (f32[64,1024]{1,0:T(8,128)}, f32[64,1024]{1,0:T(8,128)S(1)}, u32[]{:S(2)}) copy-start(f32[64,1024]{1,0:T(8,128)S(1)} %get-tuple-element.59.hat_ref) | copy-start | bytes 786436
  56.7 18.6 %all-to-all-start.2 = ((f32[16,16,512]{2,1,0:T(8,128)}), f32[16,16,512]{2,1,0:T(8,128)S(1)}, u32[]{:S(2)}, u32[]{:S(2)}) async-start(f32[16,16,512]{2,1,0:T(8,128)} %get-tuple-element.43), calls=%async_computation.2 | async-start | bytes 1048576 | tf_op jit(solution)/shard_map/all_to_all | solution.py:691
  60.9 18.6 %copy-start.7 = (bf16[128,192]{1,0:T(8,128)(2,1)S(1)}, bf16[128,192]{1,0:T(8,128)(2,1)}, u32[]{:S(2)}) copy-start(bf16[128,192]{1,0:T(8,128)(2,1)} %constant.29.clone.yi_ref) | copy-start | bytes 147460
  60.9 18.6 %copy-start.10 = (bf16[2,256,256]{2,1,0:T(8,128)(2,1)S(1)}, bf16[2,256,256]{2,1,0:T(8,128)(2,1)}, u32[]{:S(2)}) copy-start(bf16[2,256,256]{2,1,0:T(8,128)(2,1)} %constant.31.clone.zg_ref) | copy-start | bytes 786436
  60.9 84.4 %collective-permute-start = (f32[64,1024]{1,0:T(8,128)S(1)}, f32[64,1024]{1,0:T(8,128)S(1)}, u32[]{:S(2)}, u32[]{:S(2)}) collective-permute-start(f32[64,1024]{1,0:T(8,128)S(1)} %get-tuple-element.59.hat_ref), channel_id=1, source_target_pairs={{0,16},{16,0},{1,17},{17,1},{2,18},{18,2},{3,19},{19,3},{4,20},{20... | collective-permute-start | bytes 786440 | tf_op jit(solution)/shard_map/ppermute | solution.py:721
  75.3 23.5 %all-to-all-start.3 = ((f32[16,16,512]{2,1,0:T(8,128)}), f32[16,16,512]{2,1,0:T(8,128)S(1)}, u32[]{:S(2)}, u32[]{:S(2)}) async-start(f32[16,16,512]{2,1,0:T(8,128)} %get-tuple-element.46), calls=%async_computation.3 | async-start | bytes 1048576 | tf_op jit(solution)/shard_map/all_to_all | solution.py:691
  98.8 25.4 %all-to-all-start.4 = ((f32[16,16,512]{2,1,0:T(8,128)}), f32[16,16,512]{2,1,0:T(8,128)S(1)}, u32[]{:S(2)}, u32[]{:S(2)}) async-start(f32[16,16,512]{2,1,0:T(8,128)} %get-tuple-element.54), calls=%async_computation.4 | async-start | bytes 1048576 | tf_op jit(solution)/shard_map/all_to_all | solution.py:691
  124.2 21.1 %all-to-all-start.5 = ((f32[16,16,512]{2,1,0:T(8,128)}), f32[16,16,512]{2,1,0:T(8,128)S(1)}, u32[]{:S(2)}, u32[]{:S(2)}) async-start(f32[16,16,512]{2,1,0:T(8,128)} %get-tuple-element.57), calls=%async_computation.5 | async-start | bytes 1048576 | tf_op jit(solution)/shard_map/all_to_all | solution.py:691
  151.0 14.9 %copy-start.3 = (bf16[128,2048]{1,0:T(8,128)(2,1)S(1)}, bf16[128,2048]{1,0:T(8,128)(2,1)}, u32[]{:S(2)}) copy-start(bf16[128,2048]{1,0:T(8,128)(2,1)} %constant.39.clone.refs_4_.spread_ref) | copy-start | bytes 1572868
  151.0 14.9 %copy-start.5 = (f32[64,1024]{1,0:T(8,128)S(1)}, f32[64,1024]{1,0:T(8,128)}, u32[]{:S(2)}) copy-start(f32[64,1024]{1,0:T(8,128)} %copy-done.4) | copy-start | bytes 786436
  151.0 20.6 %all-to-all-start.6 = ((f32[16,16,512]{2,1,0:T(8,128)}), f32[16,16,512]{2,1,0:T(8,128)S(1)}, u32[]{:S(2)}, u32[]{:S(2)}) async-start(f32[16,16,512]{2,1,0:T(8,128)} %get-tuple-element.61), calls=%async_computation.6 | async-start | bytes 1048576 | tf_op jit(solution)/shard_map/all_to_all | solution.py:691
  157.1 8.7 %collective-permute-start.1 = (f32[2,32,1024]{2,1,0:T(8,128)S(1)}, f32[2,32,1024]{2,1,0:T(8,128)S(1)}, u32[]{:S(2)}, u32[]{:S(2)}) collective-permute-start(f32[2,32,1024]{2,1,0:T(8,128)S(1)} %get-tuple-element.62.g.g_ref), channel_id=1, source_target_pairs={{0,16},{16,0},{1,17},{17,1},{2,18},{18,2},{3,19},{19,3},{4,20},{20... | collective-permute-start | bytes 786440 | tf_op jit(solution)/shard_map/ppermute | solution.py:745
  158.7 1.0 copy-start.9
  164.1 16.0 %copy-start = (bf16[256,2048]{1,0:T(8,128)(2,1)S(1)}, bf16[256,2048]{1,0:T(8,128)(2,1)}, u32[]{:S(2)}) copy-start(bf16[256,2048]{1,0:T(8,128)(2,1)} %constant.34.clone.zjh_ref) | copy-start | bytes 3145732
  171.6 18.6 %all-to-all-start.7 = ((f32[16,16,512]{2,1,0:T(8,128)}), f32[16,16,512]{2,1,0:T(8,128)S(1)}, u32[]{:S(2)}, u32[]{:S(2)}) async-start(f32[16,16,512]{2,1,0:T(8,128)} %shard_map.204), calls=%async_computation.7 | async-start | bytes 1048576 | tf_op jit(solution)/shard_map/all_to_all | solution.py:691
  175.7 1.0 copy-start.6

commit v4 on v3

--- a/solution.py
+++ b/solution.py
@@ -245,7 +245,7 @@
     return halves(both[: 2 * KY] + both[2 * KY :])
 
 
-def call(body, us, grid, ins, outs, shapes, scratch, aliases=None):
+def call(body, us, grid, ins, outs, shapes, scratch, aliases=None, vmem=VMEM):
     return pl.pallas_call(
         body,
         grid=grid,
@@ -256,7 +256,7 @@
         input_output_aliases=aliases or {},
         cost_estimate=pl.CostEstimate(flops=int(us * 1e9), bytes_accessed=int(us * 3e6), transcendentals=0),
         compiler_params=pltpu.CompilerParams(
-            dimension_semantics=("arbitrary",), vmem_limit_bytes=VMEM
+            dimension_semantics=("arbitrary",), vmem_limit_bytes=vmem
         ),
     )
 
@@ -333,6 +333,7 @@
         moved_block(),
         moved_shape(count),
         mode_scratch(),
+        vmem=58 * 1024 * 1024,
     )(field, *tables)
 
 
@@ -544,11 +545,12 @@
 
 
 def gelu_parts(pre):
-    bell = jnp.exp(pre * pre * -0.5)
-    t = 1.0 / (1.0 + (0.3275911 * math.sqrt(0.5)) * jnp.abs(pre))
-    poly = 1.061405429 * 0.5
-    for coefficient in (-1.453152027, 1.421413741, -0.284496736, 0.254829592):
-        poly = poly * t + coefficient * 0.5
+    bell = jnp.exp2(pre * pre * (-0.5 * math.log2(math.e)))
+    rate = 0.3275911 * math.sqrt(0.5)
+    t = 1.0 / (jnp.abs(pre) + 1.0 / rate)
+    poly = 1.061405429 * 0.5 / rate**5
+    for power, coefficient in zip((4, 3, 2, 1), (-1.453152027, 1.421413741, -0.284496736, 0.254829592)):
+        poly = poly * t + coefficient * 0.5 / rate**power
     tail = poly * t * bell
     share = jnp.where(pre >= 0.0, 1.0 - tail, tail)
     return share, pre * bell * (1.0 / math.sqrt(2.0 * math.pi))
@@ -733,18 +735,18 @@
             cot_moved[-1], sent = ahead((cot_moved[-1], sent))
         cot_moved.append(swap_slabs(sent))
     result, grad_pre = so_far
-    back_sums = channel_sum(grad_pre, bypass_weight, 0, PLANES, 2, (), t)
+    back_sums = channel_sum(grad_pre, bypass_weight, 0, 6, 2, (), t)
     cot_moved[-1], back_sums, far_hat = ahead((cot_moved[-1], back_sums, far_hat))
-    grad, back_arrived, made = None, [], ()
+    grad, back_arrived = None, []
     for at, n in parts:
         grad, sent = input_modes(cot_moved, grad, spec_weight, at, n, t)
         if back_arrived:
-            made = (weight_grad(hat, far_hat, grad, far_grad, 0, n, (), t),)
-            back_arrived[-1], sent, *made = ahead((back_arrived[-1], sent, *made))
+            back_sums = channel_sum(grad_pre, bypass_weight, 6, 2, 1, (back_sums,), t)
+            back_arrived[-1], sent, back_sums = ahead((back_arrived[-1], sent, back_sums))
         else:
             far_grad = lax.ppermute(grad, "dp", swap_pair)
         back_arrived.append(swap_slabs(sent))
-    grad_spec = weight_grad(hat, far_hat, grad, far_grad, CHUNKS[0], GROUPS - CHUNKS[0], tuple(made), t)
+    grad_spec = weight_grad(hat, far_hat, grad, far_grad, 0, GROUPS, (), t)
     back = ()
     for k, (at, n) in enumerate(parts):
         if k == 1:

time: 201 us -> 197 us (0.980)
    pallas_call x4 -> x5, Pallas kernels: 35 us -> 38.4 us  [channel_sum(): call(channel_sum_body, 2 * count, (count // step,), [block, whole(matrix)...]
    unnamed x39 -> x27, local copies, waits for them, and re-layouts: 4.74 us -> 2.99 us
    pallas_call x2 -> x1, Pallas kernels: 6.9 us -> 5.82 us  [weight_grad(): call(weight_grad_body, count, (count // PER,), [hat_block(at), hat_block(...]
  transfers between devices with their start and end apart: 10 -> 10, of which waited for: 6 -> 5; matrix products, arithmetic and copies ran while one was open for 0% -> 0% of each run, Pallas kernels for 53% -> 54%
where the time goes in v4:
time: 197 us; the launch traced here: 196 us
  Pallas kernels  134 us (68%)
  starting transfers between devices  44.1 us (22%)
  waiting for transfers between devices  14.6 us (7%)
  local copies, waits for them, and re-layouts  2.99 us (2%)
    all_to_all x8, starting transfers between devices, swap_slabs(): lax.all_to_all(array, 'slab', split_axis=0, concat_axis=0, tiled=True)  41 us
    pallas_call x5, Pallas kernels, channel_sum(): call(channel_sum_body, 2 * count, (count // step,), [block, whole(matrix)...  38.4 us
    pallas_call x2, Pallas kernels, middle(): call(middle_body, 5 * count, (count,), [moved_block(), block, block] + [w...  37.6 us
    pallas_call x2, Pallas kernels, last(): call(last_body, 2.5 * count, (count,), [moved_block(), block] + [whole(a)...  18.5 us
    pallas_call x2, Pallas kernels, spectrum(): call(spectrum_body, 2 * count, (count,), [channel_block(first)] + [whole(...  14.9 us
    all_to_all x8, waiting for transfers between devices, swap_slabs(): lax.all_to_all(array, 'slab', split_axis=0, concat_axis=0, tiled=True)  14.6 us
    pallas_call x2, Pallas kernels, mix(): call(functools.partial(mix_body, first, last, count // PER), 5, (count //...  8.46 us
    pallas_call x1, Pallas kernels, weight_grad(): call(weight_grad_body, count, (count // PER,), [hat_block(at), hat_block(...  5.82 us
  transfers between devices with their start and end apart: 10, of which 5 were waited for; matrix products, arithmetic and copies ran while one was open for 0% of the time, Pallas kernels for 54%

profile of v4, /device:TPU:0, one launch (start us, length us, event | category | flops | bytes accessed | tf_op | source)
XLA Modules:
  0.0 196.1 jit_solution(8659396280617084230)
XLA Ops:
  0.7 7.4 %shard_map.193 = f32[16,16,512]{2,1,0:T(8,128)} custom-call(f32[32,8,128,128]{3,2,1,0:T(8,128)} %bitcast.8, bf16[128,256]{1,0:T(8,128)(2,1)} %constant.28.clone.yf_ref, bf16[2,256,256]{2,1,0:T(8,128)(2,1)} %constant.30.clone.table_ref), custom_call_target="tpu_custom_call" | custom-call | flops 8000000000 | bytes 24000000 | tf_op jit(solution)/shard_map/pallas_call | solution.py:328
  8.1 7.4 %all-to-all-start = ((f32[16,16,512]{2,1,0:T(8,128)}), f32[16,16,512]{2,1,0:T(8,128)S(1)}, u32[]{:S(2)}, u32[]{:S(2)}) async-start(f32[16,16,512]{2,1,0:T(8,128)} %shard_map.193), calls=%async_computation | async-start | bytes 1048576 | tf_op jit(solution)/shard_map/all_to_all | solution.py:693
  15.6 5.3 %shard_map.195.refs_0_ = f32[32,8,128,128]{3,2,1,0:T(8,128)} custom-call(f32[32,8,128,128]{3,2,1,0:T(8,128)} %bitcast.9, f32[32,32]{1,0:T(8,128)S(1)} %bitcast.5, bf16[256,32]{1,0:T(8,128)(2,1)S(1)} %copy-done), custom_call_target="tpu_custom_call" | custom-call | flops 4000000000 | bytes 12000000 | tf_op jit(solution)/shard_map/pallas_call | solution.py:613
  20.8 7.5 %shard_map.194 = f32[16,16,512]{2,1,0:T(8,128)} custom-call(f32[32,8,128,128]{3,2,1,0:T(8,128)} %bitcast.10, bf16[128,256]{1,0:T(8,128)(2,1)} %constant.28.clone.yf_ref, bf16[2,256,256]{2,1,0:T(8,128)(2,1)} %constant.30.clone.table_ref), custom_call_target="tpu_custom_call" | custom-call | flops 8000000000 | bytes 24000000 | tf_op jit(solution)/shard_map/pallas_call | solution.py:328
  28.3 1.6 all-to-all-done.refs_0_
  30.0 4.4 %all-to-all-start.1 = ((f32[16,16,512]{2,1,0:T(8,128)}), f32[16,16,512]{2,1,0:T(8,128)S(1)}, u32[]{:S(2)}, u32[]{:S(2)}) async-start(f32[16,16,512]{2,1,0:T(8,128)} %shard_map.194), calls=%async_computation.1 | async-start | bytes 1048576 | tf_op jit(solution)/shard_map/all_to_all | solution.py:693
  34.4 3.2 %shard_map.197 = (f32[64,1024]{1,0:T(8,128)S(1)}, f32[2,32,1024]{2,1,0:T(8,128)S(1)}) custom-call(f32[16,16,512]{2,1,0:T(8,128)S(1)} %all-to-all-done.refs_0_, f32[2,32,32,1024]{3,2,1,0:T(8,128)} %w.1, bf16[64,256]{1,0:T(8,128)(2,1)S(1)} %copy-done.10, bf16[64,256]{1,0:T(8,128)(2,1)S(1)} %copy-done.11, bf16[128,2048]{1,0:T(8,128)(2,1)S(1)} %copy-done.4, ...), custom_call_target="tpu_custom_call" | custom-call | flops 5000000000 | bytes 15000000 | tf_op jit(solution)/shard_map/pallas_call | solution.py:431
  37.6 9.4 %shard_map.196.refs_0_ = f32[32,8,128,128]{3,2,1,0:T(8,128)} custom-call(f32[32,8,128,128]{3,2,1,0:T(8,128)} %bitcast.11, f32[32,32]{1,0:T(8,128)S(1)} %bitcast.6, bf16[256,32]{1,0:T(8,128)(2,1)S(1)} %copy-done, f32[32,8,128,128]{3,2,1,0:T(8,128)} %shard_map.195.refs_0_), custom_call_target="tpu_custom_call", output_to_operand_aliasing={{}: (3, {})} | custom-call | flops 8000000000 | bytes 24000000 | tf_op jit(solution)/shard_map/pallas_call | solution.py:613
  46.9 1.9 all-to-all-done.1.refs_0_
  49.6 5.3 %shard_map.198 = (f32[64,1024]{1,0:T(8,128)S(1)}, f32[16,16,512]{2,1,0:T(8,128)}, f32[16,16,512]{2,1,0:T(8,128)}) custom-call(f32[16,16,512]{2,1,0:T(8,128)} %copy-done.12, f32[2,32,32,1024]{3,2,1,0:T(8,128)} %w.1, bf16[64,256]{1,0:T(8,128)(2,1)S(1)} %copy-done.10, bf16[64,256]{1,0:T(8,128)(2,1)S(1)} %copy-done.11, ...), custom_call_target="tpu_custom_call", output_to_operand_aliasing={{0}: (7, {})} | custom-call | flops 5000000000 | bytes 15000000 | tf_op jit(solution)/shard_map/pallas_call | solution.py:431
  54.9 4.2 %all-to-all-start.2 = ((f32[16,16,512]{2,1,0:T(8,128)}), f32[16,16,512]{2,1,0:T(8,128)S(1)}, u32[]{:S(2)}, u32[]{:S(2)}) async-start(f32[16,16,512]{2,1,0:T(8,128)} %get-tuple-element.43), calls=%async_computation.2 | async-start | bytes 1048576 | tf_op jit(solution)/shard_map/all_to_all | solution.py:693
  59.1 1.6 collective-permute-start
  60.6 5.2 %shard_map.199.sum_ref = f32[32,8,128,128]{3,2,1,0:T(8,128)} custom-call(f32[32,8,128,128]{3,2,1,0:T(8,128)} %bitcast.12, f32[32,32]{1,0:T(8,128)S(1)} %bitcast.7, bf16[256,32]{1,0:T(8,128)(2,1)S(1)} %copy-done, f32[32,8,128,128]{3,2,1,0:T(8,128)} %shard_map.196.refs_0_), custom_call_target="tpu_custom_call", output_to_operand_aliasing={{}: (3, {})} | custom-call | flops 4000000000 | bytes 12000000 | tf_op jit(solution)/shard_map/pallas_call | solution.py:613
  65.9 7.6 %all-to-all-done.2.arrived_ref = f32[16,16,512]{2,1,0:T(8,128)S(1)} async-done(((f32[16,16,512]{2,1,0:T(8,128)}), f32[16,16,512]{2,1,0:T(8,128)S(1)}, u32[]{:S(2)}, u32[]{:S(2)}) %all-to-all-start.2) | async-done | bytes 524320 | tf_op jit(solution)/shard_map/all_to_all | solution.py:693
  73.5 4.1 %all-to-all-start.3 = ((f32[16,16,512]{2,1,0:T(8,128)}), f32[16,16,512]{2,1,0:T(8,128)S(1)}, u32[]{:S(2)}, u32[]{:S(2)}) async-start(f32[16,16,512]{2,1,0:T(8,128)} %get-tuple-element.46), calls=%async_computation.3 | async-start | bytes 1048576 | tf_op jit(solution)/shard_map/all_to_all | solution.py:693
  77.7 18.7 %shard_map.200 = (f32[32,8,128,128]{3,2,1,0:T(8,128)}, f32[32,8,128,128]{3,2,1,0:T(8,128)}, f32[16,16,512]{2,1,0:T(8,128)}) custom-call(f32[16,16,512]{2,1,0:T(8,128)S(1)} %all-to-all-done.2.arrived_ref, f32[32,8,128,128]{3,2,1,0:T(8,128)} %shard_map.199.sum_ref, f32[32,8,128,128]{3,2,1,0:T(8,128)} %bitcast.14, bf16[128,192]{1,0:T(8,128)(2,1)S(1)} %copy-done.2, ...), custom_call_target="tpu_custom_call" | custom-call | flops 20000000000 | bytes 60000000 | tf_op jit(solution)/shard_map/pallas_call | solution.py:652
  96.4 6.0 %all-to-all-start.4 = ((f32[16,16,512]{2,1,0:T(8,128)}), f32[16,16,512]{2,1,0:T(8,128)S(1)}, u32[]{:S(2)}, u32[]{:S(2)}) async-start(f32[16,16,512]{2,1,0:T(8,128)} %get-tuple-element.54), calls=%async_computation.4 | async-start | bytes 1048576 | tf_op jit(solution)/shard_map/all_to_all | solution.py:693
  102.4 18.8 %shard_map.201 = (f32[32,8,128,128]{3,2,1,0:T(8,128)}, f32[32,8,128,128]{3,2,1,0:T(8,128)}, f32[16,16,512]{2,1,0:T(8,128)}) custom-call(f32[16,16,512]{2,1,0:T(8,128)S(1)} %all-to-all-done.3.arrived_ref, f32[32,8,128,128]{3,2,1,0:T(8,128)} %shard_map.199.sum_ref, f32[32,8,128,128]{3,2,1,0:T(8,128)} %bitcast.15, ...), custom_call_target="tpu_custom_call", output_to_operand_aliasing={{0}: (8, {}), {1}: (9, {})} | custom-call | flops 20000000000 | bytes 60000000 | tf_op jit(solution)/shard_map/pallas_call | solution.py:652
  121.2 6.0 %all-to-all-start.5 = ((f32[16,16,512]{2,1,0:T(8,128)}), f32[16,16,512]{2,1,0:T(8,128)S(1)}, u32[]{:S(2)}, u32[]{:S(2)}) async-start(f32[16,16,512]{2,1,0:T(8,128)} %get-tuple-element.57), calls=%async_computation.5 | async-start | bytes 1048576 | tf_op jit(solution)/shard_map/all_to_all | solution.py:693
  127.3 13.2 %shard_map.202.refs_0_ = f32[32,8,128,128]{3,2,1,0:T(8,128)} custom-call(f32[32,8,128,128]{3,2,1,0:T(8,128)} %get-tuple-element.58.data_ref, f32[32,32]{1,0:T(8,128)S(1)} %copy-done.3, bf16[256,32]{1,0:T(8,128)(2,1)S(1)} %copy-done), custom_call_target="tpu_custom_call" | custom-call | flops 12000000000 | bytes 36000000 | tf_op jit(solution)/shard_map/pallas_call | solution.py:613
  140.5 1.2 all-to-all-done.5.refs_1_
  141.7 5.7 %shard_map.203 = (f32[2,32,1024]{2,1,0:T(8,128)S(1)}, f32[16,16,512]{2,1,0:T(8,128)}) custom-call(f32[16,16,512]{2,1,0:T(8,128)S(1)} %all-to-all-done.4.refs_0_, f32[16,16,512]{2,1,0:T(8,128)S(1)} %all-to-all-done.5.refs_1_, f32[2,32,32,1024]{3,2,1,0:T(8,128)} %w.1, bf16[64,256]{1,0:T(8,128)(2,1)S(1)} %copy-done.10, bf16[64,256]{1,0:T(8,128)(2,1)S(1)} %copy-done.11, ...), custom_call_target="tpu_custom_call" | custom-call | flops 7000000000 | bytes 21000000 | tf_op jit(solution)/shard_map/pallas_call | solution.py:492
  147.4 4.8 %all-to-all-start.6 = ((f32[16,16,512]{2,1,0:T(8,128)}), f32[16,16,512]{2,1,0:T(8,128)S(1)}, u32[]{:S(2)}, u32[]{:S(2)}) async-start(f32[16,16,512]{2,1,0:T(8,128)} %get-tuple-element.61), calls=%async_computation.6 | async-start | bytes 1048576 | tf_op jit(solution)/shard_map/all_to_all | solution.py:693
  152.2 1.6 collective-permute-start.1
  153.8 1.0 copy-done.6
  154.8 4.4 %shard_map.204 = f32[16,16,512]{2,1,0:T(8,128)} custom-call(f32[2,32,1024]{2,1,0:T(8,128)S(1)} %get-tuple-element.62.g.g_ref, f32[2,32,32,1024]{3,2,1,0:T(8,128)} %w.1, bf16[64,256]{1,0:T(8,128)(2,1)S(1)} %copy-done.10, bf16[64,256]{1,0:T(8,128)(2,1)S(1)} %copy-done.11, bf16[2048,128]{1,0:T(8,128)(2,1)S(1)} %copy-done.6, bf16[256,192]{1,0:T(8,128)(2,1)S(1)} %copy-done.8), custom_call_target="tpu_custom_call" | custom-call | flops 6000000000 | bytes 18000000 | tf_op jit(solution)/shard_map/pallas_call | solution.py:505
  159.2 5.2 %shard_map.205.sum_ref = f32[32,8,128,128]{3,2,1,0:T(8,128)} custom-call(f32[32,8,128,128]{3,2,1,0:T(8,128)} %get-tuple-element.58.data_ref, f32[32,32]{1,0:T(8,128)S(1)} %copy-done.3, bf16[256,32]{1,0:T(8,128)(2,1)S(1)} %copy-done, f32[32,8,128,128]{3,2,1,0:T(8,128)} %shard_map.202.refs_0_), custom_call_target="tpu_custom_call", output_to_operand_aliasing={{}: (3, {})} | custom-call | flops 4000000000 | bytes 12000000 | tf_op jit(solution)/shard_map/pallas_call | solution.py:613
  164.4 2.3 %all-to-all-done.6.arrived_ref = f32[16,16,512]{2,1,0:T(8,128)S(1)} async-done(((f32[16,16,512]{2,1,0:T(8,128)}), f32[16,16,512]{2,1,0:T(8,128)S(1)}, u32[]{:S(2)}, u32[]{:S(2)}) %all-to-all-start.6) | async-done | bytes 524320 | tf_op jit(solution)/shard_map/all_to_all | solution.py:693
  166.7 4.1 %all-to-all-start.7 = ((f32[16,16,512]{2,1,0:T(8,128)}), f32[16,16,512]{2,1,0:T(8,128)S(1)}, u32[]{:S(2)}, u32[]{:S(2)}) async-start(f32[16,16,512]{2,1,0:T(8,128)} %shard_map.204), calls=%async_computation.7 | async-start | bytes 1048576 | tf_op jit(solution)/shard_map/all_to_all | solution.py:693
  171.9 5.8 %shard_map.207 = f32[2,32,32,1024]{3,2,1,0:T(8,128)} custom-call(f32[64,1024]{1,0:T(8,128)S(1)} %get-tuple-element.59.hat_ref, f32[64,1024]{1,0:T(8,128)S(1)} %collective-permute-done.far_hat_ref, f32[2,32,1024]{2,1,0:T(8,128)S(1)} %get-tuple-element.62.g.g_ref, f32[2,32,1024]{2,1,0:T(8,128)S(1)} %collective-permute-done.1.far_g_ref, ...), custom_call_target="tpu_custom_call" | custom-call | flops 8000000000 | bytes 24000000 | tf_op jit(solution)/shard_map/pallas_call | solution.py:534
  177.7 9.2 %shard_map.206.refs_0_ = f32[32,8,128,128]{3,2,1,0:T(8,128)} custom-call(f32[16,16,512]{2,1,0:T(8,128)S(1)} %all-to-all-done.6.arrived_ref, f32[32,8,128,128]{3,2,1,0:T(8,128)} %shard_map.205.sum_ref, bf16[128,192]{1,0:T(8,128)(2,1)S(1)} %copy-done.2, bf16[256,2048]{1,0:T(8,128)(2,1)S(1)} %copy-done.1, bf16[256,2048]{1,0:T(8,128)(2,1)} %constant.35.clone.zjl_ref), custom_call_target="tpu_custom_call" | custom-call | flops 10000000000 | bytes 30000000 | tf_op jit(solution)/shard_map/pallas_call | solution.py:680
  186.9 9.2 %shard_map.208 = f32[32,8,128,128]{3,2,1,0:T(8,128)} custom-call(f32[16,16,512]{2,1,0:T(8,128)S(1)} %all-to-all-done.7.arrived_ref, f32[32,8,128,128]{3,2,1,0:T(8,128)} %shard_map.205.sum_ref, bf16[128,192]{1,0:T(8,128)(2,1)S(1)} %copy-done.2, bf16[256,2048]{1,0:T(8,128)(2,1)S(1)} %copy-done.1, ...), custom_call_target="tpu_custom_call", output_to_operand_aliasing={{}: (5, {})} | custom-call | flops 10000000000 | bytes 30000000 | tf_op jit(solution)/shard_map/pallas_call | solution.py:680
  (31 shorter events, 2.0 us)
Async XLA Ops:
  0.6 14.9 %copy-start = (bf16[256,32]{1,0:T(8,128)(2,1)S(1)}, bf16[256,32]{1,0:T(8,128)(2,1)}, u32[]{:S(2)}) copy-start(bf16[256,32]{1,0:T(8,128)(2,1)} %constant.40.clone.rep_ref) | copy-start | bytes 49156
  0.6 14.8 %copy-start.3 = (f32[32,32]{1,0:T(8,128)S(1)}, f32[32,32]{1,0:T(8,128)}, u32[]{:S(2)}) copy-start(f32[32,32]{1,0:T(8,128)} %matrix_ref.3) | copy-start | bytes 12292
  8.1 21.9 %all-to-all-start = ((f32[16,16,512]{2,1,0:T(8,128)}), f32[16,16,512]{2,1,0:T(8,128)S(1)}, u32[]{:S(2)}, u32[]{:S(2)}) async-start(f32[16,16,512]{2,1,0:T(8,128)} %shard_map.193), calls=%async_computation | async-start | bytes 1048576 | tf_op jit(solution)/shard_map/all_to_all | solution.py:693
  20.8 13.5 %copy-start.4 = (bf16[128,2048]{1,0:T(8,128)(2,1)S(1)}, bf16[128,2048]{1,0:T(8,128)(2,1)}, u32[]{:S(2)}) copy-start(bf16[128,2048]{1,0:T(8,128)(2,1)} %constant.39.clone.refs_4_.spread_ref) | copy-start | bytes 1572868
  20.8 13.5 %copy-start.8 = (bf16[256,192]{1,0:T(8,128)(2,1)S(1)}, bf16[256,192]{1,0:T(8,128)(2,1)}, u32[]{:S(2)}) copy-start(bf16[256,192]{1,0:T(8,128)(2,1)} %constant.38.clone.refs_5_.refs_6_.xi) | copy-start | bytes 294916
  20.8 13.5 %copy-start.10 = (bf16[64,256]{1,0:T(8,128)(2,1)S(1)}, bf16[64,256]{1,0:T(8,128)(2,1)}, u32[]{:S(2)}) copy-start(bf16[64,256]{1,0:T(8,128)(2,1)} %constant.36.clone.refs_2_.refs_3_.xfh) | copy-start | bytes 98308
  20.8 13.5 %copy-start.11 = (bf16[64,256]{1,0:T(8,128)(2,1)S(1)}, bf16[64,256]{1,0:T(8,128)(2,1)}, u32[]{:S(2)}) copy-start(bf16[64,256]{1,0:T(8,128)(2,1)} %constant.37.clone.refs_3_.refs_4_.xfl) | copy-start | bytes 98308
  30.0 18.9 %all-to-all-start.1 = ((f32[16,16,512]{2,1,0:T(8,128)}), f32[16,16,512]{2,1,0:T(8,128)S(1)}, u32[]{:S(2)}, u32[]{:S(2)}) async-start(f32[16,16,512]{2,1,0:T(8,128)} %shard_map.194), calls=%async_computation.1 | async-start | bytes 1048576 | tf_op jit(solution)/shard_map/all_to_all | solution.py:693
  48.8 0.8 copy-start.12
  54.9 18.6 %all-to-all-start.2 = ((f32[16,16,512]{2,1,0:T(8,128)}), f32[16,16,512]{2,1,0:T(8,128)S(1)}, u32[]{:S(2)}, u32[]{:S(2)}) async-start(f32[16,16,512]{2,1,0:T(8,128)} %get-tuple-element.43), calls=%async_computation.2 | async-start | bytes 1048576 | tf_op jit(solution)/shard_map/all_to_all | solution.py:693
  59.1 18.6 %copy-start.2 = (bf16[128,192]{1,0:T(8,128)(2,1)S(1)}, bf16[128,192]{1,0:T(8,128)(2,1)}, u32[]{:S(2)}) copy-start(bf16[128,192]{1,0:T(8,128)(2,1)} %constant.29.clone.yi_ref) | copy-start | bytes 147460
  59.1 18.6 %copy-start.7 = (bf16[2,256,256]{2,1,0:T(8,128)(2,1)S(1)}, bf16[2,256,256]{2,1,0:T(8,128)(2,1)}, u32[]{:S(2)}) copy-start(bf16[2,256,256]{2,1,0:T(8,128)(2,1)} %constant.31.clone.zg_ref) | copy-start | bytes 786436
  59.1 18.6 %copy-start.9 = (bf16[128,256]{1,0:T(8,128)(2,1)S(1)}, bf16[128,256]{1,0:T(8,128)(2,1)}, u32[]{:S(2)}) copy-start(bf16[128,256]{1,0:T(8,128)(2,1)} %constant.28.clone.yf_ref) | copy-start | bytes 196612
  59.1 81.4 %collective-permute-start = (f32[64,1024]{1,0:T(8,128)S(1)}, f32[64,1024]{1,0:T(8,128)S(1)}, u32[]{:S(2)}, u32[]{:S(2)}) collective-permute-start(f32[64,1024]{1,0:T(8,128)S(1)} %get-tuple-element.59.hat_ref), channel_id=1, source_target_pairs={{0,16},{16,0},{1,17},{17,1},{2,18},{18,2},{3,19},{19,3},{4,20},{20... | collective-permute-start | bytes 786440 | tf_op jit(solution)/shard_map/ppermute | solution.py:723
  73.5 22.9 %all-to-all-start.3 = ((f32[16,16,512]{2,1,0:T(8,128)}), f32[16,16,512]{2,1,0:T(8,128)S(1)}, u32[]{:S(2)}, u32[]{:S(2)}) async-start(f32[16,16,512]{2,1,0:T(8,128)} %get-tuple-element.46), calls=%async_computation.3 | async-start | bytes 1048576 | tf_op jit(solution)/shard_map/all_to_all | solution.py:693
  96.4 24.8 %all-to-all-start.4 = ((f32[16,16,512]{2,1,0:T(8,128)}), f32[16,16,512]{2,1,0:T(8,128)S(1)}, u32[]{:S(2)}, u32[]{:S(2)}) async-start(f32[16,16,512]{2,1,0:T(8,128)} %get-tuple-element.54), calls=%async_computation.4 | async-start | bytes 1048576 | tf_op jit(solution)/shard_map/all_to_all | solution.py:693
  121.2 20.5 %all-to-all-start.5 = ((f32[16,16,512]{2,1,0:T(8,128)}), f32[16,16,512]{2,1,0:T(8,128)S(1)}, u32[]{:S(2)}, u32[]{:S(2)}) async-start(f32[16,16,512]{2,1,0:T(8,128)} %get-tuple-element.57), calls=%async_computation.5 | async-start | bytes 1048576 | tf_op jit(solution)/shard_map/all_to_all | solution.py:693
  147.4 19.3 %all-to-all-start.6 = ((f32[16,16,512]{2,1,0:T(8,128)}), f32[16,16,512]{2,1,0:T(8,128)S(1)}, u32[]{:S(2)}, u32[]{:S(2)}) async-start(f32[16,16,512]{2,1,0:T(8,128)} %get-tuple-element.61), calls=%async_computation.6 | async-start | bytes 1048576 | tf_op jit(solution)/shard_map/all_to_all | solution.py:693
  152.2 18.6 %collective-permute-start.1 = (f32[2,32,1024]{2,1,0:T(8,128)S(1)}, f32[2,32,1024]{2,1,0:T(8,128)S(1)}, u32[]{:S(2)}, u32[]{:S(2)}) collective-permute-start(f32[2,32,1024]{2,1,0:T(8,128)S(1)} %get-tuple-element.62.g.g_ref), channel_id=1, source_target_pairs={{0,16},{16,0},{1,17},{17,1},{2,18},{18,2},{3,19},{19,3},{4,20},{20... | collective-permute-start | bytes 786440 | tf_op jit(solution)/shard_map/ppermute | solution.py:747
  153.8 1.0 copy-start.6
  164.4 13.3 %copy-start.1 = (bf16[256,2048]{1,0:T(8,128)(2,1)S(1)}, bf16[256,2048]{1,0:T(8,128)(2,1)}, u32[]{:S(2)}) copy-start(bf16[256,2048]{1,0:T(8,128)(2,1)} %constant.34.clone.zjh_ref) | copy-start | bytes 3145732
  166.7 20.2 %all-to-all-start.7 = ((f32[16,16,512]{2,1,0:T(8,128)}), f32[16,16,512]{2,1,0:T(8,128)S(1)}, u32[]{:S(2)}, u32[]{:S(2)}) async-start(f32[16,16,512]{2,1,0:T(8,128)} %shard_map.204), calls=%async_computation.7 | async-start | bytes 1048576 | tf_op jit(solution)/shard_map/all_to_all | solution.py:693
  170.8 1.0 copy-start.5

commit v5 on v4

--- a/solution.py
+++ b/solution.py
@@ -233,12 +233,6 @@
     return jnp.dot(left, right, preferred_element_type=F32)
 
 
-def dot3(high, low, table_high, table_low):
-    rows = high.shape[0]
-    both = dot(jnp.concatenate([high, low], axis=0), table_high)
-    return both[:rows] + both[rows:] + dot(high, table_low)
-
-
 def lines_to_modes(pair, yf):
     high, low = halves(pair)
     both = dot(yf, jnp.concatenate([high, low], axis=0))
@@ -279,7 +273,8 @@
 
 
 def send_modes(high_s, low_s, table_ref, out_ref):
-    full = dot3(high_s[...], low_s[...], table_ref[0], table_ref[1])
+    high, low = high_s[...], low_s[...]
+    full = dot(high, table_ref[0]) + dot(low, table_ref[0]) + dot(high, table_ref[1])
     owner = lax.broadcasted_iota(jnp.int32, (ROWS, 2 * TILE), 1) % TILE // KZ
     sums = full[:ROWS]
     for i in range(1, BLOCKS):
@@ -437,6 +432,7 @@
         [hat] + outs,
         scratch,
         aliases={} if first else {7: 0},
+        vmem=48 * 1024 * 1024,
     )(moved, weights, *tables, *so_far)
 
 
@@ -562,7 +558,8 @@
         block = arrived_ref[:, part * PLANES : (part + 1) * PLANES, :]
         parts.append(jnp.swapaxes(block, 0, 1).reshape(PLANES * KYH, TILE))
     high, low = halves(jnp.concatenate(parts, axis=1))
-    return halves(dot3(high, low, zih, zil))
+    tables = jnp.concatenate([zih, zih, zil], axis=0)
+    return halves(dot(jnp.concatenate([high, low, high], axis=1), tables))
 
 
 def inverse_pair(high, low, x, half, yi):

time: 197 us -> 196 us (level)
  no operation moved by 1% of the time
where the time goes in v5:
time: 196 us; the launch traced here: 195 us
  Pallas kernels  133 us (68%)
  starting transfers between devices  44.1 us (22%)
  waiting for transfers between devices  14.6 us (7%)
  local copies, waits for them, and re-layouts  2.2 us (1%)
    all_to_all x8, starting transfers between devices, swap_slabs(): lax.all_to_all(array, 'slab', split_axis=0, concat_axis=0, tiled=True)  41 us
    pallas_call x5, Pallas kernels, channel_sum(): call(channel_sum_body, 2 * count, (count // step,), [block, whole(matrix)...  38.4 us
    pallas_call x2, Pallas kernels, middle(): call(middle_body, 5 * count, (count,), [moved_block(), block, block] + [w...  36.9 us
    pallas_call x2, Pallas kernels, last(): call(last_body, 2.5 * count, (count,), [moved_block(), block] + [whole(a)...  18.5 us
    pallas_call x2, Pallas kernels, spectrum(): call(spectrum_body, 2 * count, (count,), [channel_block(first)] + [whole(...  15 us
    all_to_all x8, waiting for transfers between devices, swap_slabs(): lax.all_to_all(array, 'slab', split_axis=0, concat_axis=0, tiled=True)  14.6 us
    pallas_call x2, Pallas kernels, mix(): call(functools.partial(mix_body, first, last, count // PER), 5, (count //...  8.31 us
    pallas_call x1, Pallas kernels, weight_grad(): call(weight_grad_body, count, (count // PER,), [hat_block(at), hat_block(...  5.83 us
  transfers between devices with their start and end apart: 10, of which 5 were waited for; matrix products, arithmetic and copies ran while one was open for 0% of the time, Pallas kernels for 54%

profile of v5, /device:TPU:0, one launch (start us, length us, event | category | flops | bytes accessed | tf_op | source)
XLA Modules:
  0.0 194.6 jit_solution(1696813179136195608)
XLA Ops:
  0.7 7.5 %shard_map.193 = f32[16,16,512]{2,1,0:T(8,128)} custom-call(f32[32,8,128,128]{3,2,1,0:T(8,128)} %bitcast.8, bf16[128,256]{1,0:T(8,128)(2,1)} %constant.28.clone.yf_ref, bf16[2,256,256]{2,1,0:T(8,128)(2,1)} %constant.30.clone.table_ref), custom_call_target="tpu_custom_call" | custom-call | flops 8000000000 | bytes 24000000 | tf_op jit(solution)/shard_map/pallas_call | solution.py:323
  8.1 7.4 %all-to-all-start = ((f32[16,16,512]{2,1,0:T(8,128)}), f32[16,16,512]{2,1,0:T(8,128)S(1)}, u32[]{:S(2)}, u32[]{:S(2)}) async-start(f32[16,16,512]{2,1,0:T(8,128)} %shard_map.193), calls=%async_computation | async-start | bytes 1048576 | tf_op jit(solution)/shard_map/all_to_all | solution.py:690
  15.6 5.3 %shard_map.195.refs_0_ = f32[32,8,128,128]{3,2,1,0:T(8,128)} custom-call(f32[32,8,128,128]{3,2,1,0:T(8,128)} %bitcast.9, f32[32,32]{1,0:T(8,128)S(1)} %bitcast.5, bf16[256,32]{1,0:T(8,128)(2,1)S(1)} %copy-done), custom_call_target="tpu_custom_call" | custom-call | flops 4000000000 | bytes 12000000 | tf_op jit(solution)/shard_map/pallas_call | solution.py:610
  20.9 7.5 %shard_map.194 = f32[16,16,512]{2,1,0:T(8,128)} custom-call(f32[32,8,128,128]{3,2,1,0:T(8,128)} %bitcast.10, bf16[128,256]{1,0:T(8,128)(2,1)} %constant.28.clone.yf_ref, bf16[2,256,256]{2,1,0:T(8,128)(2,1)} %constant.30.clone.table_ref), custom_call_target="tpu_custom_call" | custom-call | flops 8000000000 | bytes 24000000 | tf_op jit(solution)/shard_map/pallas_call | solution.py:323
  28.3 1.6 all-to-all-done.refs_0_
  30.0 4.4 %all-to-all-start.1 = ((f32[16,16,512]{2,1,0:T(8,128)}), f32[16,16,512]{2,1,0:T(8,128)S(1)}, u32[]{:S(2)}, u32[]{:S(2)}) async-start(f32[16,16,512]{2,1,0:T(8,128)} %shard_map.194), calls=%async_computation.1 | async-start | bytes 1048576 | tf_op jit(solution)/shard_map/all_to_all | solution.py:690
  34.4 3.2 %shard_map.197 = (f32[64,1024]{1,0:T(8,128)S(1)}, f32[2,32,1024]{2,1,0:T(8,128)S(1)}) custom-call(f32[16,16,512]{2,1,0:T(8,128)S(1)} %all-to-all-done.refs_0_, f32[2,32,32,1024]{3,2,1,0:T(8,128)} %w.1, bf16[64,256]{1,0:T(8,128)(2,1)S(1)} %copy-done.10, bf16[64,256]{1,0:T(8,128)(2,1)S(1)} %copy-done.11, bf16[128,2048]{1,0:T(8,128)(2,1)S(1)} %copy-done.4, ...), custom_call_target="tpu_custom_call" | custom-call | flops 5000000000 | bytes 15000000 | tf_op jit(solution)/shard_map/pallas_call | solution.py:426
  37.6 9.4 %shard_map.196.refs_0_ = f32[32,8,128,128]{3,2,1,0:T(8,128)} custom-call(f32[32,8,128,128]{3,2,1,0:T(8,128)} %bitcast.11, f32[32,32]{1,0:T(8,128)S(1)} %bitcast.6, bf16[256,32]{1,0:T(8,128)(2,1)S(1)} %copy-done, f32[32,8,128,128]{3,2,1,0:T(8,128)} %shard_map.195.refs_0_), custom_call_target="tpu_custom_call", output_to_operand_aliasing={{}: (3, {})} | custom-call | flops 8000000000 | bytes 24000000 | tf_op jit(solution)/shard_map/pallas_call | solution.py:610
  47.0 1.9 all-to-all-done.1.refs_0_
  48.8 5.2 %shard_map.198 = (f32[64,1024]{1,0:T(8,128)S(1)}, f32[16,16,512]{2,1,0:T(8,128)}, f32[16,16,512]{2,1,0:T(8,128)}) custom-call(f32[16,16,512]{2,1,0:T(8,128)S(1)} %all-to-all-done.1.refs_0_, f32[2,32,32,1024]{3,2,1,0:T(8,128)} %w.1, bf16[64,256]{1,0:T(8,128)(2,1)S(1)} %copy-done.10, bf16[64,256]{1,0:T(8,128)(2,1)S(1)} %copy-done.11, ...), custom_call_target="tpu_custom_call", output_to_operand_aliasing={{0}: (7, {})} | custom-call | flops 5000000000 | bytes 15000000 | tf_op jit(solution)/shard_map/pallas_call | solution.py:426
  54.0 4.1 %all-to-all-start.2 = ((f32[16,16,512]{2,1,0:T(8,128)}), f32[16,16,512]{2,1,0:T(8,128)S(1)}, u32[]{:S(2)}, u32[]{:S(2)}) async-start(f32[16,16,512]{2,1,0:T(8,128)} %get-tuple-element.43), calls=%async_computation.2 | async-start | bytes 1048576 | tf_op jit(solution)/shard_map/all_to_all | solution.py:690
  58.2 1.6 collective-permute-start
  59.7 5.3 %shard_map.199.sum_ref = f32[32,8,128,128]{3,2,1,0:T(8,128)} custom-call(f32[32,8,128,128]{3,2,1,0:T(8,128)} %bitcast.12, f32[32,32]{1,0:T(8,128)S(1)} %bitcast.7, bf16[256,32]{1,0:T(8,128)(2,1)S(1)} %copy-done, f32[32,8,128,128]{3,2,1,0:T(8,128)} %shard_map.196.refs_0_), custom_call_target="tpu_custom_call", output_to_operand_aliasing={{}: (3, {})} | custom-call | flops 4000000000 | bytes 12000000 | tf_op jit(solution)/shard_map/pallas_call | solution.py:610
  65.0 7.6 %all-to-all-done.2.arrived_ref = f32[16,16,512]{2,1,0:T(8,128)S(1)} async-done(((f32[16,16,512]{2,1,0:T(8,128)}), f32[16,16,512]{2,1,0:T(8,128)S(1)}, u32[]{:S(2)}, u32[]{:S(2)}) %all-to-all-start.2) | async-done | bytes 524320 | tf_op jit(solution)/shard_map/all_to_all | solution.py:690
  72.6 4.1 %all-to-all-start.3 = ((f32[16,16,512]{2,1,0:T(8,128)}), f32[16,16,512]{2,1,0:T(8,128)S(1)}, u32[]{:S(2)}, u32[]{:S(2)}) async-start(f32[16,16,512]{2,1,0:T(8,128)} %get-tuple-element.46), calls=%async_computation.3 | async-start | bytes 1048576 | tf_op jit(solution)/shard_map/all_to_all | solution.py:690
  76.7 18.4 %shard_map.200 = (f32[32,8,128,128]{3,2,1,0:T(8,128)}, f32[32,8,128,128]{3,2,1,0:T(8,128)}, f32[16,16,512]{2,1,0:T(8,128)}) custom-call(f32[16,16,512]{2,1,0:T(8,128)S(1)} %all-to-all-done.2.arrived_ref, f32[32,8,128,128]{3,2,1,0:T(8,128)} %shard_map.199.sum_ref, f32[32,8,128,128]{3,2,1,0:T(8,128)} %bitcast.14, bf16[128,192]{1,0:T(8,128)(2,1)S(1)} %copy-done.2, ...), custom_call_target="tpu_custom_call" | custom-call | flops 20000000000 | bytes 60000000 | tf_op jit(solution)/shard_map/pallas_call | solution.py:649
  95.1 6.0 %all-to-all-start.4 = ((f32[16,16,512]{2,1,0:T(8,128)}), f32[16,16,512]{2,1,0:T(8,128)S(1)}, u32[]{:S(2)}, u32[]{:S(2)}) async-start(f32[16,16,512]{2,1,0:T(8,128)} %get-tuple-element.54), calls=%async_computation.4 | async-start | bytes 1048576 | tf_op jit(solution)/shard_map/all_to_all | solution.py:690
  101.2 18.5 %shard_map.201 = (f32[32,8,128,128]{3,2,1,0:T(8,128)}, f32[32,8,128,128]{3,2,1,0:T(8,128)}, f32[16,16,512]{2,1,0:T(8,128)}) custom-call(f32[16,16,512]{2,1,0:T(8,128)S(1)} %all-to-all-done.3.arrived_ref, f32[32,8,128,128]{3,2,1,0:T(8,128)} %shard_map.199.sum_ref, f32[32,8,128,128]{3,2,1,0:T(8,128)} %bitcast.15, ...), custom_call_target="tpu_custom_call", output_to_operand_aliasing={{0}: (8, {}), {1}: (9, {})} | custom-call | flops 20000000000 | bytes 60000000 | tf_op jit(solution)/shard_map/pallas_call | solution.py:649
  119.6 6.0 %all-to-all-start.5 = ((f32[16,16,512]{2,1,0:T(8,128)}), f32[16,16,512]{2,1,0:T(8,128)S(1)}, u32[]{:S(2)}, u32[]{:S(2)}) async-start(f32[16,16,512]{2,1,0:T(8,128)} %get-tuple-element.57), calls=%async_computation.5 | async-start | bytes 1048576 | tf_op jit(solution)/shard_map/all_to_all | solution.py:690
  125.6 13.3 %shard_map.202.refs_0_ = f32[32,8,128,128]{3,2,1,0:T(8,128)} custom-call(f32[32,8,128,128]{3,2,1,0:T(8,128)} %get-tuple-element.58.data_ref, f32[32,32]{1,0:T(8,128)S(1)} %copy-done.3, bf16[256,32]{1,0:T(8,128)(2,1)S(1)} %copy-done), custom_call_target="tpu_custom_call" | custom-call | flops 12000000000 | bytes 36000000 | tf_op jit(solution)/shard_map/pallas_call | solution.py:610
  138.9 1.2 all-to-all-done.5.refs_1_
  140.1 5.7 %shard_map.203 = (f32[2,32,1024]{2,1,0:T(8,128)S(1)}, f32[16,16,512]{2,1,0:T(8,128)}) custom-call(f32[16,16,512]{2,1,0:T(8,128)S(1)} %all-to-all-done.4.refs_0_, f32[16,16,512]{2,1,0:T(8,128)S(1)} %all-to-all-done.5.refs_1_, f32[2,32,32,1024]{3,2,1,0:T(8,128)} %w.1, bf16[64,256]{1,0:T(8,128)(2,1)S(1)} %copy-done.10, bf16[64,256]{1,0:T(8,128)(2,1)S(1)} %copy-done.11, ...), custom_call_target="tpu_custom_call" | custom-call | flops 7000000000 | bytes 21000000 | tf_op jit(solution)/shard_map/pallas_call | solution.py:488
  145.8 4.8 %all-to-all-start.6 = ((f32[16,16,512]{2,1,0:T(8,128)}), f32[16,16,512]{2,1,0:T(8,128)S(1)}, u32[]{:S(2)}, u32[]{:S(2)}) async-start(f32[16,16,512]{2,1,0:T(8,128)} %get-tuple-element.61), calls=%async_computation.6 | async-start | bytes 1048576 | tf_op jit(solution)/shard_map/all_to_all | solution.py:690
  150.6 1.6 collective-permute-start.1
  152.2 1.0 copy-done.6
  153.2 4.4 %shard_map.204 = f32[16,16,512]{2,1,0:T(8,128)} custom-call(f32[2,32,1024]{2,1,0:T(8,128)S(1)} %get-tuple-element.62.g.g_ref, f32[2,32,32,1024]{3,2,1,0:T(8,128)} %w.1, bf16[64,256]{1,0:T(8,128)(2,1)S(1)} %copy-done.10, bf16[64,256]{1,0:T(8,128)(2,1)S(1)} %copy-done.11, bf16[2048,128]{1,0:T(8,128)(2,1)S(1)} %copy-done.6, bf16[256,192]{1,0:T(8,128)(2,1)S(1)} %copy-done.8), custom_call_target="tpu_custom_call" | custom-call | flops 6000000000 | bytes 18000000 | tf_op jit(solution)/shard_map/pallas_call | solution.py:501
  157.6 5.2 %shard_map.205.sum_ref = f32[32,8,128,128]{3,2,1,0:T(8,128)} custom-call(f32[32,8,128,128]{3,2,1,0:T(8,128)} %get-tuple-element.58.data_ref, f32[32,32]{1,0:T(8,128)S(1)} %copy-done.3, bf16[256,32]{1,0:T(8,128)(2,1)S(1)} %copy-done, f32[32,8,128,128]{3,2,1,0:T(8,128)} %shard_map.202.refs_0_), custom_call_target="tpu_custom_call", output_to_operand_aliasing={{}: (3, {})} | custom-call | flops 4000000000 | bytes 12000000 | tf_op jit(solution)/shard_map/pallas_call | solution.py:610
  162.8 2.3 %all-to-all-done.6.arrived_ref = f32[16,16,512]{2,1,0:T(8,128)S(1)} async-done(((f32[16,16,512]{2,1,0:T(8,128)}), f32[16,16,512]{2,1,0:T(8,128)S(1)}, u32[]{:S(2)}, u32[]{:S(2)}) %all-to-all-start.6) | async-done | bytes 524320 | tf_op jit(solution)/shard_map/all_to_all | solution.py:690
  165.1 4.1 %all-to-all-start.7 = ((f32[16,16,512]{2,1,0:T(8,128)}), f32[16,16,512]{2,1,0:T(8,128)S(1)}, u32[]{:S(2)}, u32[]{:S(2)}) async-start(f32[16,16,512]{2,1,0:T(8,128)} %shard_map.204), calls=%async_computation.7 | async-start | bytes 1048576 | tf_op jit(solution)/shard_map/all_to_all | solution.py:690
  170.3 5.8 %shard_map.207 = f32[2,32,32,1024]{3,2,1,0:T(8,128)} custom-call(f32[64,1024]{1,0:T(8,128)S(1)} %get-tuple-element.59.hat_ref, f32[64,1024]{1,0:T(8,128)S(1)} %collective-permute-done.far_hat_ref, f32[2,32,1024]{2,1,0:T(8,128)S(1)} %get-tuple-element.62.g.g_ref, f32[2,32,1024]{2,1,0:T(8,128)S(1)} %collective-permute-done.1.far_g_ref, ...), custom_call_target="tpu_custom_call" | custom-call | flops 8000000000 | bytes 24000000 | tf_op jit(solution)/shard_map/pallas_call | solution.py:530
  176.1 9.3 %shard_map.206.refs_0_ = f32[32,8,128,128]{3,2,1,0:T(8,128)} custom-call(f32[16,16,512]{2,1,0:T(8,128)S(1)} %all-to-all-done.6.arrived_ref, f32[32,8,128,128]{3,2,1,0:T(8,128)} %shard_map.205.sum_ref, bf16[128,192]{1,0:T(8,128)(2,1)S(1)} %copy-done.2, bf16[256,2048]{1,0:T(8,128)(2,1)S(1)} %copy-done.1, bf16[256,2048]{1,0:T(8,128)(2,1)} %constant.35.clone.zjl_ref), custom_call_target="tpu_custom_call" | custom-call | flops 10000000000 | bytes 30000000 | tf_op jit(solution)/shard_map/pallas_call | solution.py:677
  185.4 9.3 %shard_map.208 = f32[32,8,128,128]{3,2,1,0:T(8,128)} custom-call(f32[16,16,512]{2,1,0:T(8,128)S(1)} %all-to-all-done.7.arrived_ref, f32[32,8,128,128]{3,2,1,0:T(8,128)} %shard_map.205.sum_ref, bf16[128,192]{1,0:T(8,128)(2,1)S(1)} %copy-done.2, bf16[256,2048]{1,0:T(8,128)(2,1)S(1)} %copy-done.1, ...), custom_call_target="tpu_custom_call", output_to_operand_aliasing={{}: (5, {})} | custom-call | flops 10000000000 | bytes 30000000 | tf_op jit(solution)/shard_map/pallas_call | solution.py:677
  (29 shorter events, 1.2 us)
Async XLA Ops:
  0.6 15.0 %copy-start = (bf16[256,32]{1,0:T(8,128)(2,1)S(1)}, bf16[256,32]{1,0:T(8,128)(2,1)}, u32[]{:S(2)}) copy-start(bf16[256,32]{1,0:T(8,128)(2,1)} %constant.40.clone.rep_ref) | copy-start | bytes 49156
  0.6 14.9 %copy-start.3 = (f32[32,32]{1,0:T(8,128)S(1)}, f32[32,32]{1,0:T(8,128)}, u32[]{:S(2)}) copy-start(f32[32,32]{1,0:T(8,128)} %matrix_ref.3) | copy-start | bytes 12292
  8.1 21.9 %all-to-all-start = ((f32[16,16,512]{2,1,0:T(8,128)}), f32[16,16,512]{2,1,0:T(8,128)S(1)}, u32[]{:S(2)}, u32[]{:S(2)}) async-start(f32[16,16,512]{2,1,0:T(8,128)} %shard_map.193), calls=%async_computation | async-start | bytes 1048576 | tf_op jit(solution)/shard_map/all_to_all | solution.py:690
  20.8 13.5 %copy-start.4 = (bf16[128,2048]{1,0:T(8,128)(2,1)S(1)}, bf16[128,2048]{1,0:T(8,128)(2,1)}, u32[]{:S(2)}) copy-start(bf16[128,2048]{1,0:T(8,128)(2,1)} %constant.39.clone.refs_4_.spread_ref) | copy-start | bytes 1572868
  20.8 13.5 %copy-start.8 = (bf16[256,192]{1,0:T(8,128)(2,1)S(1)}, bf16[256,192]{1,0:T(8,128)(2,1)}, u32[]{:S(2)}) copy-start(bf16[256,192]{1,0:T(8,128)(2,1)} %constant.38.clone.refs_5_.refs_6_.xi) | copy-start | bytes 294916
  20.8 13.6 %copy-start.10 = (bf16[64,256]{1,0:T(8,128)(2,1)S(1)}, bf16[64,256]{1,0:T(8,128)(2,1)}, u32[]{:S(2)}) copy-start(bf16[64,256]{1,0:T(8,128)(2,1)} %constant.36.clone.refs_2_.refs_3_.xfh) | copy-start | bytes 98308
  20.8 13.6 %copy-start.11 = (bf16[64,256]{1,0:T(8,128)(2,1)S(1)}, bf16[64,256]{1,0:T(8,128)(2,1)}, u32[]{:S(2)}) copy-start(bf16[64,256]{1,0:T(8,128)(2,1)} %constant.37.clone.refs_3_.refs_4_.xfl) | copy-start | bytes 98308
  30.0 18.9 %all-to-all-start.1 = ((f32[16,16,512]{2,1,0:T(8,128)}), f32[16,16,512]{2,1,0:T(8,128)S(1)}, u32[]{:S(2)}, u32[]{:S(2)}) async-start(f32[16,16,512]{2,1,0:T(8,128)} %shard_map.194), calls=%async_computation.1 | async-start | bytes 1048576 | tf_op jit(solution)/shard_map/all_to_all | solution.py:690
  54.0 18.6 %all-to-all-start.2 = ((f32[16,16,512]{2,1,0:T(8,128)}), f32[16,16,512]{2,1,0:T(8,128)S(1)}, u32[]{:S(2)}, u32[]{:S(2)}) async-start(f32[16,16,512]{2,1,0:T(8,128)} %get-tuple-element.43), calls=%async_computation.2 | async-start | bytes 1048576 | tf_op jit(solution)/shard_map/all_to_all | solution.py:690
  58.1 18.6 %copy-start.2 = (bf16[128,192]{1,0:T(8,128)(2,1)S(1)}, bf16[128,192]{1,0:T(8,128)(2,1)}, u32[]{:S(2)}) copy-start(bf16[128,192]{1,0:T(8,128)(2,1)} %constant.29.clone.yi_ref) | copy-start | bytes 147460
  58.2 18.6 %copy-start.7 = (bf16[2,256,256]{2,1,0:T(8,128)(2,1)S(1)}, bf16[2,256,256]{2,1,0:T(8,128)(2,1)}, u32[]{:S(2)}) copy-start(bf16[2,256,256]{2,1,0:T(8,128)(2,1)} %constant.31.clone.zg_ref) | copy-start | bytes 786436
  58.2 18.6 %copy-start.9 = (bf16[128,256]{1,0:T(8,128)(2,1)S(1)}, bf16[128,256]{1,0:T(8,128)(2,1)}, u32[]{:S(2)}) copy-start(bf16[128,256]{1,0:T(8,128)(2,1)} %constant.28.clone.yf_ref) | copy-start | bytes 196612
  58.2 80.8 %collective-permute-start = (f32[64,1024]{1,0:T(8,128)S(1)}, f32[64,1024]{1,0:T(8,128)S(1)}, u32[]{:S(2)}, u32[]{:S(2)}) collective-permute-start(f32[64,1024]{1,0:T(8,128)S(1)} %get-tuple-element.59.hat_ref), channel_id=1, source_target_pairs={{0,16},{16,0},{1,17},{17,1},{2,18},{18,2},{3,19},{19,3},{4,20},{20... | collective-permute-start | bytes 786440 | tf_op jit(solution)/shard_map/ppermute | solution.py:720
  72.6 22.5 %all-to-all-start.3 = ((f32[16,16,512]{2,1,0:T(8,128)}), f32[16,16,512]{2,1,0:T(8,128)S(1)}, u32[]{:S(2)}, u32[]{:S(2)}) async-start(f32[16,16,512]{2,1,0:T(8,128)} %get-tuple-element.46), calls=%async_computation.3 | async-start | bytes 1048576 | tf_op jit(solution)/shard_map/all_to_all | solution.py:690
  95.1 24.5 %all-to-all-start.4 = ((f32[16,16,512]{2,1,0:T(8,128)}), f32[16,16,512]{2,1,0:T(8,128)S(1)}, u32[]{:S(2)}, u32[]{:S(2)}) async-start(f32[16,16,512]{2,1,0:T(8,128)} %get-tuple-element.54), calls=%async_computation.4 | async-start | bytes 1048576 | tf_op jit(solution)/shard_map/all_to_all | solution.py:690
  119.6 20.5 %all-to-all-start.5 = ((f32[16,16,512]{2,1,0:T(8,128)}), f32[16,16,512]{2,1,0:T(8,128)S(1)}, u32[]{:S(2)}, u32[]{:S(2)}) async-start(f32[16,16,512]{2,1,0:T(8,128)} %get-tuple-element.57), calls=%async_computation.5 | async-start | bytes 1048576 | tf_op jit(solution)/shard_map/all_to_all | solution.py:690
  145.8 19.3 %all-to-all-start.6 = ((f32[16,16,512]{2,1,0:T(8,128)}), f32[16,16,512]{2,1,0:T(8,128)S(1)}, u32[]{:S(2)}, u32[]{:S(2)}) async-start(f32[16,16,512]{2,1,0:T(8,128)} %get-tuple-element.61), calls=%async_computation.6 | async-start | bytes 1048576 | tf_op jit(solution)/shard_map/all_to_all | solution.py:690
  150.6 18.6 %collective-permute-start.1 = (f32[2,32,1024]{2,1,0:T(8,128)S(1)}, f32[2,32,1024]{2,1,0:T(8,128)S(1)}, u32[]{:S(2)}, u32[]{:S(2)}) collective-permute-start(f32[2,32,1024]{2,1,0:T(8,128)S(1)} %get-tuple-element.62.g.g_ref), channel_id=1, source_target_pairs={{0,16},{16,0},{1,17},{17,1},{2,18},{18,2},{3,19},{19,3},{4,20},{20... | collective-permute-start | bytes 786440 | tf_op jit(solution)/shard_map/ppermute | solution.py:744
  152.2 1.0 copy-start.6
  162.8 13.3 %copy-start.1 = (bf16[256,2048]{1,0:T(8,128)(2,1)S(1)}, bf16[256,2048]{1,0:T(8,128)(2,1)}, u32[]{:S(2)}) copy-start(bf16[256,2048]{1,0:T(8,128)(2,1)} %constant.34.clone.zjh_ref) | copy-start | bytes 3145732
  165.1 20.3 %all-to-all-start.7 = ((f32[16,16,512]{2,1,0:T(8,128)}), f32[16,16,512]{2,1,0:T(8,128)S(1)}, u32[]{:S(2)}, u32[]{:S(2)}) async-start(f32[16,16,512]{2,1,0:T(8,128)} %shard_map.204), calls=%async_computation.7 | async-start | bytes 1048576 | tf_op jit(solution)/shard_map/all_to_all | solution.py:690
  169.2 1.0 copy-start.5

commit v6 on v5

--- a/solution.py
+++ b/solution.py
@@ -739,11 +739,12 @@
         grad, sent = input_modes(cot_moved, grad, spec_weight, at, n, t)
         if back_arrived:
             back_sums = channel_sum(grad_pre, bypass_weight, 6, 2, 1, (back_sums,), t)
-            back_arrived[-1], sent, back_sums = ahead((back_arrived[-1], sent, back_sums))
+            made = weight_grad(hat, far_hat, grad, far_grad, 0, PER, (), t)
+            back_arrived[-1], sent, back_sums, made = ahead((back_arrived[-1], sent, back_sums, made))
         else:
             far_grad = lax.ppermute(grad, "dp", swap_pair)
         back_arrived.append(swap_slabs(sent))
-    grad_spec = weight_grad(hat, far_hat, grad, far_grad, 0, GROUPS, (), t)
+    grad_spec = weight_grad(hat, far_hat, grad, far_grad, PER, GROUPS - PER, (made,), t)
     back = ()
     for k, (at, n) in enumerate(parts):
         if k == 1:

time: 196 us -> 197 us (level)
    pallas_call x1 -> x2, Pallas kernels: 5.83 us -> 7.12 us  [weight_grad(): call(weight_grad_body, count, (count // PER,), [hat_block(at), hat_block(...]
  transfers between devices with their start and end apart: 10 -> 10, of which waited for: 5 -> 5; matrix products, arithmetic and copies ran while one was open for 0% -> 0% of each run, Pallas kernels for 54% -> 55%
where the time goes in v6:
time: 197 us; the launch traced here: 195 us
  Pallas kernels  134 us (68%)
  starting transfers between devices  44.5 us (23%)
  waiting for transfers between devices  13.7 us (7%)
  local copies, waits for them, and re-layouts  2.11 us (1%)
    all_to_all x8, starting transfers between devices, swap_slabs(): lax.all_to_all(array, 'slab', split_axis=0, concat_axis=0, tiled=True)  41.5 us
    pallas_call x5, Pallas kernels, channel_sum(): call(channel_sum_body, 2 * count, (count // step,), [block, whole(matrix)...  38.5 us
    pallas_call x2, Pallas kernels, middle(): call(middle_body, 5 * count, (count,), [moved_block(), block, block] + [w...  36.9 us
    pallas_call x2, Pallas kernels, last(): call(last_body, 2.5 * count, (count,), [moved_block(), block] + [whole(a)...  18.5 us
    pallas_call x2, Pallas kernels, spectrum(): call(spectrum_body, 2 * count, (count,), [channel_block(first)] + [whole(...  15 us
    all_to_all x8, waiting for transfers between devices, swap_slabs(): lax.all_to_all(array, 'slab', split_axis=0, concat_axis=0, tiled=True)  13.7 us
    pallas_call x2, Pallas kernels, mix(): call(functools.partial(mix_body, first, last, count // PER), 5, (count //...  8.32 us
    pallas_call x2, Pallas kernels, weight_grad(): call(weight_grad_body, count, (count // PER,), [hat_block(at), hat_block(...  7.12 us
  transfers between devices with their start and end apart: 10, of which 5 were waited for; matrix products, arithmetic and copies ran while one was open for 0% of the time, Pallas kernels for 55%

profile of v6, /device:TPU:0, one launch (start us, length us, event | category | flops | bytes accessed | tf_op | source)
XLA Modules:
  0.0 195.5 jit_solution(2587309410877563840)
XLA Ops:
  0.7 7.5 %shard_map.193 = f32[16,16,512]{2,1,0:T(8,128)} custom-call(f32[32,8,128,128]{3,2,1,0:T(8,128)} %bitcast.8, bf16[128,256]{1,0:T(8,128)(2,1)} %constant.28.clone.yf_ref, bf16[2,256,256]{2,1,0:T(8,128)(2,1)} %constant.30.clone.table_ref), custom_call_target="tpu_custom_call" | custom-call | flops 8000000000 | bytes 24000000 | tf_op jit(solution)/shard_map/pallas_call | solution.py:323
  8.1 7.4 %all-to-all-start = ((f32[16,16,512]{2,1,0:T(8,128)}), f32[16,16,512]{2,1,0:T(8,128)S(1)}, u32[]{:S(2)}, u32[]{:S(2)}) async-start(f32[16,16,512]{2,1,0:T(8,128)} %shard_map.193), calls=%async_computation | async-start | bytes 1048576 | tf_op jit(solution)/shard_map/all_to_all | solution.py:690
  15.6 5.3 %shard_map.195.refs_0_ = f32[32,8,128,128]{3,2,1,0:T(8,128)} custom-call(f32[32,8,128,128]{3,2,1,0:T(8,128)} %bitcast.9, f32[32,32]{1,0:T(8,128)S(1)} %bitcast.5, bf16[256,32]{1,0:T(8,128)(2,1)S(1)} %copy-done), custom_call_target="tpu_custom_call" | custom-call | flops 4000000000 | bytes 12000000 | tf_op jit(solution)/shard_map/pallas_call | solution.py:610
  20.9 7.5 %shard_map.194 = f32[16,16,512]{2,1,0:T(8,128)} custom-call(f32[32,8,128,128]{3,2,1,0:T(8,128)} %bitcast.10, bf16[128,256]{1,0:T(8,128)(2,1)} %constant.28.clone.yf_ref, bf16[2,256,256]{2,1,0:T(8,128)(2,1)} %constant.30.clone.table_ref), custom_call_target="tpu_custom_call" | custom-call | flops 8000000000 | bytes 24000000 | tf_op jit(solution)/shard_map/pallas_call | solution.py:323
  28.3 1.6 all-to-all-done.refs_0_
  30.0 4.4 %all-to-all-start.1 = ((f32[16,16,512]{2,1,0:T(8,128)}), f32[16,16,512]{2,1,0:T(8,128)S(1)}, u32[]{:S(2)}, u32[]{:S(2)}) async-start(f32[16,16,512]{2,1,0:T(8,128)} %shard_map.194), calls=%async_computation.1 | async-start | bytes 1048576 | tf_op jit(solution)/shard_map/all_to_all | solution.py:690
  34.4 3.2 %shard_map.197 = (f32[64,1024]{1,0:T(8,128)S(1)}, f32[2,32,1024]{2,1,0:T(8,128)S(1)}) custom-call(f32[16,16,512]{2,1,0:T(8,128)S(1)} %all-to-all-done.refs_0_, f32[2,32,32,1024]{3,2,1,0:T(8,128)} %w.1, bf16[64,256]{1,0:T(8,128)(2,1)S(1)} %copy-done.12, bf16[64,256]{1,0:T(8,128)(2,1)S(1)} %copy-done.13, bf16[128,2048]{1,0:T(8,128)(2,1)S(1)} %copy-done.2, ...), custom_call_target="tpu_custom_call" | custom-call | flops 5000000000 | bytes 15000000 | tf_op jit(solution)/shard_map/pallas_call | solution.py:426
  37.6 9.4 %shard_map.196.refs_0_ = f32[32,8,128,128]{3,2,1,0:T(8,128)} custom-call(f32[32,8,128,128]{3,2,1,0:T(8,128)} %bitcast.11, f32[32,32]{1,0:T(8,128)S(1)} %bitcast.6, bf16[256,32]{1,0:T(8,128)(2,1)S(1)} %copy-done, f32[32,8,128,128]{3,2,1,0:T(8,128)} %shard_map.195.refs_0_), custom_call_target="tpu_custom_call", output_to_operand_aliasing={{}: (3, {})} | custom-call | flops 8000000000 | bytes 24000000 | tf_op jit(solution)/shard_map/pallas_call | solution.py:610
  47.0 1.9 all-to-all-done.1.refs_0_
  48.8 5.2 %shard_map.198 = (f32[64,1024]{1,0:T(8,128)S(1)}, f32[16,16,512]{2,1,0:T(8,128)}, f32[16,16,512]{2,1,0:T(8,128)}) custom-call(f32[16,16,512]{2,1,0:T(8,128)S(1)} %all-to-all-done.1.refs_0_, f32[2,32,32,1024]{3,2,1,0:T(8,128)} %w.1, bf16[64,256]{1,0:T(8,128)(2,1)S(1)} %copy-done.12, bf16[64,256]{1,0:T(8,128)(2,1)S(1)} %copy-done.13, ...), custom_call_target="tpu_custom_call", output_to_operand_aliasing={{0}: (7, {})} | custom-call | flops 5000000000 | bytes 15000000 | tf_op jit(solution)/shard_map/pallas_call | solution.py:426
  54.0 4.1 %all-to-all-start.2 = ((f32[16,16,512]{2,1,0:T(8,128)}), f32[16,16,512]{2,1,0:T(8,128)S(1)}, u32[]{:S(2)}, u32[]{:S(2)}) async-start(f32[16,16,512]{2,1,0:T(8,128)} %get-tuple-element.44), calls=%async_computation.2 | async-start | bytes 1048576 | tf_op jit(solution)/shard_map/all_to_all | solution.py:690
  58.2 1.6 collective-permute-start
  59.7 5.2 %shard_map.199.sum_ref = f32[32,8,128,128]{3,2,1,0:T(8,128)} custom-call(f32[32,8,128,128]{3,2,1,0:T(8,128)} %bitcast.12, f32[32,32]{1,0:T(8,128)S(1)} %bitcast.7, bf16[256,32]{1,0:T(8,128)(2,1)S(1)} %copy-done, f32[32,8,128,128]{3,2,1,0:T(8,128)} %shard_map.196.refs_0_), custom_call_target="tpu_custom_call", output_to_operand_aliasing={{}: (3, {})} | custom-call | flops 4000000000 | bytes 12000000 | tf_op jit(solution)/shard_map/pallas_call | solution.py:610
  65.0 7.6 %all-to-all-done.2.arrived_ref = f32[16,16,512]{2,1,0:T(8,128)S(1)} async-done(((f32[16,16,512]{2,1,0:T(8,128)}), f32[16,16,512]{2,1,0:T(8,128)S(1)}, u32[]{:S(2)}, u32[]{:S(2)}) %all-to-all-start.2) | async-done | bytes 524320 | tf_op jit(solution)/shard_map/all_to_all | solution.py:690
  72.6 4.1 %all-to-all-start.3 = ((f32[16,16,512]{2,1,0:T(8,128)}), f32[16,16,512]{2,1,0:T(8,128)S(1)}, u32[]{:S(2)}, u32[]{:S(2)}) async-start(f32[16,16,512]{2,1,0:T(8,128)} %get-tuple-element.47), calls=%async_computation.3 | async-start | bytes 1048576 | tf_op jit(solution)/shard_map/all_to_all | solution.py:690
  76.7 18.4 %shard_map.200 = (f32[32,8,128,128]{3,2,1,0:T(8,128)}, f32[32,8,128,128]{3,2,1,0:T(8,128)}, f32[16,16,512]{2,1,0:T(8,128)}) custom-call(f32[16,16,512]{2,1,0:T(8,128)S(1)} %all-to-all-done.2.arrived_ref, f32[32,8,128,128]{3,2,1,0:T(8,128)} %shard_map.199.sum_ref, f32[32,8,128,128]{3,2,1,0:T(8,128)} %bitcast.14, bf16[128,192]{1,0:T(8,128)(2,1)S(1)} %copy-done.6, ...), custom_call_target="tpu_custom_call" | custom-call | flops 20000000000 | bytes 60000000 | tf_op jit(solution)/shard_map/pallas_call | solution.py:649
  95.1 6.0 %all-to-all-start.4 = ((f32[16,16,512]{2,1,0:T(8,128)}), f32[16,16,512]{2,1,0:T(8,128)S(1)}, u32[]{:S(2)}, u32[]{:S(2)}) async-start(f32[16,16,512]{2,1,0:T(8,128)} %get-tuple-element.55), calls=%async_computation.4 | async-start | bytes 1048576 | tf_op jit(solution)/shard_map/all_to_all | solution.py:690
  101.2 18.5 %shard_map.201 = (f32[32,8,128,128]{3,2,1,0:T(8,128)}, f32[32,8,128,128]{3,2,1,0:T(8,128)}, f32[16,16,512]{2,1,0:T(8,128)}) custom-call(f32[16,16,512]{2,1,0:T(8,128)S(1)} %all-to-all-done.3.arrived_ref, f32[32,8,128,128]{3,2,1,0:T(8,128)} %shard_map.199.sum_ref, f32[32,8,128,128]{3,2,1,0:T(8,128)} %bitcast.15, ...), custom_call_target="tpu_custom_call", output_to_operand_aliasing={{0}: (8, {}), {1}: (9, {})} | custom-call | flops 20000000000 | bytes 60000000 | tf_op jit(solution)/shard_map/pallas_call | solution.py:649
  119.6 6.0 %all-to-all-start.5 = ((f32[16,16,512]{2,1,0:T(8,128)}), f32[16,16,512]{2,1,0:T(8,128)S(1)}, u32[]{:S(2)}, u32[]{:S(2)}) async-start(f32[16,16,512]{2,1,0:T(8,128)} %get-tuple-element.58), calls=%async_computation.5 | async-start | bytes 1048576 | tf_op jit(solution)/shard_map/all_to_all | solution.py:690
  125.6 13.3 %shard_map.202.refs_0_ = f32[32,8,128,128]{3,2,1,0:T(8,128)} custom-call(f32[32,8,128,128]{3,2,1,0:T(8,128)} %get-tuple-element.59.data_ref, f32[32,32]{1,0:T(8,128)S(1)} %copy-done.7, bf16[256,32]{1,0:T(8,128)(2,1)S(1)} %copy-done), custom_call_target="tpu_custom_call" | custom-call | flops 12000000000 | bytes 36000000 | tf_op jit(solution)/shard_map/pallas_call | solution.py:610
  138.9 1.2 all-to-all-done.5.refs_1_
  140.1 5.7 %shard_map.203 = (f32[2,32,1024]{2,1,0:T(8,128)S(1)}, f32[16,16,512]{2,1,0:T(8,128)}) custom-call(f32[16,16,512]{2,1,0:T(8,128)S(1)} %all-to-all-done.4.refs_0_, f32[16,16,512]{2,1,0:T(8,128)S(1)} %all-to-all-done.5.refs_1_, f32[2,32,32,1024]{3,2,1,0:T(8,128)} %w.1, bf16[64,256]{1,0:T(8,128)(2,1)S(1)} %copy-done.12, bf16[64,256]{1,0:T(8,128)(2,1)S(1)} %copy-done.13, ...), custom_call_target="tpu_custom_call" | custom-call | flops 7000000000 | bytes 21000000 | tf_op jit(solution)/shard_map/pallas_call | solution.py:488
  145.8 1.5 collective-permute-start.1
  147.2 4.9 %all-to-all-start.6 = ((f32[16,16,512]{2,1,0:T(8,128)}), f32[16,16,512]{2,1,0:T(8,128)S(1)}, u32[]{:S(2)}, u32[]{:S(2)}) async-start(f32[16,16,512]{2,1,0:T(8,128)} %get-tuple-element.62), calls=%async_computation.6 | async-start | bytes 1048576 | tf_op jit(solution)/shard_map/all_to_all | solution.py:690
  153.2 4.4 %shard_map.204 = f32[16,16,512]{2,1,0:T(8,128)} custom-call(f32[2,32,1024]{2,1,0:T(8,128)S(1)} %get-tuple-element.63.g.g_ref, f32[2,32,32,1024]{3,2,1,0:T(8,128)} %w.1, bf16[64,256]{1,0:T(8,128)(2,1)S(1)} %copy-done.12, bf16[64,256]{1,0:T(8,128)(2,1)S(1)} %copy-done.13, bf16[2048,128]{1,0:T(8,128)(2,1)S(1)} %copy-done.8, bf16[256,192]{1,0:T(8,128)(2,1)S(1)} %copy-done.10), custom_call_target="tpu_custom_call" | custom-call | flops 6000000000 | bytes 18000000 | tf_op jit(solution)/shard_map/pallas_call | solution.py:501
  157.6 5.3 %shard_map.205.sum_ref = f32[32,8,128,128]{3,2,1,0:T(8,128)} custom-call(f32[32,8,128,128]{3,2,1,0:T(8,128)} %get-tuple-element.59.data_ref, f32[32,32]{1,0:T(8,128)S(1)} %copy-done.7, bf16[256,32]{1,0:T(8,128)(2,1)S(1)} %copy-done, f32[32,8,128,128]{3,2,1,0:T(8,128)} %shard_map.202.refs_0_), custom_call_target="tpu_custom_call", output_to_operand_aliasing={{}: (3, {})} | custom-call | flops 4000000000 | bytes 12000000 | tf_op jit(solution)/shard_map/pallas_call | solution.py:610
  162.8 2.4 %shard_map.206.refs_0_ = f32[2,32,32,1024]{3,2,1,0:T(8,128)} custom-call(f32[64,1024]{1,0:T(8,128)S(1)} %copy-done.4, f32[64,1024]{1,0:T(8,128)S(1)} %collective-permute-done.far_hat_ref, f32[2,32,1024]{2,1,0:T(8,128)S(1)} %get-tuple-element.63.g.g_ref, f32[2,32,1024]{2,1,0:T(8,128)S(1)} %collective-permute-done.1.far_g_ref, bf16[128,2048]{1,0:T(8,128)(2,1)S(1)} %copy-done.2), custom_call_target="tpu_custom_call" | custom-call | flops 2000000000 | bytes 6000000 | tf_op jit(solution)/shard_map/pallas_call | solution.py:530
  165.2 1.4 all-to-all-done.6.arrived_ref
  166.6 4.6 %all-to-all-start.7 = ((f32[16,16,512]{2,1,0:T(8,128)}), f32[16,16,512]{2,1,0:T(8,128)S(1)}, u32[]{:S(2)}, u32[]{:S(2)}) async-start(f32[16,16,512]{2,1,0:T(8,128)} %shard_map.204), calls=%async_computation.7 | async-start | bytes 1048576 | tf_op jit(solution)/shard_map/all_to_all | solution.py:690
  172.2 4.8 %shard_map.208 = f32[2,32,32,1024]{3,2,1,0:T(8,128)} custom-call(f32[64,1024]{1,0:T(8,128)S(1)} %copy-done.5, f32[64,1024]{1,0:T(8,128)S(1)} %collective-permute-done.far_hat_ref, f32[2,32,1024]{2,1,0:T(8,128)S(1)} %get-tuple-element.63.g.g_ref, f32[2,32,1024]{2,1,0:T(8,128)S(1)} %collective-permute-done.1.far_g_ref, ...), custom_call_target="tpu_custom_call", output_to_operand_aliasing={{}: (5, {})} | custom-call | flops 6000000000 | bytes 18000000 | tf_op jit(solution)/shard_map/pallas_call | solution.py:530
  176.9 9.3 %shard_map.207.refs_0_ = f32[32,8,128,128]{3,2,1,0:T(8,128)} custom-call(f32[16,16,512]{2,1,0:T(8,128)S(1)} %all-to-all-done.6.arrived_ref, f32[32,8,128,128]{3,2,1,0:T(8,128)} %shard_map.205.sum_ref, bf16[128,192]{1,0:T(8,128)(2,1)S(1)} %copy-done.6, bf16[256,2048]{1,0:T(8,128)(2,1)S(1)} %copy-done.1, bf16[256,2048]{1,0:T(8,128)(2,1)} %constant.35.clone.zjl_ref), custom_call_target="tpu_custom_call" | custom-call | flops 10000000000 | bytes 30000000 | tf_op jit(solution)/shard_map/pallas_call | solution.py:677
  186.2 9.3 %shard_map.209 = f32[32,8,128,128]{3,2,1,0:T(8,128)} custom-call(f32[16,16,512]{2,1,0:T(8,128)S(1)} %all-to-all-done.7.arrived_ref, f32[32,8,128,128]{3,2,1,0:T(8,128)} %shard_map.205.sum_ref, bf16[128,192]{1,0:T(8,128)(2,1)S(1)} %copy-done.6, bf16[256,2048]{1,0:T(8,128)(2,1)S(1)} %copy-done.1, ...), custom_call_target="tpu_custom_call", output_to_operand_aliasing={{}: (5, {})} | custom-call | flops 10000000000 | bytes 30000000 | tf_op jit(solution)/shard_map/pallas_call | solution.py:677
  (34 shorter events, 2.1 us)
Async XLA Ops:
  0.6 15.0 %copy-start = (bf16[256,32]{1,0:T(8,128)(2,1)S(1)}, bf16[256,32]{1,0:T(8,128)(2,1)}, u32[]{:S(2)}) copy-start(bf16[256,32]{1,0:T(8,128)(2,1)} %constant.40.clone.rep_ref) | copy-start | bytes 49156
  0.6 14.9 %copy-start.7 = (f32[32,32]{1,0:T(8,128)S(1)}, f32[32,32]{1,0:T(8,128)}, u32[]{:S(2)}) copy-start(f32[32,32]{1,0:T(8,128)} %matrix_ref.3) | copy-start | bytes 12292
  8.1 21.9 %all-to-all-start = ((f32[16,16,512]{2,1,0:T(8,128)}), f32[16,16,512]{2,1,0:T(8,128)S(1)}, u32[]{:S(2)}, u32[]{:S(2)}) async-start(f32[16,16,512]{2,1,0:T(8,128)} %shard_map.193), calls=%async_computation | async-start | bytes 1048576 | tf_op jit(solution)/shard_map/all_to_all | solution.py:690
  20.8 13.5 %copy-start.2 = (bf16[128,2048]{1,0:T(8,128)(2,1)S(1)}, bf16[128,2048]{1,0:T(8,128)(2,1)}, u32[]{:S(2)}) copy-start(bf16[128,2048]{1,0:T(8,128)(2,1)} %constant.39.clone.refs_4_.spread_ref) | copy-start | bytes 1572868
  20.8 13.5 %copy-start.10 = (bf16[256,192]{1,0:T(8,128)(2,1)S(1)}, bf16[256,192]{1,0:T(8,128)(2,1)}, u32[]{:S(2)}) copy-start(bf16[256,192]{1,0:T(8,128)(2,1)} %constant.38.clone.refs_5_.refs_6_.xi) | copy-start | bytes 294916
  20.8 13.6 %copy-start.12 = (bf16[64,256]{1,0:T(8,128)(2,1)S(1)}, bf16[64,256]{1,0:T(8,128)(2,1)}, u32[]{:S(2)}) copy-start(bf16[64,256]{1,0:T(8,128)(2,1)} %constant.36.clone.refs_2_.refs_3_.xfh) | copy-start | bytes 98308
  20.8 13.6 %copy-start.13 = (bf16[64,256]{1,0:T(8,128)(2,1)S(1)}, bf16[64,256]{1,0:T(8,128)(2,1)}, u32[]{:S(2)}) copy-start(bf16[64,256]{1,0:T(8,128)(2,1)} %constant.37.clone.refs_3_.refs_4_.xfl) | copy-start | bytes 98308
  30.0 18.9 %all-to-all-start.1 = ((f32[16,16,512]{2,1,0:T(8,128)}), f32[16,16,512]{2,1,0:T(8,128)S(1)}, u32[]{:S(2)}, u32[]{:S(2)}) async-start(f32[16,16,512]{2,1,0:T(8,128)} %shard_map.194), calls=%async_computation.1 | async-start | bytes 1048576 | tf_op jit(solution)/shard_map/all_to_all | solution.py:690
  54.0 11.0 %copy-start.3 = (f32[64,1024]{1,0:T(8,128)}, f32[64,1024]{1,0:T(8,128)S(1)}, u32[]{:S(2)}) copy-start(f32[64,1024]{1,0:T(8,128)S(1)} %get-tuple-element.60.hat_ref) | copy-start | bytes 786436
  54.0 18.6 %all-to-all-start.2 = ((f32[16,16,512]{2,1,0:T(8,128)}), f32[16,16,512]{2,1,0:T(8,128)S(1)}, u32[]{:S(2)}, u32[]{:S(2)}) async-start(f32[16,16,512]{2,1,0:T(8,128)} %get-tuple-element.44), calls=%async_computation.2 | async-start | bytes 1048576 | tf_op jit(solution)/shard_map/all_to_all | solution.py:690
  58.1 18.6 %copy-start.6 = (bf16[128,192]{1,0:T(8,128)(2,1)S(1)}, bf16[128,192]{1,0:T(8,128)(2,1)}, u32[]{:S(2)}) copy-start(bf16[128,192]{1,0:T(8,128)(2,1)} %constant.29.clone.yi_ref) | copy-start | bytes 147460
  58.1 18.6 %copy-start.9 = (bf16[2,256,256]{2,1,0:T(8,128)(2,1)S(1)}, bf16[2,256,256]{2,1,0:T(8,128)(2,1)}, u32[]{:S(2)}) copy-start(bf16[2,256,256]{2,1,0:T(8,128)(2,1)} %constant.31.clone.zg_ref) | copy-start | bytes 786436
  58.2 18.6 %copy-start.11 = (bf16[128,256]{1,0:T(8,128)(2,1)S(1)}, bf16[128,256]{1,0:T(8,128)(2,1)}, u32[]{:S(2)}) copy-start(bf16[128,256]{1,0:T(8,128)(2,1)} %constant.28.clone.yf_ref) | copy-start | bytes 196612
  58.2 80.8 %collective-permute-start = (f32[64,1024]{1,0:T(8,128)S(1)}, f32[64,1024]{1,0:T(8,128)S(1)}, u32[]{:S(2)}, u32[]{:S(2)}) collective-permute-start(f32[64,1024]{1,0:T(8,128)S(1)} %get-tuple-element.60.hat_ref), channel_id=1, source_target_pairs={{0,16},{16,0},{1,17},{17,1},{2,18},{18,2},{3,19},{19,3},{4,20},{20... | collective-permute-start | bytes 786440 | tf_op jit(solution)/shard_map/ppermute | solution.py:720
  72.6 22.5 %all-to-all-start.3 = ((f32[16,16,512]{2,1,0:T(8,128)}), f32[16,16,512]{2,1,0:T(8,128)S(1)}, u32[]{:S(2)}, u32[]{:S(2)}) async-start(f32[16,16,512]{2,1,0:T(8,128)} %get-tuple-element.47), calls=%async_computation.3 | async-start | bytes 1048576 | tf_op jit(solution)/shard_map/all_to_all | solution.py:690
  95.1 24.5 %all-to-all-start.4 = ((f32[16,16,512]{2,1,0:T(8,128)}), f32[16,16,512]{2,1,0:T(8,128)S(1)}, u32[]{:S(2)}, u32[]{:S(2)}) async-start(f32[16,16,512]{2,1,0:T(8,128)} %get-tuple-element.55), calls=%async_computation.4 | async-start | bytes 1048576 | tf_op jit(solution)/shard_map/all_to_all | solution.py:690
  119.6 20.5 %all-to-all-start.5 = ((f32[16,16,512]{2,1,0:T(8,128)}), f32[16,16,512]{2,1,0:T(8,128)S(1)}, u32[]{:S(2)}, u32[]{:S(2)}) async-start(f32[16,16,512]{2,1,0:T(8,128)} %get-tuple-element.58), calls=%async_computation.5 | async-start | bytes 1048576 | tf_op jit(solution)/shard_map/all_to_all | solution.py:690
  145.8 17.1 %collective-permute-start.1 = (f32[2,32,1024]{2,1,0:T(8,128)S(1)}, f32[2,32,1024]{2,1,0:T(8,128)S(1)}, u32[]{:S(2)}, u32[]{:S(2)}) collective-permute-start(f32[2,32,1024]{2,1,0:T(8,128)S(1)} %get-tuple-element.63.g.g_ref), channel_id=1, source_target_pairs={{0,16},{16,0},{1,17},{17,1},{2,18},{18,2},{3,19},{19,3},{4,20},{20... | collective-permute-start | bytes 786440 | tf_op jit(solution)/shard_map/ppermute | solution.py:745
  147.2 19.4 %all-to-all-start.6 = ((f32[16,16,512]{2,1,0:T(8,128)}), f32[16,16,512]{2,1,0:T(8,128)S(1)}, u32[]{:S(2)}, u32[]{:S(2)}) async-start(f32[16,16,512]{2,1,0:T(8,128)} %get-tuple-element.62), calls=%async_computation.6 | async-start | bytes 1048576 | tf_op jit(solution)/shard_map/all_to_all | solution.py:690
  152.1 1.0 copy-start.8
  157.6 5.3 %copy-start.4 = (f32[64,1024]{1,0:T(8,128)S(1)}, f32[64,1024]{1,0:T(8,128)}, u32[]{:S(2)}) copy-start(f32[64,1024]{1,0:T(8,128)} %copy-done.3) | copy-start | bytes 786436
  162.8 14.1 %copy-start.1 = (bf16[256,2048]{1,0:T(8,128)(2,1)S(1)}, bf16[256,2048]{1,0:T(8,128)(2,1)}, u32[]{:S(2)}) copy-start(bf16[256,2048]{1,0:T(8,128)(2,1)} %constant.34.clone.zjh_ref) | copy-start | bytes 3145732
  166.6 19.6 %all-to-all-start.7 = ((f32[16,16,512]{2,1,0:T(8,128)}), f32[16,16,512]{2,1,0:T(8,128)S(1)}, u32[]{:S(2)}, u32[]{:S(2)}) async-start(f32[16,16,512]{2,1,0:T(8,128)} %shard_map.204), calls=%async_computation.7 | async-start | bytes 1048576 | tf_op jit(solution)/shard_map/all_to_all | solution.py:690
  171.2 1.0 copy-start.5
